TPU v7x, 32 devices: a whole 2x2x4 slice. The times are simulated.
32 devices in a mesh: row: 8 (over z, x), col: 4 (over y, core).
Axes of the slice: x: 2, y: 2, z: 4, core: 2. Of those that a mesh axis runs over, the one named last changes fastest.
Arguments:
- tiles: bfloat16 [5376, 128, 128], P(('row', 'col')), may hold values from -0.0625 to 0.0625
- tile_slots: int32 [5376], P(('row', 'col')), may hold values from 0 to 383, as said below
- sketch: bfloat16 [24576, 512], P('col'), may hold values from -6 to 6
- row_sketch: bfloat16 [8192, 512], P(('row', 'col')), may hold values from -6 to 6
- subsketch: float32 [512, 128], replicated, may hold values from -0.25 to 0.25
- couplings: bfloat16 [32, 5, 128, 128], P(('row', 'col')), may hold values from -0.25 to 0.25, as said below
Outputs:
- leaf_basis: float32 [8192, 128], P(('row', 'col'))
- transfer: float32 [32, 5, 128, 128], P(('row', 'col'))
- top_samples: float32 [32, 128, 512], P(('row', 'col'))
Inputs may be any that keep to these rules, and one draw needn't show every extreme that they name: `tile_slots`: the 168 slots of one device are distinct; slot v names row tile v // 48 and column tile v % 48. couplings[i, l] equals couplings[j, l] whenever i // 2 ** (l + 1) equals j // 2 ** (l + 1).
All inputs are finite; a program needn't handle non-finite values.
Results may differ from a plain program's by a relative error of at most 0.0003.
Values may be sent and summed in bfloat16 or wider, within the bound.
No kernel may reach another device: no remote copies, remote signals or barrier semaphores. Data moves between devices by JAX's collectives and lax.ppermute only.
A program may use at most 128 MiB of HBM per device.

v0:
```python
import functools
import math

import jax
import jax.numpy as jnp
from jax import lax
from jax.experimental import pallas as pl
from jax.experimental.pallas import tpu as pltpu
from jax.sharding import PartitionSpec as P

LEVELS = 5
ROW_COL = ("row", "col")
VMEM = pl.BlockSpec(memory_space=pltpu.VMEM)


def from_partner(block, axis, distance):
    count = lax.axis_size(axis)
    route = []
    for low in range(count):
        high = low ^ distance
        if high < count:
            route.append((low, high))
    return lax.ppermute(block, axis, route)


def dot(left, right):
    return jnp.dot(left, right, precision=lax.Precision.HIGHEST, preferred_element_type=jnp.float32)


def dot_nt(left, right):
    return lax.dot_general(
        left,
        right,
        (((1,), (1,)), ((), ())),
        precision=lax.Precision.HIGHEST,
        preferred_element_type=jnp.float32,
    )


def inverse_factor(gram):
    size = gram.shape[0]
    high = 8
    count = size // high
    lane_all = lax.broadcasted_iota(jnp.int32, (size, size), 1)
    diag = lane_all == lax.broadcasted_iota(jnp.int32, (size, size), 0)
    trace = jnp.sum(
        jnp.sum(jnp.where(diag, gram, 0.0), axis=0, keepdims=True), axis=1, keepdims=True
    )
    shift = 0.0001 * trace / size + 1e-06
    gram = jnp.where(diag, gram + shift, gram)
    rows = [gram[high * g : high * g + high, :] for g in range(count)]
    shape = (high, size)
    lane = lax.broadcasted_iota(jnp.int32, shape, 1)
    sub = lax.broadcasted_iota(jnp.int32, shape, 0)

    def along_lanes(block, at):
        return jnp.broadcast_to(block[:, at : at + 1], shape)

    def along_rows(block, at):
        return jnp.broadcast_to(block[at : at + 1, :], shape)

    found = []
    for b in range(count):
        first = b * high
        panel = rows[b]
        columns = [along_lanes(panel, first + k) for k in range(high)]
        inside = (lane >= first) & (lane < first + high)
        panel = jnp.where(inside, jnp.where(lane - first == sub, 1.0, 0.0), panel)
        forward, full = panel, panel
        forward_scale = jnp.zeros(shape, jnp.float32)
        full_scale = jnp.zeros(shape, jnp.float32)
        for i in range(high):
            pivot = along_rows(columns[i], i)
            inverse = 1.0 / pivot
            others = jnp.where(sub == i, 0.0, columns[i])
            below = jnp.where(sub > i, columns[i], 0.0)
            for k in range(i + 1, high):
                columns[k] = columns[k] - others * along_rows(columns[k], i) * inverse
            row = along_rows(forward, i) * inverse
            forward = forward - below * row
            full = full - others * row
            forward_scale = jnp.where(sub == i, lax.rsqrt(pivot), forward_scale)
            full_scale = jnp.where(sub == i, inverse, full_scale)
        found.append(jnp.where(lane < first + high, forward * forward_scale, 0.0))
        if b + 1 == count:
            break
        full = full * full_scale
        full_rows = [along_rows(full, k) for k in range(high)]
        for g in range(b + 1, count):
            terms = [along_lanes(rows[g], first + k) * full_rows[k] for k in range(high)]
            while len(terms) > 1:
                terms = [terms[t] + terms[t + 1] for t in range(0, len(terms), 2)]
            rows[g] = jnp.where(inside, 0.0, rows[g]) - terms[0]
    return jnp.concatenate(found, axis=0)


def spmm_body(
    slots_ref,
    tiles_ref,
    sketch_ref,
    sub_ref,
    leaf_sketch_ref,
    keep_ref,
    send_ref,
    keep_red_ref,
    send_red_ref,
    sketch_red_ref,
    dense,
    held,
    tile_sem,
    sketch_sems,
):
    tile_count, tile_size, _ = tiles_ref.shape
    depth = sketch_ref.shape[0]
    rows = dense.shape[0]
    half = rows // 2
    col_tiles = depth // tile_size
    chunks = sketch_sems.shape[0]
    chunk = depth // chunks
    leaf_tiles = leaf_sketch_ref.shape[0] // tile_size
    leaves = rows // leaf_sketch_ref.shape[0]
    me = lax.axis_index("col")
    loads = [
        pltpu.make_async_copy(
            sketch_ref.at[pl.ds(k * chunk, chunk)], held.at[pl.ds(k * chunk, chunk)], sketch_sems.at[k]
        )
        for k in range(chunks)
    ]

    @pl.loop(0, rows // 64)
    def _(i):
        dense[pl.ds(pl.multiple_of(i * 64, 64), 64), :] = jnp.zeros((64, depth), dense.dtype)

    @pl.loop(0, tile_count)
    def _(t):
        slot = slots_ref[t]
        row_tile = slot // col_tiles
        away = (row_tile // leaf_tiles) ^ me
        block = away % 2 * (leaves // 2) + away // 2
        row = pl.multiple_of((block * leaf_tiles + row_tile % leaf_tiles) * tile_size, tile_size)
        col = pl.multiple_of(slot % col_tiles * tile_size, tile_size)
        pltpu.make_async_copy(
            tiles_ref.at[t], dense.at[pl.ds(row, tile_size), pl.ds(col, tile_size)], tile_sem
        ).start()

    for load in loads:
        load.start()
    subsketch = sub_ref[...]
    sketch_red_ref[...] = dot(leaf_sketch_ref[...].astype(jnp.float32), subsketch)
    pltpu.make_async_copy(tiles_ref, tiles_ref, tile_sem).wait()
    for k in range(chunks):
        loads[k].wait()
        for start, ref in ((half, send_ref), (0, keep_ref)):
            part = jnp.dot(
                dense[start : start + half, k * chunk : (k + 1) * chunk],
                held[k * chunk : (k + 1) * chunk, :],
                preferred_element_type=jnp.float32,
            )
            if k == 0:
                ref[...] = part
            else:
                ref[...] += part
    send_red_ref[...] = dot(send_ref[...], subsketch)
    keep_red_ref[...] = dot(keep_ref[...], subsketch)


def sample_rows(tiles, tile_slots, sketch, subsketch, row_sketch):
    tile_size = tiles.shape[1]
    depth, width = sketch.shape
    rank = subsketch.shape[1]
    leaf = row_sketch.shape[0]
    rows = leaf * lax.axis_size("col")
    half = rows // 2
    chunks = math.gcd(depth // tile_size, 4)
    f32 = jnp.float32
    return pl.pallas_call(
        spmm_body,
        out_shape=[
            jax.ShapeDtypeStruct((half, width), f32),
            jax.ShapeDtypeStruct((half, width), f32),
            jax.ShapeDtypeStruct((half, rank), f32),
            jax.ShapeDtypeStruct((half, rank), f32),
            jax.ShapeDtypeStruct((leaf, rank), f32),
        ],
        in_specs=[
            pl.BlockSpec(memory_space=pltpu.SMEM),
            pl.BlockSpec(memory_space=pl.ANY),
            pl.BlockSpec(memory_space=pl.ANY),
            VMEM,
            VMEM,
        ],
        out_specs=[VMEM] * 5,
        scratch_shapes=[
            pltpu.VMEM((rows, depth), jnp.bfloat16),
            pltpu.VMEM((depth, width), jnp.bfloat16),
            pltpu.SemaphoreType.DMA,
            pltpu.SemaphoreType.DMA((chunks,)),
        ],
        compiler_params=pltpu.CompilerParams(vmem_limit_bytes=48 * 2**20),
        cost_estimate=pl.CostEstimate(
            flops=2 * rows * depth * width,
            bytes_accessed=2 * (tiles.size + sketch.size) + 4 * rows * width,
            transcendentals=0,
        ),
        name="spmm",
    )(tile_slots, tiles, sketch, subsketch, row_sketch)


def leaf_body(keep_ref, first_ref, second_ref, sketch_red_ref, basis_ref, basis_t_ref, pair_ref):
    rank = keep_ref.shape[-1]
    reduced = keep_ref[...] + first_ref[...] + second_ref[...]
    reduced_t = reduced.T
    both = dot(reduced_t, jnp.concatenate([reduced, sketch_red_ref[...]], axis=1))
    inverse = inverse_factor(both[:, :rank])
    moved = dot(inverse, both)
    pair_ref[:rank, :] = moved[:, :rank]
    pair_ref[rank:, :] = moved[:, rank:]
    basis_ref[...] = dot_nt(reduced, inverse)
    basis_t_ref[...] = dot(inverse, reduced_t)


def small_params():
    return pltpu.CompilerParams(vmem_limit_bytes=32 * 2**20)


def small_cost(micros):
    return pl.CostEstimate(flops=micros * 10**9, bytes_accessed=micros * 3 * 10**6, transcendentals=0)


def leaf_step(keep, first, second, sketch_red):
    leaf, rank = sketch_red.shape
    f32 = jnp.float32
    part = pl.BlockSpec((leaf, rank), lambda step: (0, 0))
    return pl.pallas_call(
        leaf_body,
        grid=(1,),
        out_shape=[
            jax.ShapeDtypeStruct((leaf, rank), f32),
            jax.ShapeDtypeStruct((rank, leaf), f32),
            jax.ShapeDtypeStruct((2 * rank, rank), f32),
        ],
        in_specs=[part, part, VMEM, VMEM],
        out_specs=[VMEM] * 3,
        compiler_params=small_params(),
        cost_estimate=small_cost(8),
        name="leaf_orth",
    )(keep, first, second, sketch_red)


def turned(coupling_ref, tree_level):
    position = lax.axis_index("row") * lax.axis_size("col") + lax.axis_index("col")
    upper = position // 2**tree_level % 2 == 1
    coupling = coupling_ref[0, 0].astype(jnp.float32)
    coupling_t = coupling.T
    return jnp.where(upper, coupling_t, coupling), jnp.where(upper, coupling, coupling_t)


def merge_body(tree_level, own_ref, other_ref, coupling_ref, block_ref, maps_ref, pair_ref):
    rank = own_ref.shape[-1]
    ahead, back = turned(coupling_ref, tree_level)
    own_sample, own_sketch = own_ref[:rank], own_ref[rank:]
    other_sample, other_sketch = other_ref[:rank], other_ref[rank:]
    own = own_sample - dot(ahead, other_sketch)
    other = other_sample - dot(back, own_sketch)
    own_t, other_t = own.T, other.T
    stacked_t = jnp.concatenate([own_t, other_t], axis=1)
    right = jnp.concatenate(
        [
            jnp.concatenate([own, own_sketch], axis=1),
            jnp.concatenate([other, other_sketch], axis=1),
        ],
        axis=0,
    )
    both = dot(stacked_t, right)
    inverse = inverse_factor(both[:, :rank])
    moved = dot(inverse, both)
    pair_ref[:rank, :] = moved[:, :rank]
    pair_ref[rank:, :] = moved[:, rank:]
    block_ref[...] = dot_nt(own, inverse)
    maps_ref[0] = dot(inverse, own_t)
    maps_ref[1] = dot(inverse, dot(other_t, back))


def coupling_spec(couplings, tree_level):
    return pl.BlockSpec((1, 1) + couplings.shape[2:], lambda step: (0, tree_level, 0, 0))


def merge_step(tree_level, own, other, couplings):
    rank = own.shape[1]
    f32 = jnp.float32
    return pl.pallas_call(
        functools.partial(merge_body, tree_level),
        grid=(1,),
        out_shape=[
            jax.ShapeDtypeStruct((rank, rank), f32),
            jax.ShapeDtypeStruct((2, rank, rank), f32),
            jax.ShapeDtypeStruct((2 * rank, rank), f32),
        ],
        in_specs=[VMEM, VMEM, coupling_spec(couplings, tree_level)],
        out_specs=[VMEM] * 3,
        compiler_params=small_params(),
        cost_estimate=small_cost(8),
        name=f"merge_orth_{tree_level}",
    )(own, other, couplings)


def lower_body(*refs):
    keep_ref, first_ref, second_ref, leaf_sketch_ref, basis_t_ref = refs[:5]
    ways = (refs[-1].shape[1]) // refs[-2].shape[1]
    maps_refs = refs[5 : -1 - ways]
    out_refs = refs[-1 - ways : -1]
    wide = refs[-1]
    rank = basis_t_ref.shape[0]
    sample = keep_ref[...] + first_ref[...] + second_ref[...]
    sketch = leaf_sketch_ref[...].astype(jnp.float32)
    on_sample = basis_t_ref[...]
    on_sketch = jnp.zeros_like(on_sample)
    for maps_ref in maps_refs:
        lifted, crossed = maps_ref[0], maps_ref[1]
        on_sketch = dot(lifted, on_sketch) - dot(crossed, on_sample)
        on_sample = dot(lifted, on_sample)
    wide[:rank, :] = dot(on_sample, sample) + dot(on_sketch, sketch)
    wide[rank:, :] = dot(on_sample, sketch)
    me = lax.axis_index("col")
    part = wide.shape[1] // ways
    for away in range(ways):
        out_refs[away][...] = wide[:, pl.ds(pl.multiple_of((me ^ away) * part, part), part)]


def lower_step(keep, first, second, row_sketch, basis_t, maps):
    ways = lax.axis_size("col")
    leaf, width = row_sketch.shape
    rank = basis_t.shape[0]
    part = pl.BlockSpec((leaf, width), lambda step: (0, 0))
    return pl.pallas_call(
        lower_body,
        grid=(1,),
        out_shape=[jax.ShapeDtypeStruct((2 * rank, width // ways), jnp.float32)] * ways,
        in_specs=[part, part] + [VMEM] * (3 + len(maps)),
        out_specs=[VMEM] * ways,
        scratch_shapes=[pltpu.VMEM((2 * rank, width), jnp.float32)],
        compiler_params=small_params(),
        cost_estimate=small_cost(2),
        name="lower_maps",
    )(keep, first, second, row_sketch, basis_t, *maps)


def upper_body(last, *refs):
    maps_ref, out_ref = refs[-2:]
    total = refs[0][...]
    for ref in refs[1:-2]:
        total = total + ref[...]
    rank = maps_ref.shape[1]
    sample, sketch = total[:rank], total[rank:]
    lifted = maps_ref[0]
    out_ref[:rank, :] = dot(lifted, sample) - dot(maps_ref[1], sketch)
    if not last:
        out_ref[rank:, :] = dot(lifted, sketch)


def upper_step(tree_level, parts, maps):
    last = tree_level == LEVELS - 1
    rows, width = parts[0].shape
    return pl.pallas_call(
        functools.partial(upper_body, last),
        out_shape=jax.ShapeDtypeStruct((rows // 2 if last else rows, width), jnp.float32),
        in_specs=[VMEM] * (len(parts) + 1),
        out_specs=VMEM,
        compiler_params=small_params(),
        cost_estimate=small_cost(1),
        name=f"upper_maps_{tree_level}",
    )(*parts, maps)


def top_body(ways, *refs):
    out_ref = refs[-1]
    me = lax.axis_index("col")
    part = out_ref.shape[2] // ways
    for away in range(ways):
        out_ref[0, :, pl.ds(pl.multiple_of((me ^ away) * part, part), part)] = refs[away][...]


def per_device(tiles, tile_slots, sketch, row_sketch, subsketch, couplings):
    ways = lax.axis_size("col")
    col_bits = ways.bit_length() - 1
    leaf = row_sketch.shape[0]
    keep, send, keep_red, send_red, sketch_red = sample_rows(
        tiles, tile_slots, sketch, subsketch, row_sketch
    )

    def gathered(kept, sent):
        first = from_partner(sent, "col", 1)
        second = from_partner(kept[leaf:] + first[leaf:], "col", 2)
        return kept, first, second

    reduced = gathered(keep_red, send_red)
    samples = gathered(keep, send)
    leaf_basis, basis_t, pair = leaf_step(*reduced, sketch_red)
    blocks, low_maps, parts = [], [], []
    for tree_level in range(LEVELS):
        other = from_partner(pair, ROW_COL, 2**tree_level)
        block, maps, pair = merge_step(tree_level, pair, other, couplings)
        blocks.append(block)
        if tree_level < col_bits:
            low_maps.append(maps)
        else:
            mine = upper_step(tree_level, parts, maps)
            parts = [mine, from_partner(mine, ROW_COL, 2**tree_level)]
        if tree_level == col_bits - 1:
            cut = lower_step(*samples, row_sketch, basis_t, low_maps)
            parts = [cut[0]] + [from_partner(cut[away], "col", away) for away in range(1, ways)]
    top = [parts[0] + parts[1]]
    for bit in reversed(range(col_bits)):
        top += [from_partner(piece, "col", 2**bit) for piece in top]
    order = [0]
    for bit in reversed(range(col_bits)):
        order += [away ^ 2**bit for away in order]
    pieces = [top[order.index(away)] for away in range(ways)]
    rank, part = pieces[0].shape
    top_sample = pl.pallas_call(
        functools.partial(top_body, ways),
        out_shape=jax.ShapeDtypeStruct((1, rank, part * ways), jnp.float32),
        in_specs=[VMEM] * ways,
        out_specs=VMEM,
        name="top_columns",
    )(*pieces)
    transfer = jnp.stack(blocks, axis=0)[None]
    return (leaf_basis, transfer, top_sample)


def solution(mesh):
    return jax.shard_map(
        per_device,
        mesh=mesh,
        in_specs=(
            P(("row", "col"), None, None),
            P(("row", "col")),
            P("col", None),
            P(("row", "col"), None),
            P(),
            P(("row", "col"), None, None, None),
        ),
        out_specs=(
            P(("row", "col"), None),
            P(("row", "col"), None, None, None),
            P(("row", "col"), None, None),
        ),
        check_vma=False,
    )
```

profile of v0, /device:TPU:0, one launch (start us, length us, event | category | flops | bytes accessed | tf_op | source)
XLA Modules:
  0.0 116.9 jit_solution(6220234304415195803)
XLA Ops:
  0.6 0.0 copy-start
  0.6 0.9 copy-done
  1.6 0.0 copy-start.1
  1.6 0.9 copy-done.1
  2.5 0.0 copy-start.3
  2.5 0.7 copy-done.3
  3.2 18.0 %spmm.1 = (f32[512,512]{1,0:T(8,128)S(1)}, f32[512,512]{1,0:T(8,128)S(1)}, f32[512,128]{1,0:T(8,128)S(1)}, f32[512,128]{1,0:T(8,128)S(1)}, f32[256,128]{1,0:T(8,128)S(1)}) custom-call(s32[168]{0:T(256)S(1)} %copy-done.3, bf16[168,128,128]{2,1,0:T(8,128)(2,1)} %tiles_ref.1, bf16[6144,512]{1,0:T(8,128)(2,1)} %sketch_ref.1, f32[512,128]{1,0:T(8,128)S(1)} %copy-done, ...), custom_call_target="tpu_custom_call" | custom-call | flops 6442450944 | bytes 13893632 | tf_op jit(solution)/shard_map/spmm/pallas_call | solution.py:176
  21.2 0.5 collective-permute-start
  21.7 1.2 collective-permute-done.first_ref
  22.9 3.0 %collective-permute-start.1 = (f32[256,128]{1,0:T(8,128)S(1)}, f32[256,128]{1,0:T(8,128)S(1)}, u32[]{:S(2)}, u32[]{:S(2)}) collective-permute-start(f32[256,128]{1,0:T(8,128)S(1)} %slice_add_fusion.1), channel_id=1, source_target_pairs={{0,2},{1,3},{2,0},{3,1},{4,6},{5,7},{6,4},{7,5},{8,10},{9,11},{10,... | collective-permute-start | bytes 393224 | tf_op jit(solution)/shard_map/ppermute | solution.py:23
  25.9 3.8 %collective-permute-done.1.second_ref = f32[256,128]{1,0:T(8,128)S(1)} collective-permute-done((f32[256,128]{1,0:T(8,128)S(1)}, f32[256,128]{1,0:T(8,128)S(1)}, u32[]{:S(2)}, u32[]{:S(2)}) %collective-permute-start.1) | collective-permute-done | bytes 131104 | tf_op jit(solution)/shard_map/ppermute | solution.py:23
  29.7 6.4 %leaf_orth.1 = (f32[256,128]{1,0:T(8,128)}, f32[128,256]{1,0:T(8,128)S(1)}, f32[256,128]{1,0:T(8,128)S(1)}) custom-call(f32[512,128]{1,0:T(8,128)S(1)} %get-tuple-element.29.keep_ref, f32[512,128]{1,0:T(8,128)S(1)} %collective-permute-done.first_ref, f32[256,128]{1,0:T(8,128)S(1)} %collective-permute-done.1.second_ref, ...), custom_call_target="tpu_custom_call" | custom-call | flops 8000000000 | bytes 24000000 | tf_op jit(solution)/shard_map/leaf_orth/pallas_call | solution.py:234
  36.1 0.0 collective-permute-start.2
  36.1 0.5 collective-permute-start.7
  36.6 0.8 collective-permute-done.2.other_ref
  37.4 0.0 copy-done.2
  37.4 6.3 %merge_orth_0.1 = (f32[128,128]{1,0:T(8,128)S(1)}, f32[2,128,128]{2,1,0:T(8,128)S(1)}, f32[256,128]{1,0:T(8,128)S(1)}) custom-call(f32[256,128]{1,0:T(8,128)S(1)} %get-tuple-element.33.own_ref, f32[256,128]{1,0:T(8,128)S(1)} %collective-permute-done.2.other_ref, bf16[1,5,128,128]{3,2,1,0:T(8,128)(2,1)S(1)} %copy-done.2), custom_call_target="tpu_custom_call" | custom-call | flops 8000000000 | bytes 24000000 | tf_op jit(solution)/shard_map/merge_orth_0/pallas_call | solution.py:291
  43.7 1.8 %collective-permute-start.3 = (f32[256,128]{1,0:T(8,128)S(1)}, f32[256,128]{1,0:T(8,128)S(1)}, u32[]{:S(2)}, u32[]{:S(2)}) collective-permute-start(f32[256,128]{1,0:T(8,128)S(1)} %get-tuple-element.35.own_ref), channel_id=1, source_target_pairs={{0,2},{1,3},{2,0},{3,1},{4,6},{5,7},{6,4},{7,5},{8,10},{9,11},{10,... | collective-permute-start | bytes 393224 | tf_op jit(solution)/shard_map/ppermute | solution.py:23
  45.5 3.8 %collective-permute-done.3.other_ref = f32[256,128]{1,0:T(8,128)S(1)} collective-permute-done((f32[256,128]{1,0:T(8,128)S(1)}, f32[256,128]{1,0:T(8,128)S(1)}, u32[]{:S(2)}, u32[]{:S(2)}) %collective-permute-start.3) | collective-permute-done | bytes 131104 | tf_op jit(solution)/shard_map/ppermute | solution.py:23
  49.3 6.1 %merge_orth_1.1 = (f32[128,128]{1,0:T(8,128)S(1)}, f32[2,128,128]{2,1,0:T(8,128)S(1)}, f32[256,128]{1,0:T(8,128)S(1)}) custom-call(f32[256,128]{1,0:T(8,128)S(1)} %get-tuple-element.35.own_ref, f32[256,128]{1,0:T(8,128)S(1)} %collective-permute-done.3.other_ref, bf16[1,5,128,128]{3,2,1,0:T(8,128)(2,1)S(1)} %copy-done.2), custom_call_target="tpu_custom_call" | custom-call | flops 8000000000 | bytes 24000000 | tf_op jit(solution)/shard_map/merge_orth_1/pallas_call | solution.py:291
  55.4 1.8 %collective-permute-start.4 = (f32[256,128]{1,0:T(8,128)S(1)}, f32[256,128]{1,0:T(8,128)S(1)}, u32[]{:S(2)}, u32[]{:S(2)}) collective-permute-start(f32[256,128]{1,0:T(8,128)S(1)} %get-tuple-element.37.own_ref), channel_id=1, source_target_pairs={{0,4},{1,5},{2,6},{3,7},{4,0},{5,1},{6,2},{7,3},{8,12},{9,13},{10,... | collective-permute-start | bytes 393224 | tf_op jit(solution)/shard_map/ppermute | solution.py:23
  57.2 0.0 collective-permute-done.7.refs_1_
  57.2 0.1 slice_add_fusion
  57.3 1.6 %collective-permute-start.8 = (f32[256,512]{1,0:T(8,128)S(1)}, f32[256,512]{1,0:T(8,128)S(1)}, u32[]{:S(2)}, u32[]{:S(2)}) collective-permute-start(f32[256,512]{1,0:T(8,128)S(1)} %slice_add_fusion), channel_id=1, source_target_pairs={{0,2},{1,3},{2,0},{3,1},{4,6},{5,7},{6,4},{7,5},{8,10},{9,11},{10,... | collective-permute-start | bytes 1572872 | tf_op jit(solution)/shard_map/ppermute | solution.py:23
  58.9 1.6 %collective-permute-done.4.other_ref = f32[256,128]{1,0:T(8,128)S(1)} collective-permute-done((f32[256,128]{1,0:T(8,128)S(1)}, f32[256,128]{1,0:T(8,128)S(1)}, u32[]{:S(2)}, u32[]{:S(2)}) %collective-permute-start.4) | collective-permute-done | bytes 131104 | tf_op jit(solution)/shard_map/ppermute | solution.py:23
  60.4 6.1 %merge_orth_2.1 = (f32[128,128]{1,0:T(8,128)S(1)}, f32[2,128,128]{2,1,0:T(8,128)S(1)}, f32[256,128]{1,0:T(8,128)S(1)}) custom-call(f32[256,128]{1,0:T(8,128)S(1)} %get-tuple-element.37.own_ref, f32[256,128]{1,0:T(8,128)S(1)} %collective-permute-done.4.other_ref, bf16[1,5,128,128]{3,2,1,0:T(8,128)(2,1)S(1)} %copy-done.2), custom_call_target="tpu_custom_call" | custom-call | flops 8000000000 | bytes 24000000 | tf_op jit(solution)/shard_map/merge_orth_2/pallas_call | solution.py:291
  66.5 1.9 %collective-permute-start.5 = (f32[256,128]{1,0:T(8,128)S(1)}, f32[256,128]{1,0:T(8,128)S(1)}, u32[]{:S(2)}, u32[]{:S(2)}) collective-permute-start(f32[256,128]{1,0:T(8,128)S(1)} %get-tuple-element.39.own_ref), channel_id=1, source_target_pairs={{0,8},{1,9},{2,10},{3,11},{4,12},{5,13},{6,14},{7,15},{8,0},{9,1},... | collective-permute-start | bytes 393224 | tf_op jit(solution)/shard_map/ppermute | solution.py:23
  68.4 1.8 %collective-permute-done.8.refs_2_ = f32[256,512]{1,0:T(8,128)S(1)} collective-permute-done((f32[256,512]{1,0:T(8,128)S(1)}, f32[256,512]{1,0:T(8,128)S(1)}, u32[]{:S(2)}, u32[]{:S(2)}) %collective-permute-start.8) | collective-permute-done | bytes 524320 | tf_op jit(solution)/shard_map/ppermute | solution.py:23
  70.2 1.8 %lower_maps.1 = (f32[256,128]{1,0:T(8,128)S(1)}, f32[256,128]{1,0:T(8,128)S(1)}, f32[256,128]{1,0:T(8,128)S(1)}, f32[256,128]{1,0:T(8,128)S(1)}) custom-call(f32[512,512]{1,0:T(8,128)S(1)} %get-tuple-element.43.refs_0_, f32[512,512]{1,0:T(8,128)S(1)} %collective-permute-done.7.refs_1_, f32[256,512]{1,0:T(8,128)S(1)} %collective-permute-done.8.refs_2_, ...), custom_call_target="tpu_custom_call" | custom-call | flops 2000000000 | bytes 6000000 | tf_op jit(solution)/shard_map/lower_maps/pallas_call | solution.py:335
  72.0 1.6 %collective-permute-start.10 = (f32[256,128]{1,0:T(8,128)S(1)}, f32[256,128]{1,0:T(8,128)S(1)}, u32[]{:S(2)}, u32[]{:S(2)}) collective-permute-start(f32[256,128]{1,0:T(8,128)S(1)} %get-tuple-element.50), channel_id=1, source_target_pairs={{0,2},{1,3},{2,0},{3,1},{4,6},{5,7},{6,4},{7,5},{8,10},{9,11},{10,... | collective-permute-start | bytes 393224 | tf_op jit(solution)/shard_map/ppermute | solution.py:23
  73.6 0.0 collective-permute-start.11
  73.6 0.6 collective-permute-start.9
  74.2 3.3 %collective-permute-done.10.refs_2_ = f32[256,128]{1,0:T(8,128)S(1)} collective-permute-done((f32[256,128]{1,0:T(8,128)S(1)}, f32[256,128]{1,0:T(8,128)S(1)}, u32[]{:S(2)}, u32[]{:S(2)}) %collective-permute-start.10) | collective-permute-done | bytes 131104 | tf_op jit(solution)/shard_map/ppermute | solution.py:23
  77.5 1.9 %collective-permute-done.11.refs_3_ = f32[256,128]{1,0:T(8,128)S(1)} collective-permute-done((f32[256,128]{1,0:T(8,128)S(1)}, f32[256,128]{1,0:T(8,128)S(1)}, u32[]{:S(2)}, u32[]{:S(2)}) %collective-permute-start.11) | collective-permute-done | bytes 131104 | tf_op jit(solution)/shard_map/ppermute | solution.py:23
  79.4 0.0 collective-permute-done.9.refs_1_
  79.4 0.3 upper_maps_2.1.refs_0_
  79.7 0.6 collective-permute-start.12
  80.4 0.0 collective-permute-done.5.other_ref
  80.4 6.3 %merge_orth_3.1 = (f32[128,128]{1,0:T(8,128)S(1)}, f32[2,128,128]{2,1,0:T(8,128)S(1)}, f32[256,128]{1,0:T(8,128)S(1)}) custom-call(f32[256,128]{1,0:T(8,128)S(1)} %get-tuple-element.39.own_ref, f32[256,128]{1,0:T(8,128)S(1)} %collective-permute-done.5.other_ref, bf16[1,5,128,128]{3,2,1,0:T(8,128)(2,1)S(1)} %copy-done.2), custom_call_target="tpu_custom_call" | custom-call | flops 8000000000 | bytes 24000000 | tf_op jit(solution)/shard_map/merge_orth_3/pallas_call | solution.py:291
  86.6 2.6 %collective-permute-start.6 = (f32[256,128]{1,0:T(8,128)S(1)}, f32[256,128]{1,0:T(8,128)S(1)}, u32[]{:S(2)}, u32[]{:S(2)}) collective-permute-start(f32[256,128]{1,0:T(8,128)S(1)} %get-tuple-element.41), channel_id=1, source_target_pairs={{0,16},{1,17},{2,18},{3,19},{4,20},{5,21},{6,22},{7,23},{8,24},{9,... | collective-permute-start | bytes 393224 | tf_op jit(solution)/shard_map/ppermute | solution.py:23
  89.3 0.0 collective-permute-done.12.refs_1_
  89.3 0.3 upper_maps_3.1.refs_0_
  89.6 1.6 %collective-permute-start.13 = (f32[256,128]{1,0:T(8,128)S(1)}, f32[256,128]{1,0:T(8,128)S(1)}, u32[]{:S(2)}, u32[]{:S(2)}) collective-permute-start(f32[256,128]{1,0:T(8,128)S(1)} %upper_maps_3.1.refs_0_), channel_id=1, source_target_pairs={{0,8},{1,9},{2,10},{3,11},{4,12},{5,13},{6,14},{7,15},{8,0},{9,1},... | collective-permute-start | bytes 393224 | tf_op jit(solution)/shard_map/ppermute | solution.py:23
  91.2 4.6 %collective-permute-done.6 = f32[256,128]{1,0:T(8,128)S(1)} collective-permute-done((f32[256,128]{1,0:T(8,128)S(1)}, f32[256,128]{1,0:T(8,128)S(1)}, u32[]{:S(2)}, u32[]{:S(2)}) %collective-permute-start.6) | collective-permute-done | bytes 131104 | tf_op jit(solution)/shard_map/ppermute | solution.py:23
  95.8 6.4 %merge_orth_4.1 = (f32[5,128,128]{2,1,0:T(8,128)S(1)}, f32[2,128,128]{2,1,0:T(8,128)S(1)}, f32[256,128]{1,0:T(8,128)}) fusion(f32[5,128,128]{2,1,0:T(8,128)S(1)} %bitcast_dynamic-update-slice_fusion.1, f32[256,128]{1,0:T(8,128)S(1)} %get-tuple-element.41, f32[256,128]{1,0:T(8,128)S(1)} %collective-permute-done.6, bf16[1,5,128,128]{3,2,1,0:T(8,128)(2,1)S(1)} %copy-done.2), kind=kCustom, calls=%fused_computation.2 | custom fusion | flops 8000000000 | bytes 753664 | tf_op jit(solution)/shard_map/merge_orth_4/pallas_call | solution.py:291
  102.3 0.0 collective-permute-done.13.refs_1_
  102.3 0.3 upper_maps_4.1
  102.5 0.8 collective-permute-start.14
  103.3 5.7 %collective-permute-done.14 = f32[128,128]{1,0:T(8,128)S(1)} collective-permute-done((f32[128,128]{1,0:T(8,128)S(1)}, f32[128,128]{1,0:T(8,128)S(1)}, u32[]{:S(2)}, u32[]{:S(2)}) %collective-permute-start.14) | collective-permute-done | bytes 65568 | tf_op jit(solution)/shard_map/ppermute | solution.py:23
  109.0 0.0 copy-start.4
  109.0 1.4 %collective-permute-start.16 = (f32[128,128]{1,0:T(8,128)S(1)}, f32[128,128]{1,0:T(8,128)S(1)}, u32[]{:S(2)}, u32[]{:S(2)}) collective-permute-start(f32[128,128]{1,0:T(8,128)S(1)} %add.11.refs_0_), channel_id=1, source_target_pairs={{0,2},{1,3},{2,0},{3,1},{4,6},{5,7},{6,4},{7,5},{8,10},{9,11},{10,... | collective-permute-start | bytes 196616 | tf_op jit(solution)/shard_map/ppermute | solution.py:23
  110.4 0.0 collective-permute-start.15
  110.4 2.9 %collective-permute-done.16.refs_2_ = f32[128,128]{1,0:T(8,128)S(1)} collective-permute-done((f32[128,128]{1,0:T(8,128)S(1)}, f32[128,128]{1,0:T(8,128)S(1)}, u32[]{:S(2)}, u32[]{:S(2)}) %collective-permute-start.16) | collective-permute-done | bytes 65568 | tf_op jit(solution)/shard_map/ppermute | solution.py:23
  113.4 0.0 collective-permute-start.17
  113.4 0.0 collective-permute-done.15.refs_1_
  113.4 0.0 copy-start.6
  113.4 1.2 %collective-permute-done.17.refs_3_ = f32[128,128]{1,0:T(8,128)S(1)} collective-permute-done((f32[128,128]{1,0:T(8,128)S(1)}, f32[128,128]{1,0:T(8,128)S(1)}, u32[]{:S(2)}, u32[]{:S(2)}) %collective-permute-start.17) | collective-permute-done | bytes 65568 | tf_op jit(solution)/shard_map/ppermute | solution.py:23
  114.6 0.0 copy-done.4
  114.6 0.0 copy-done.5
  114.6 0.0 copy-done.6
  114.6 0.0 copy-start.7
  114.7 0.6 copy-done.7
  115.3 1.7 %top_columns.1 = f32[1,128,512]{2,1,0:T(8,128)} custom-call(f32[128,128]{1,0:T(8,128)} %copy-done.4, f32[128,128]{1,0:T(8,128)} %copy-done.6, f32[128,128]{1,0:T(8,128)} %copy-done.5, f32[128,128]{1,0:T(8,128)} %copy-done.7), custom_call_target="tpu_custom_call" | custom-call | tf_op jit(solution)/shard_map/top_columns/pallas_call | solution.py:420
  116.9 0.0 copy-done.8
  (9 shorter events, 0.1 us)
Async XLA Ops:
  0.6 1.0 copy-start
  1.6 0.9 copy-start.1
  2.5 0.7 copy-start.3
  21.2 1.7 %collective-permute-start = (f32[512,128]{1,0:T(8,128)S(1)}, f32[512,128]{1,0:T(8,128)S(1)}, u32[]{:S(2)}, u32[]{:S(2)}) collective-permute-start(f32[512,128]{1,0:T(8,128)S(1)} %get-tuple-element.30), channel_id=1, source_target_pairs={{0,1},{1,0},{2,3},{3,2},{4,5},{5,4},{6,7},{7,6},{8,9},{9,8},{10,11... | collective-permute-start | bytes 786440 | tf_op jit(solution)/shard_map/ppermute | solution.py:23
  22.9 6.8 %collective-permute-start.1 = (f32[256,128]{1,0:T(8,128)S(1)}, f32[256,128]{1,0:T(8,128)S(1)}, u32[]{:S(2)}, u32[]{:S(2)}) collective-permute-start(f32[256,128]{1,0:T(8,128)S(1)} %slice_add_fusion.1), channel_id=1, source_target_pairs={{0,2},{1,3},{2,0},{3,1},{4,6},{5,7},{6,4},{7,5},{8,10},{9,11},{10,... | collective-permute-start | bytes 393224 | tf_op jit(solution)/shard_map/ppermute | solution.py:23
  29.7 7.7 %copy-start.2 = (bf16[1,5,128,128]{3,2,1,0:T(8,128)(2,1)S(1)}, bf16[1,5,128,128]{3,2,1,0:T(8,128)(2,1)}, u32[]{:S(2)}) copy-start(bf16[1,5,128,128]{3,2,1,0:T(8,128)(2,1)} %coupling_ref.8) | copy-start | bytes 491524
  36.1 1.3 %collective-permute-start.2 = (f32[256,128]{1,0:T(8,128)S(1)}, f32[256,128]{1,0:T(8,128)S(1)}, u32[]{:S(2)}, u32[]{:S(2)}) collective-permute-start(f32[256,128]{1,0:T(8,128)S(1)} %get-tuple-element.33.own_ref), channel_id=1, source_target_pairs={{0,1},{1,0},{2,3},{3,2},{4,5},{5,4},{6,7},{7,6},{8,9},{9,8},{10,11... | collective-permute-start | bytes 393224 | tf_op jit(solution)/shard_map/ppermute | solution.py:23
  36.1 21.1 %collective-permute-start.7 = (f32[512,512]{1,0:T(8,128)S(1)}, f32[512,512]{1,0:T(8,128)S(1)}, u32[]{:S(2)}, u32[]{:S(2)}) collective-permute-start(f32[512,512]{1,0:T(8,128)S(1)} %get-tuple-element.44), channel_id=1, source_target_pairs={{0,1},{1,0},{2,3},{3,2},{4,5},{5,4},{6,7},{7,6},{8,9},{9,8},{10,11... | collective-permute-start | bytes 3145736 | tf_op jit(solution)/shard_map/ppermute | solution.py:23
  43.7 5.6 %collective-permute-start.3 = (f32[256,128]{1,0:T(8,128)S(1)}, f32[256,128]{1,0:T(8,128)S(1)}, u32[]{:S(2)}, u32[]{:S(2)}) collective-permute-start(f32[256,128]{1,0:T(8,128)S(1)} %get-tuple-element.35.own_ref), channel_id=1, source_target_pairs={{0,2},{1,3},{2,0},{3,1},{4,6},{5,7},{6,4},{7,5},{8,10},{9,11},{10,... | collective-permute-start | bytes 393224 | tf_op jit(solution)/shard_map/ppermute | solution.py:23
  55.4 5.0 %collective-permute-start.4 = (f32[256,128]{1,0:T(8,128)S(1)}, f32[256,128]{1,0:T(8,128)S(1)}, u32[]{:S(2)}, u32[]{:S(2)}) collective-permute-start(f32[256,128]{1,0:T(8,128)S(1)} %get-tuple-element.37.own_ref), channel_id=1, source_target_pairs={{0,4},{1,5},{2,6},{3,7},{4,0},{5,1},{6,2},{7,3},{8,12},{9,13},{10,... | collective-permute-start | bytes 393224 | tf_op jit(solution)/shard_map/ppermute | solution.py:23
  57.3 12.9 %collective-permute-start.8 = (f32[256,512]{1,0:T(8,128)S(1)}, f32[256,512]{1,0:T(8,128)S(1)}, u32[]{:S(2)}, u32[]{:S(2)}) collective-permute-start(f32[256,512]{1,0:T(8,128)S(1)} %slice_add_fusion), channel_id=1, source_target_pairs={{0,2},{1,3},{2,0},{3,1},{4,6},{5,7},{6,4},{7,5},{8,10},{9,11},{10,... | collective-permute-start | bytes 1572872 | tf_op jit(solution)/shard_map/ppermute | solution.py:23
  66.5 13.8 %collective-permute-start.5 = (f32[256,128]{1,0:T(8,128)S(1)}, f32[256,128]{1,0:T(8,128)S(1)}, u32[]{:S(2)}, u32[]{:S(2)}) collective-permute-start(f32[256,128]{1,0:T(8,128)S(1)} %get-tuple-element.39.own_ref), channel_id=1, source_target_pairs={{0,8},{1,9},{2,10},{3,11},{4,12},{5,13},{6,14},{7,15},{8,0},{9,1},... | collective-permute-start | bytes 393224 | tf_op jit(solution)/shard_map/ppermute | solution.py:23
  72.0 5.5 %collective-permute-start.10 = (f32[256,128]{1,0:T(8,128)S(1)}, f32[256,128]{1,0:T(8,128)S(1)}, u32[]{:S(2)}, u32[]{:S(2)}) collective-permute-start(f32[256,128]{1,0:T(8,128)S(1)} %get-tuple-element.50), channel_id=1, source_target_pairs={{0,2},{1,3},{2,0},{3,1},{4,6},{5,7},{6,4},{7,5},{8,10},{9,11},{10,... | collective-permute-start | bytes 393224 | tf_op jit(solution)/shard_map/ppermute | solution.py:23
  73.6 5.8 %collective-permute-start.11 = (f32[256,128]{1,0:T(8,128)S(1)}, f32[256,128]{1,0:T(8,128)S(1)}, u32[]{:S(2)}, u32[]{:S(2)}) collective-permute-start(f32[256,128]{1,0:T(8,128)S(1)} %get-tuple-element.51), channel_id=1, source_target_pairs={{0,3},{1,2},{2,1},{3,0},{4,7},{5,6},{6,5},{7,4},{8,11},{9,10},{10,... | collective-permute-start | bytes 393224 | tf_op jit(solution)/shard_map/ppermute | solution.py:23
  73.6 5.8 %collective-permute-start.9 = (f32[256,128]{1,0:T(8,128)S(1)}, f32[256,128]{1,0:T(8,128)S(1)}, u32[]{:S(2)}, u32[]{:S(2)}) collective-permute-start(f32[256,128]{1,0:T(8,128)S(1)} %get-tuple-element.49), channel_id=1, source_target_pairs={{0,1},{1,0},{2,3},{3,2},{4,5},{5,4},{6,7},{7,6},{8,9},{9,8},{10,11... | collective-permute-start | bytes 393224 | tf_op jit(solution)/shard_map/ppermute | solution.py:23
  79.7 9.5 %collective-permute-start.12 = (f32[256,128]{1,0:T(8,128)S(1)}, f32[256,128]{1,0:T(8,128)S(1)}, u32[]{:S(2)}, u32[]{:S(2)}) collective-permute-start(f32[256,128]{1,0:T(8,128)S(1)} %upper_maps_2.1.refs_0_), channel_id=1, source_target_pairs={{0,4},{1,5},{2,6},{3,7},{4,0},{5,1},{6,2},{7,3},{8,12},{9,13},{10,... | collective-permute-start | bytes 393224 | tf_op jit(solution)/shard_map/ppermute | solution.py:23
  86.6 9.2 %collective-permute-start.6 = (f32[256,128]{1,0:T(8,128)S(1)}, f32[256,128]{1,0:T(8,128)S(1)}, u32[]{:S(2)}, u32[]{:S(2)}) collective-permute-start(f32[256,128]{1,0:T(8,128)S(1)} %get-tuple-element.41), channel_id=1, source_target_pairs={{0,16},{1,17},{2,18},{3,19},{4,20},{5,21},{6,22},{7,23},{8,24},{9,... | collective-permute-start | bytes 393224 | tf_op jit(solution)/shard_map/ppermute | solution.py:23
  89.6 12.7 %collective-permute-start.13 = (f32[256,128]{1,0:T(8,128)S(1)}, f32[256,128]{1,0:T(8,128)S(1)}, u32[]{:S(2)}, u32[]{:S(2)}) collective-permute-start(f32[256,128]{1,0:T(8,128)S(1)} %upper_maps_3.1.refs_0_), channel_id=1, source_target_pairs={{0,8},{1,9},{2,10},{3,11},{4,12},{5,13},{6,14},{7,15},{8,0},{9,1},... | collective-permute-start | bytes 393224 | tf_op jit(solution)/shard_map/ppermute | solution.py:23
  102.3 14.7 %copy-start.8 = (f32[5,128,128]{2,1,0:T(8,128)}, f32[5,128,128]{2,1,0:T(8,128)S(1)}, u32[]{:S(2)}) copy-start(f32[5,128,128]{2,1,0:T(8,128)S(1)} %get-tuple-element.58) | copy-start | bytes 983044
  102.5 6.5 %collective-permute-start.14 = (f32[128,128]{1,0:T(8,128)S(1)}, f32[128,128]{1,0:T(8,128)S(1)}, u32[]{:S(2)}, u32[]{:S(2)}) collective-permute-start(f32[128,128]{1,0:T(8,128)S(1)} %upper_maps_4.1), channel_id=1, source_target_pairs={{0,16},{1,17},{2,18},{3,19},{4,20},{5,21},{6,22},{7,23},{8,24},{9,... | collective-permute-start | bytes 196616 | tf_op jit(solution)/shard_map/ppermute | solution.py:23
  109.0 5.6 %copy-start.4 = (f32[128,128]{1,0:T(8,128)}, f32[128,128]{1,0:T(8,128)S(1)}, u32[]{:S(2)}) copy-start(f32[128,128]{1,0:T(8,128)S(1)} %add.11.refs_0_) | copy-start | bytes 196612
  109.0 4.3 %collective-permute-start.16 = (f32[128,128]{1,0:T(8,128)S(1)}, f32[128,128]{1,0:T(8,128)S(1)}, u32[]{:S(2)}, u32[]{:S(2)}) collective-permute-start(f32[128,128]{1,0:T(8,128)S(1)} %add.11.refs_0_), channel_id=1, source_target_pairs={{0,2},{1,3},{2,0},{3,1},{4,6},{5,7},{6,4},{7,5},{8,10},{9,11},{10,... | collective-permute-start | bytes 196616 | tf_op jit(solution)/shard_map/ppermute | solution.py:23
  110.4 3.0 %collective-permute-start.15 = (f32[128,128]{1,0:T(8,128)S(1)}, f32[128,128]{1,0:T(8,128)S(1)}, u32[]{:S(2)}, u32[]{:S(2)}) collective-permute-start(f32[128,128]{1,0:T(8,128)S(1)} %add.11.refs_0_), channel_id=1, source_target_pairs={{0,1},{1,0},{2,3},{3,2},{4,5},{5,4},{6,7},{7,6},{8,9},{9,8},{10,11... | collective-permute-start | bytes 196616 | tf_op jit(solution)/shard_map/ppermute | solution.py:23
  113.4 1.3 %copy-start.5 = (f32[128,128]{1,0:T(8,128)}, f32[128,128]{1,0:T(8,128)S(1)}, u32[]{:S(2)}) copy-start(f32[128,128]{1,0:T(8,128)S(1)} %collective-permute-done.16.refs_2_) | copy-start | bytes 196612
  113.4 1.3 %collective-permute-start.17 = (f32[128,128]{1,0:T(8,128)S(1)}, f32[128,128]{1,0:T(8,128)S(1)}, u32[]{:S(2)}, u32[]{:S(2)}) collective-permute-start(f32[128,128]{1,0:T(8,128)S(1)} %collective-permute-done.16.refs_2_), channel_id=1, source_target_pairs={{0,1},{1,0},{2,3},{3,2},{4,5},{5,4},{6,7},{7,6},{8,9},{9,8},{10,11... | collective-permute-start | bytes 196616 | tf_op jit(solution)/shard_map/ppermute | solution.py:23
  113.4 1.3 %copy-start.6 = (f32[128,128]{1,0:T(8,128)}, f32[128,128]{1,0:T(8,128)S(1)}, u32[]{:S(2)}) copy-start(f32[128,128]{1,0:T(8,128)S(1)} %collective-permute-done.15.refs_1_) | copy-start | bytes 196612
  114.6 0.6 copy-start.7
where the time goes:
time: 117 us
  Pallas kernels  53.4 us (46%)
  waiting for transfers between devices  32.7 us (28%)
  starting transfers between devices  20.3 us (17%)
  other arithmetic  6.56 us (6%)
  local copies, waits for them, and re-layouts  3.22 us (3%)
    ppermute x18, waiting for transfers between devices, from_partner(): return lax.ppermute(block, axis, route)  32.7 us
    pallas_call x4, Pallas kernels, merge_step(): pl.pallas_call(functools.partial(merge_body, tree_level), grid=(1,), out_...  24.7 us
    ppermute x18, starting transfers between devices, from_partner(): return lax.ppermute(block, axis, route)  20.3 us
    pallas_call x1, Pallas kernels, sample_rows(): pl.pallas_call(spmm_body, out_shape=[jax.ShapeDtypeStruct((half, width),...  18 us
    pallas_call x1, other arithmetic, merge_step(): pl.pallas_call(functools.partial(merge_body, tree_level), grid=(1,), out_...  6.45 us
    pallas_call x1, Pallas kernels, leaf_step(): pl.pallas_call(leaf_body, grid=(1,), out_shape=[jax.ShapeDtypeStruct((lea...  6.39 us
    unnamed x22, local copies, waits for them, and re-layouts  3.22 us
  transfers between devices with their start and end apart: 18, of which 12 were waited for; matrix products, arithmetic and copies ran while one was open for 6% of the time, Pallas kernels for 23%

commit v1 on v0

--- a/solution.py
+++ b/solution.py
@@ -11,6 +11,8 @@
 LEVELS = 5
 ROW_COL = ("row", "col")
 VMEM = pl.BlockSpec(memory_space=pltpu.VMEM)
+ANY = pl.BlockSpec(memory_space=pl.ANY)
+HBM = pl.BlockSpec(memory_space=pltpu.HBM)
 
 
 def from_partner(block, axis, distance):
@@ -94,6 +96,25 @@
     return jnp.concatenate(found, axis=0)
 
 
+def in_parts(block):
+    high = block.astype(jnp.bfloat16)
+    rest = block - high.astype(jnp.float32)
+    middle = rest.astype(jnp.bfloat16)
+    return high, middle, (rest - middle.astype(jnp.float32)).astype(jnp.bfloat16)
+
+
+def short_dot(left, right):
+    return jnp.dot(left, right, preferred_element_type=jnp.float32)
+
+
+def quotient(value, divisor, below):
+    shift = 20
+    factor = -(-(2**shift) // divisor)
+    assert all(v * factor >> shift == v // divisor for v in range(below))
+    assert below * factor < 2**31
+    return value * factor >> shift
+
+
 def spmm_body(
     slots_ref,
     tiles_ref,
@@ -107,46 +128,70 @@
     sketch_red_ref,
     dense,
     held,
+    slots,
+    sub,
+    leaf_sketch,
     tile_sem,
     sketch_sems,
+    small_sems,
 ):
     tile_count, tile_size, _ = tiles_ref.shape
     depth = sketch_ref.shape[0]
     rows = dense.shape[0]
     half = rows // 2
+    rank = sub.shape[1]
     col_tiles = depth // tile_size
     chunks = sketch_sems.shape[0]
     chunk = depth // chunks
     leaf_tiles = leaf_sketch_ref.shape[0] // tile_size
     leaves = rows // leaf_sketch_ref.shape[0]
     me = lax.axis_index("col")
+    small = [
+        pltpu.make_async_copy(source, target, small_sems.at[k])
+        for k, (source, target) in enumerate(
+            ((slots_ref, slots), (sub_ref, sub), (leaf_sketch_ref, leaf_sketch))
+        )
+    ]
     loads = [
         pltpu.make_async_copy(
             sketch_ref.at[pl.ds(k * chunk, chunk)], held.at[pl.ds(k * chunk, chunk)], sketch_sems.at[k]
         )
         for k in range(chunks)
     ]
+    for load in small + loads:
+        load.start()
 
     @pl.loop(0, rows // 64)
     def _(i):
         dense[pl.ds(pl.multiple_of(i * 64, 64), 64), :] = jnp.zeros((64, depth), dense.dtype)
 
-    @pl.loop(0, tile_count)
-    def _(t):
-        slot = slots_ref[t]
-        row_tile = slot // col_tiles
-        away = (row_tile // leaf_tiles) ^ me
-        block = away % 2 * (leaves // 2) + away // 2
-        row = pl.multiple_of((block * leaf_tiles + row_tile % leaf_tiles) * tile_size, tile_size)
-        col = pl.multiple_of(slot % col_tiles * tile_size, tile_size)
-        pltpu.make_async_copy(
-            tiles_ref.at[t], dense.at[pl.ds(row, tile_size), pl.ds(col, tile_size)], tile_sem
-        ).start()
-
-    for load in loads:
-        load.start()
-    subsketch = sub_ref[...]
-    sketch_red_ref[...] = dot(leaf_sketch_ref[...].astype(jnp.float32), subsketch)
+    small[0].wait()
+    together = math.gcd(tile_count, 8)
+
+    @pl.loop(0, tile_count // together)
+    def _(group):
+        for member in range(together):
+            t = group * together + member
+            slot = slots[t]
+            row_tile = quotient(slot, col_tiles, rows // tile_size * col_tiles)
+            column = slot - row_tile * col_tiles
+            leaf = quotient(row_tile, leaf_tiles, rows // tile_size)
+            away = leaf ^ me
+            block = (away & 1) * (leaves // 2) + (away >> 1)
+            row = pl.multiple_of((block * leaf_tiles + row_tile - leaf * leaf_tiles) * tile_size, tile_size)
+            col = pl.multiple_of(column * tile_size, tile_size)
+            pltpu.make_async_copy(
+                tiles_ref.at[t], dense.at[pl.ds(row, tile_size), pl.ds(col, tile_size)], tile_sem
+            ).start()
+
+    small[1].wait()
+    small[2].wait()
+    high, middle, low = in_parts(sub[...])
+    two = jnp.concatenate([high, middle], axis=1)
+    sketch_two = short_dot(leaf_sketch[...], two)
+    sketch_red_ref[...] = sketch_two[:, :rank] + (
+        sketch_two[:, rank:] + short_dot(leaf_sketch[...], low)
+    )
     pltpu.make_async_copy(tiles_ref, tiles_ref, tile_sem).wait()
     for k in range(chunks):
         loads[k].wait()
@@ -160,8 +205,11 @@
                 ref[...] = part
             else:
                 ref[...] += part
-    send_red_ref[...] = dot(send_ref[...], subsketch)
-    keep_red_ref[...] = dot(keep_ref[...], subsketch)
+    for ref, red_ref in ((send_ref, send_red_ref), (keep_ref, keep_red_ref)):
+        first, second, third = in_parts(ref[...])
+        wide = short_dot(second, two) + short_dot(first, two)
+        rest = short_dot(third, high) + short_dot(first, low)
+        red_ref[...] = wide[:, :rank] + (wide[:, rank:] + rest)
 
 
 def sample_rows(tiles, tile_slots, sketch, subsketch, row_sketch):
@@ -182,19 +230,17 @@
             jax.ShapeDtypeStruct((half, rank), f32),
             jax.ShapeDtypeStruct((leaf, rank), f32),
         ],
-        in_specs=[
-            pl.BlockSpec(memory_space=pltpu.SMEM),
-            pl.BlockSpec(memory_space=pl.ANY),
-            pl.BlockSpec(memory_space=pl.ANY),
-            VMEM,
-            VMEM,
-        ],
+        in_specs=[HBM] * 5,
         out_specs=[VMEM] * 5,
         scratch_shapes=[
             pltpu.VMEM((rows, depth), jnp.bfloat16),
             pltpu.VMEM((depth, width), jnp.bfloat16),
+            pltpu.SMEM(tile_slots.shape, jnp.int32),
+            pltpu.VMEM(subsketch.shape, f32),
+            pltpu.VMEM(row_sketch.shape, jnp.bfloat16),
             pltpu.SemaphoreType.DMA,
             pltpu.SemaphoreType.DMA((chunks,)),
+            pltpu.SemaphoreType.DMA((3,)),
         ],
         compiler_params=pltpu.CompilerParams(vmem_limit_bytes=48 * 2**20),
         cost_estimate=pl.CostEstimate(
@@ -206,7 +252,7 @@
     )(tile_slots, tiles, sketch, subsketch, row_sketch)
 
 
-def leaf_body(keep_ref, first_ref, second_ref, sketch_red_ref, basis_ref, basis_t_ref, pair_ref):
+def leaf_body(keep_ref, first_ref, second_ref, sketch_red_ref, _, basis_ref, basis_t_ref, pair_ref):
     rank = keep_ref.shape[-1]
     reduced = keep_ref[...] + first_ref[...] + second_ref[...]
     reduced_t = reduced.T
@@ -227,7 +273,7 @@
     return pl.CostEstimate(flops=micros * 10**9, bytes_accessed=micros * 3 * 10**6, transcendentals=0)
 
 
-def leaf_step(keep, first, second, sketch_red):
+def leaf_step(keep, first, second, sketch_red, after):
     leaf, rank = sketch_red.shape
     f32 = jnp.float32
     part = pl.BlockSpec((leaf, rank), lambda step: (0, 0))
@@ -239,12 +285,12 @@
             jax.ShapeDtypeStruct((rank, leaf), f32),
             jax.ShapeDtypeStruct((2 * rank, rank), f32),
         ],
-        in_specs=[part, part, VMEM, VMEM],
+        in_specs=[part, part, VMEM, VMEM, ANY],
         out_specs=[VMEM] * 3,
         compiler_params=small_params(),
         cost_estimate=small_cost(8),
         name="leaf_orth",
-    )(keep, first, second, sketch_red)
+    )(keep, first, second, sketch_red, after)
 
 
 def turned(coupling_ref, tree_level):
@@ -255,7 +301,10 @@
     return jnp.where(upper, coupling_t, coupling), jnp.where(upper, coupling, coupling_t)
 
 
-def merge_body(tree_level, own_ref, other_ref, coupling_ref, block_ref, maps_ref, pair_ref):
+def merge_body(tree_level, *refs):
+    own_ref, other_ref, coupling_ref = refs[:3]
+    block_ref, maps_ref, pair_ref = refs[-3:]
+    last = tree_level == LEVELS - 1
     rank = own_ref.shape[-1]
     ahead, back = turned(coupling_ref, tree_level)
     own_sample, own_sketch = own_ref[:rank], own_ref[rank:]
@@ -273,10 +322,13 @@
     )
     both = dot(stacked_t, right)
     inverse = inverse_factor(both[:, :rank])
+    block_ref[...] = dot_nt(own, inverse)
+    if last:
+        pair_ref[...] = dot(inverse, stacked_t)
+        return
     moved = dot(inverse, both)
     pair_ref[:rank, :] = moved[:, :rank]
     pair_ref[rank:, :] = moved[:, rank:]
-    block_ref[...] = dot_nt(own, inverse)
     maps_ref[0] = dot(inverse, own_t)
     maps_ref[1] = dot(inverse, dot(other_t, back))
 
@@ -285,23 +337,24 @@
     return pl.BlockSpec((1, 1) + couplings.shape[2:], lambda step: (0, tree_level, 0, 0))
 
 
-def merge_step(tree_level, own, other, couplings):
+def merge_step(tree_level, own, other, couplings, after):
     rank = own.shape[1]
     f32 = jnp.float32
+    last = tree_level == LEVELS - 1
     return pl.pallas_call(
         functools.partial(merge_body, tree_level),
         grid=(1,),
         out_shape=[
             jax.ShapeDtypeStruct((rank, rank), f32),
-            jax.ShapeDtypeStruct((2, rank, rank), f32),
-            jax.ShapeDtypeStruct((2 * rank, rank), f32),
+            jax.ShapeDtypeStruct((8, rank) if last else (2, rank, rank), f32),
+            jax.ShapeDtypeStruct((rank, 2 * rank) if last else (2 * rank, rank), f32),
         ],
-        in_specs=[VMEM, VMEM, coupling_spec(couplings, tree_level)],
-        out_specs=[VMEM] * 3,
+        in_specs=[VMEM, VMEM, coupling_spec(couplings, tree_level)] + [ANY] * len(after),
+        out_specs=[VMEM, ANY if last else VMEM, VMEM],
         compiler_params=small_params(),
         cost_estimate=small_cost(8),
         name=f"merge_orth_{tree_level}",
-    )(own, other, couplings)
+    )(own, other, couplings, *after)
 
 
 def lower_body(*refs):
@@ -345,7 +398,7 @@
     )(keep, first, second, row_sketch, basis_t, *maps)
 
 
-def upper_body(last, *refs):
+def upper_body(*refs):
     maps_ref, out_ref = refs[-2:]
     total = refs[0][...]
     for ref in refs[1:-2]:
@@ -354,16 +407,13 @@
     sample, sketch = total[:rank], total[rank:]
     lifted = maps_ref[0]
     out_ref[:rank, :] = dot(lifted, sample) - dot(maps_ref[1], sketch)
-    if not last:
-        out_ref[rank:, :] = dot(lifted, sketch)
+    out_ref[rank:, :] = dot(lifted, sketch)
 
 
 def upper_step(tree_level, parts, maps):
-    last = tree_level == LEVELS - 1
-    rows, width = parts[0].shape
-    return pl.pallas_call(
-        functools.partial(upper_body, last),
-        out_shape=jax.ShapeDtypeStruct((rows // 2 if last else rows, width), jnp.float32),
+    return pl.pallas_call(
+        upper_body,
+        out_shape=jax.ShapeDtypeStruct(parts[0].shape, jnp.float32),
         in_specs=[VMEM] * (len(parts) + 1),
         out_specs=VMEM,
         compiler_params=small_params(),
@@ -372,12 +422,59 @@
     )(*parts, maps)
 
 
-def top_body(ways, *refs):
-    out_ref = refs[-1]
+def top_body(own_ref, other_ref, coupling_ref, basis_t_ref, out_ref):
+    rank = own_ref.shape[0] // 2
+    ahead, back = turned(coupling_ref, LEVELS - 1)
+    own = own_ref[:rank] - dot(ahead, other_ref[rank:])
+    other = other_ref[:rank] - dot(back, own_ref[rank:])
+    out_ref[...] = dot(basis_t_ref[...], jnp.concatenate([own, other], axis=0))
+
+
+def top_step(own, other, couplings, basis_t):
+    return pl.pallas_call(
+        top_body,
+        grid=(1,),
+        out_shape=jax.ShapeDtypeStruct((own.shape[0] // 2, own.shape[1]), jnp.float32),
+        in_specs=[VMEM, VMEM, coupling_spec(couplings, LEVELS - 1), VMEM],
+        out_specs=VMEM,
+        compiler_params=small_params(),
+        cost_estimate=small_cost(1),
+        name="top_sample",
+    )(own, other, couplings, basis_t)
+
+
+def columns_body(*refs):
+    sems = refs[-1]
+    out_ref = refs[-2]
+    pieces = refs[:-2]
+    ways = len(pieces)
     me = lax.axis_index("col")
     part = out_ref.shape[2] // ways
-    for away in range(ways):
-        out_ref[0, :, pl.ds(pl.multiple_of((me ^ away) * part, part), part)] = refs[away][...]
+    copies = [
+        pltpu.make_async_copy(
+            pieces[away],
+            out_ref.at[0, :, pl.ds(pl.multiple_of((me ^ away) * part, part), part)],
+            sems.at[away],
+        )
+        for away in range(ways)
+    ]
+    for copy in copies:
+        copy.start()
+    for copy in copies:
+        copy.wait()
+
+
+def columns_step(pieces):
+    rank, part = pieces[0].shape
+    ways = len(pieces)
+    return pl.pallas_call(
+        columns_body,
+        out_shape=jax.ShapeDtypeStruct((1, rank, part * ways), jnp.float32),
+        in_specs=[VMEM] * ways,
+        out_specs=ANY,
+        scratch_shapes=[pltpu.SemaphoreType.DMA((ways,))],
+        name="top_columns",
+    )(*pieces)
 
 
 def per_device(tiles, tile_slots, sketch, row_sketch, subsketch, couplings):
@@ -387,45 +484,39 @@
     keep, send, keep_red, send_red, sketch_red = sample_rows(
         tiles, tile_slots, sketch, subsketch, row_sketch
     )
-
-    def gathered(kept, sent):
-        first = from_partner(sent, "col", 1)
-        second = from_partner(kept[leaf:] + first[leaf:], "col", 2)
-        return kept, first, second
-
-    reduced = gathered(keep_red, send_red)
-    samples = gathered(keep, send)
-    leaf_basis, basis_t, pair = leaf_step(*reduced, sketch_red)
-    blocks, low_maps, parts = [], [], []
+    first_red = from_partner(send_red, "col", 1)
+    first = from_partner(send, "col", 1)
+    second_red = from_partner(keep_red[leaf:] + first_red[leaf:], "col", 2)
+    passed = keep[leaf:] + first[leaf:]
+    second = from_partner(passed, "col", 2)
+    leaf_basis, basis_t, pair = leaf_step(keep_red, first_red, second_red, sketch_red, passed)
+    blocks, low_maps, after, parts = [], [], [], []
     for tree_level in range(LEVELS):
         other = from_partner(pair, ROW_COL, 2**tree_level)
-        block, maps, pair = merge_step(tree_level, pair, other, couplings)
+        if tree_level == col_bits - 1:
+            after = [second]
+        block, maps, pair = merge_step(tree_level, pair, other, couplings, after)
         blocks.append(block)
+        if tree_level == LEVELS - 1:
+            break
         if tree_level < col_bits:
             low_maps.append(maps)
         else:
             mine = upper_step(tree_level, parts, maps)
             parts = [mine, from_partner(mine, ROW_COL, 2**tree_level)]
+            after = [mine]
         if tree_level == col_bits - 1:
-            cut = lower_step(*samples, row_sketch, basis_t, low_maps)
+            cut = lower_step(keep, first, second, row_sketch, basis_t, low_maps)
             parts = [cut[0]] + [from_partner(cut[away], "col", away) for away in range(1, ways)]
-    top = [parts[0] + parts[1]]
-    for bit in reversed(range(col_bits)):
-        top += [from_partner(piece, "col", 2**bit) for piece in top]
-    order = [0]
-    for bit in reversed(range(col_bits)):
-        order += [away ^ 2**bit for away in order]
-    pieces = [top[order.index(away)] for away in range(ways)]
-    rank, part = pieces[0].shape
-    top_sample = pl.pallas_call(
-        functools.partial(top_body, ways),
-        out_shape=jax.ShapeDtypeStruct((1, rank, part * ways), jnp.float32),
-        in_specs=[VMEM] * ways,
-        out_specs=VMEM,
-        name="top_columns",
-    )(*pieces)
+            after = [cut[0]]
+        if tree_level == LEVELS - 2:
+            whole = parts[0] + parts[1]
+            far = from_partner(whole, ROW_COL, 2 ** (LEVELS - 1))
+            after = [whole]
+    top = top_step(whole, far, couplings, pair)
+    pieces = [top] + [from_partner(top, "col", away) for away in range(1, ways)]
     transfer = jnp.stack(blocks, axis=0)[None]
-    return (leaf_basis, transfer, top_sample)
+    return (leaf_basis, transfer, columns_step(pieces))
 
 
 def solution(mesh):

time: 117 us -> 106 us (0.906)
  waiting for transfers between devices: 32.7 us -> 26 us
  Pallas kernels: 53.4 us -> 48.3 us
    ppermute x18, waiting for transfers between devices: 32.7 us -> 26 us  [from_partner(): return lax.ppermute(block, axis, route)]
    pallas_call x1, Pallas kernels: 18 us -> 12.4 us  [sample_rows(): pl.pallas_call(spmm_body, out_shape=[jax.ShapeDtypeStruct((half, width),...]
  transfers between devices with their start and end apart: 18 -> 18, of which waited for: 12 -> 8; matrix products, arithmetic and copies ran while one was open for 6% -> 6% of each run, Pallas kernels for 23% -> 20%
where the time goes in v1:
time: 106 us
  Pallas kernels  48.3 us (46%)
  waiting for transfers between devices  26 us (25%)
  starting transfers between devices  21.3 us (20%)
  other arithmetic  6 us (6%)
  local copies, waits for them, and re-layouts  3.23 us (3%)
    ppermute x18, waiting for transfers between devices, from_partner(): return lax.ppermute(block, axis, route)  26 us
    pallas_call x4, Pallas kernels, merge_step(): pl.pallas_call(functools.partial(merge_body, tree_level), grid=(1,), out_...  24.8 us
    ppermute x18, starting transfers between devices, from_partner(): return lax.ppermute(block, axis, route)  21.3 us
    pallas_call x1, Pallas kernels, sample_rows(): pl.pallas_call(spmm_body, out_shape=[jax.ShapeDtypeStruct((half, width),...  12.4 us
    pallas_call x1, Pallas kernels, leaf_step(): pl.pallas_call(leaf_body, grid=(1,), out_shape=[jax.ShapeDtypeStruct((lea...  6.39 us
    pallas_call x1, other arithmetic, merge_step(): pl.pallas_call(functools.partial(merge_body, tree_level), grid=(1,), out_...  5.89 us
    unnamed x22, local copies, waits for them, and re-layouts  3.23 us
  transfers between devices with their start and end apart: 18, of which 8 were waited for; matrix products, arithmetic and copies ran while one was open for 6% of the time, Pallas kernels for 20%

profile of v1, /device:TPU:0, one launch (start us, length us, event | category | flops | bytes accessed | tf_op | source)
XLA Modules:
  0.0 105.8 jit_solution(3511976965293023742)
XLA Ops:
  0.6 0.0 copy-start.1
  0.6 0.9 copy-done.1
  1.6 0.0 copy-start.2
  1.6 0.9 copy-done.2
  2.5 0.0 copy-start.4
  2.5 0.7 copy-done.4
  3.2 12.4 %spmm.1 = (f32[512,512]{1,0:T(8,128)S(1)}, f32[512,512]{1,0:T(8,128)S(1)}, f32[512,128]{1,0:T(8,128)S(1)}, f32[512,128]{1,0:T(8,128)S(1)}, f32[256,128]{1,0:T(8,128)S(1)}) custom-call(s32[168]{0:T(256)S(1)} %copy-done.4, bf16[168,128,128]{2,1,0:T(8,128)(2,1)} %tiles_ref.1, bf16[6144,512]{1,0:T(8,128)(2,1)} %sketch_ref.1, f32[512,128]{1,0:T(8,128)S(1)} %copy-done.1, ...), custom_call_target="tpu_custom_call" | custom-call | flops 6442450944 | bytes 13893632 | tf_op jit(solution)/shard_map/spmm/pallas_call | solution.py:224
  15.7 0.5 collective-permute-start.2
  16.2 0.1 collective-permute-start
  16.3 2.6 %collective-permute-done.first_ref = f32[512,128]{1,0:T(8,128)S(1)} collective-permute-done((f32[512,128]{1,0:T(8,128)S(1)}, f32[512,128]{1,0:T(8,128)S(1)}, u32[]{:S(2)}, u32[]{:S(2)}) %collective-permute-start) | collective-permute-done | bytes 262176 | tf_op jit(solution)/shard_map/ppermute | solution.py:25
  18.9 3.0 %collective-permute-start.1 = (f32[256,128]{1,0:T(8,128)S(1)}, f32[256,128]{1,0:T(8,128)S(1)}, u32[]{:S(2)}, u32[]{:S(2)}) collective-permute-start(f32[256,128]{1,0:T(8,128)S(1)} %slice_add_fusion.1), channel_id=1, source_target_pairs={{0,2},{1,3},{2,0},{3,1},{4,6},{5,7},{6,4},{7,5},{8,10},{9,11},{10,... | collective-permute-start | bytes 393224 | tf_op jit(solution)/shard_map/ppermute | solution.py:25
  21.8 0.0 collective-permute-done.2.refs_1_
  21.8 0.1 slice_add_fusion._
  21.9 3.7 %collective-permute-done.1.second_ref = f32[256,128]{1,0:T(8,128)S(1)} collective-permute-done((f32[256,128]{1,0:T(8,128)S(1)}, f32[256,128]{1,0:T(8,128)S(1)}, u32[]{:S(2)}, u32[]{:S(2)}) %collective-permute-start.1) | collective-permute-done | bytes 131104 | tf_op jit(solution)/shard_map/ppermute | solution.py:25
  25.6 6.4 %leaf_orth.1 = (f32[256,128]{1,0:T(8,128)}, f32[128,256]{1,0:T(8,128)S(1)}, f32[256,128]{1,0:T(8,128)S(1)}) custom-call(f32[512,128]{1,0:T(8,128)S(1)} %get-tuple-element.29.keep_ref, f32[512,128]{1,0:T(8,128)S(1)} %collective-permute-done.first_ref, f32[256,128]{1,0:T(8,128)S(1)} %collective-permute-done.1.second_ref, ...), custom_call_target="tpu_custom_call" | custom-call | flops 8000000000 | bytes 24000000 | tf_op jit(solution)/shard_map/leaf_orth/pallas_call | solution.py:280
  32.0 0.0 collective-permute-start.3
  32.0 1.7 %collective-permute-start.5 = (f32[256,512]{1,0:T(8,128)S(1)}, f32[256,512]{1,0:T(8,128)S(1)}, u32[]{:S(2)}, u32[]{:S(2)}) collective-permute-start(f32[256,512]{1,0:T(8,128)S(1)} %slice_add_fusion._), channel_id=1, source_target_pairs={{0,2},{1,3},{2,0},{3,1},{4,6},{5,7},{6,4},{7,5},{8,10},{9,11},{10,... | collective-permute-start | bytes 1572872 | tf_op jit(solution)/shard_map/ppermute | solution.py:25
  33.7 0.0 collective-permute-done.3.refs_1_
  33.8 0.0 copy-done.3
  33.8 6.1 %merge_orth_0.1 = (f32[128,128]{1,0:T(8,128)S(1)}, f32[2,128,128]{2,1,0:T(8,128)S(1)}, f32[256,128]{1,0:T(8,128)S(1)}) custom-call(f32[256,128]{1,0:T(8,128)S(1)} %get-tuple-element.35.refs_0_, f32[256,128]{1,0:T(8,128)S(1)} %collective-permute-done.3.refs_1_, bf16[1,5,128,128]{3,2,1,0:T(8,128)(2,1)S(1)} %copy-done.3), custom_call_target="tpu_custom_call" | custom-call | flops 8000000000 | bytes 24000000 | tf_op jit(solution)/shard_map/merge_orth_0/pallas_call | solution.py:344
  39.9 1.4 %collective-permute-start.4 = (f32[256,128]{1,0:T(8,128)S(1)}, f32[256,128]{1,0:T(8,128)S(1)}, u32[]{:S(2)}, u32[]{:S(2)}) collective-permute-start(f32[256,128]{1,0:T(8,128)S(1)} %get-tuple-element.37.refs_0_), channel_id=1, source_target_pairs={{0,2},{1,3},{2,0},{3,1},{4,6},{5,7},{6,4},{7,5},{8,10},{9,11},{10,... | collective-permute-start | bytes 393224 | tf_op jit(solution)/shard_map/ppermute | solution.py:25
  41.3 7.9 %collective-permute-done.4.refs_1_ = f32[256,128]{1,0:T(8,128)S(1)} collective-permute-done((f32[256,128]{1,0:T(8,128)S(1)}, f32[256,128]{1,0:T(8,128)S(1)}, u32[]{:S(2)}, u32[]{:S(2)}) %collective-permute-start.4) | collective-permute-done | bytes 131104 | tf_op jit(solution)/shard_map/ppermute | solution.py:25
  49.2 0.0 collective-permute-done.5.refs_3_.refs_2_
  49.2 6.3 %merge_orth_1.1 = (f32[128,128]{1,0:T(8,128)S(1)}, f32[2,128,128]{2,1,0:T(8,128)S(1)}, f32[256,128]{1,0:T(8,128)S(1)}) custom-call(f32[256,128]{1,0:T(8,128)S(1)} %get-tuple-element.37.refs_0_, f32[256,128]{1,0:T(8,128)S(1)} %collective-permute-done.4.refs_1_, bf16[1,5,128,128]{3,2,1,0:T(8,128)(2,1)S(1)} %copy-done.3, ...), custom_call_target="tpu_custom_call" | custom-call | flops 8000000000 | bytes 24000000 | tf_op jit(solution)/shard_map/merge_orth_1/pallas_call | solution.py:344
  55.4 1.8 %collective-permute-start.6 = (f32[256,128]{1,0:T(8,128)S(1)}, f32[256,128]{1,0:T(8,128)S(1)}, u32[]{:S(2)}, u32[]{:S(2)}) collective-permute-start(f32[256,128]{1,0:T(8,128)S(1)} %get-tuple-element.39.refs_0_), channel_id=1, source_target_pairs={{0,4},{1,5},{2,6},{3,7},{4,0},{5,1},{6,2},{7,3},{8,12},{9,13},{10,... | collective-permute-start | bytes 393224 | tf_op jit(solution)/shard_map/ppermute | solution.py:25
  57.2 1.8 %lower_maps.1 = (f32[256,128]{1,0:T(8,128)S(1)}, f32[256,128]{1,0:T(8,128)S(1)}, f32[256,128]{1,0:T(8,128)S(1)}, f32[256,128]{1,0:T(8,128)S(1)}) custom-call(f32[512,512]{1,0:T(8,128)S(1)} %get-tuple-element.32.refs_0_, f32[512,512]{1,0:T(8,128)S(1)} %collective-permute-done.2.refs_1_, f32[256,512]{1,0:T(8,128)S(1)} %collective-permute-done.5.refs_3_.refs_2_, ...), custom_call_target="tpu_custom_call" | custom-call | flops 2000000000 | bytes 6000000 | tf_op jit(solution)/shard_map/lower_maps/pallas_call | solution.py:388
  59.0 0.7 collective-permute-start.10
  59.7 1.1 %collective-permute-start.8 = (f32[256,128]{1,0:T(8,128)S(1)}, f32[256,128]{1,0:T(8,128)S(1)}, u32[]{:S(2)}, u32[]{:S(2)}) collective-permute-start(f32[256,128]{1,0:T(8,128)S(1)} %get-tuple-element.46), channel_id=1, source_target_pairs={{0,1},{1,0},{2,3},{3,2},{4,5},{5,4},{6,7},{7,6},{8,9},{9,8},{10,11... | collective-permute-start | bytes 393224 | tf_op jit(solution)/shard_map/ppermute | solution.py:25
  60.7 0.5 collective-permute-start.9
  61.2 0.0 collective-permute-done.6.refs_1_
  61.2 6.1 %merge_orth_2.1 = (f32[128,128]{1,0:T(8,128)S(1)}, f32[2,128,128]{2,1,0:T(8,128)S(1)}, f32[256,128]{1,0:T(8,128)S(1)}) custom-call(f32[256,128]{1,0:T(8,128)S(1)} %get-tuple-element.39.refs_0_, f32[256,128]{1,0:T(8,128)S(1)} %collective-permute-done.6.refs_1_, bf16[1,5,128,128]{3,2,1,0:T(8,128)(2,1)S(1)} %copy-done.3, ...), custom_call_target="tpu_custom_call" | custom-call | flops 8000000000 | bytes 24000000 | tf_op jit(solution)/shard_map/merge_orth_2/pallas_call | solution.py:344
  67.3 1.6 %collective-permute-start.7 = (f32[256,128]{1,0:T(8,128)S(1)}, f32[256,128]{1,0:T(8,128)S(1)}, u32[]{:S(2)}, u32[]{:S(2)}) collective-permute-start(f32[256,128]{1,0:T(8,128)S(1)} %get-tuple-element.45.refs_0_), channel_id=1, source_target_pairs={{0,8},{1,9},{2,10},{3,11},{4,12},{5,13},{6,14},{7,15},{8,0},{9,1},... | collective-permute-start | bytes 393224 | tf_op jit(solution)/shard_map/ppermute | solution.py:25
  69.0 0.0 collective-permute-done.10.refs_3_
  69.0 0.0 collective-permute-done.8.refs_1_
  69.0 0.0 collective-permute-done.9.refs_2_
  69.0 0.3 upper_maps_2.1.refs_3_.refs_0_
  69.3 1.2 %collective-permute-start.12 = (f32[256,128]{1,0:T(8,128)S(1)}, f32[256,128]{1,0:T(8,128)S(1)}, u32[]{:S(2)}, u32[]{:S(2)}) collective-permute-start(f32[256,128]{1,0:T(8,128)S(1)} %upper_maps_2.1.refs_3_.refs_0_), channel_id=1, source_target_pairs={{0,4},{1,5},{2,6},{3,7},{4,0},{5,1},{6,2},{7,3},{8,12},{9,13},{10,... | collective-permute-start | bytes 393224 | tf_op jit(solution)/shard_map/ppermute | solution.py:25
  70.5 2.0 %collective-permute-done.7.refs_1_ = f32[256,128]{1,0:T(8,128)S(1)} collective-permute-done((f32[256,128]{1,0:T(8,128)S(1)}, f32[256,128]{1,0:T(8,128)S(1)}, u32[]{:S(2)}, u32[]{:S(2)}) %collective-permute-start.7) | collective-permute-done | bytes 131104 | tf_op jit(solution)/shard_map/ppermute | solution.py:25
  72.5 6.3 %merge_orth_3.1 = (f32[128,128]{1,0:T(8,128)S(1)}, f32[2,128,128]{2,1,0:T(8,128)S(1)}, f32[256,128]{1,0:T(8,128)S(1)}) custom-call(f32[256,128]{1,0:T(8,128)S(1)} %get-tuple-element.45.refs_0_, f32[256,128]{1,0:T(8,128)S(1)} %collective-permute-done.7.refs_1_, bf16[1,5,128,128]{3,2,1,0:T(8,128)(2,1)S(1)} %copy-done.3, f32[256,128]{1,0:T(8,128)S(1)} %upper_maps_2.1.refs_3_.refs_0_), custom_call_target="tpu_custom_call" | custom-call | flops 8000000000 | bytes 24000000 | tf_op jit(solution)/shard_map/merge_orth_3/pallas_call | solution.py:344
  78.8 0.0 collective-permute-done.12.refs_1_
  78.9 0.3 upper_maps_3.1
  79.2 1.6 %collective-permute-start.13 = (f32[256,128]{1,0:T(8,128)S(1)}, f32[256,128]{1,0:T(8,128)S(1)}, u32[]{:S(2)}, u32[]{:S(2)}) collective-permute-start(f32[256,128]{1,0:T(8,128)S(1)} %upper_maps_3.1), channel_id=1, source_target_pairs={{0,8},{1,9},{2,10},{3,11},{4,12},{5,13},{6,14},{7,15},{8,0},{9,1},... | collective-permute-start | bytes 393224 | tf_op jit(solution)/shard_map/ppermute | solution.py:25
  80.8 2.6 %collective-permute-start.11 = (f32[256,128]{1,0:T(8,128)S(1)}, f32[256,128]{1,0:T(8,128)S(1)}, u32[]{:S(2)}, u32[]{:S(2)}) collective-permute-start(f32[256,128]{1,0:T(8,128)S(1)} %get-tuple-element.51), channel_id=1, source_target_pairs={{0,16},{1,17},{2,18},{3,19},{4,20},{5,21},{6,22},{7,23},{8,24},{9,... | collective-permute-start | bytes 393224 | tf_op jit(solution)/shard_map/ppermute | solution.py:25
  83.4 2.5 %collective-permute-done.13 = f32[256,128]{1,0:T(8,128)S(1)} collective-permute-done((f32[256,128]{1,0:T(8,128)S(1)}, f32[256,128]{1,0:T(8,128)S(1)}, u32[]{:S(2)}, u32[]{:S(2)}) %collective-permute-start.13) | collective-permute-done | bytes 131104 | tf_op jit(solution)/shard_map/ppermute | solution.py:25
  85.9 1.7 %collective-permute-start.14 = (f32[256,128]{1,0:T(8,128)S(1)}, f32[256,128]{1,0:T(8,128)S(1)}, u32[]{:S(2)}, u32[]{:S(2)}) collective-permute-start(f32[256,128]{1,0:T(8,128)S(1)} %add.11.own_ref), channel_id=1, source_target_pairs={{0,16},{1,17},{2,18},{3,19},{4,20},{5,21},{6,22},{7,23},{8,24},{9,... | collective-permute-start | bytes 393224 | tf_op jit(solution)/shard_map/ppermute | solution.py:25
  87.6 3.5 %collective-permute-done.11 = f32[256,128]{1,0:T(8,128)S(1)} collective-permute-done((f32[256,128]{1,0:T(8,128)S(1)}, f32[256,128]{1,0:T(8,128)S(1)}, u32[]{:S(2)}, u32[]{:S(2)}) %collective-permute-start.11) | collective-permute-done | bytes 131104 | tf_op jit(solution)/shard_map/ppermute | solution.py:25
  91.1 5.9 %merge_orth_4.1 = (f32[5,128,128]{2,1,0:T(8,128)S(1)}, f32[128,256]{1,0:T(8,128)S(1)}, f32[8,128]{1,0:T(8,128)}) fusion(f32[5,128,128]{2,1,0:T(8,128)S(1)} %bitcast_dynamic-update-slice_fusion.1, f32[256,128]{1,0:T(8,128)S(1)} %get-tuple-element.51, f32[256,128]{1,0:T(8,128)S(1)} %collective-permute-done.11, bf16[1,5,128,128]{3,2,1,0:T(8,128)(2,1)S(1)} %copy-done.3, ...), kind=kCustom, calls=%fused_computation.2 | custom fusion | flops 8000000000 | bytes 757760 | tf_op jit(solution)/shard_map/merge_orth_4/pallas_call | solution.py:344
  97.0 0.0 copy-start.8
  97.0 0.0 collective-permute-done.14.other_ref
  97.0 0.6 top_sample.1.refs_0_
  97.6 0.0 copy-start
  97.6 0.1 collective-permute-start.15
  97.7 1.6 %collective-permute-start.16 = (f32[128,128]{1,0:T(8,128)S(1)}, f32[128,128]{1,0:T(8,128)S(1)}, u32[]{:S(2)}, u32[]{:S(2)}) collective-permute-start(f32[128,128]{1,0:T(8,128)S(1)} %top_sample.1.refs_0_), channel_id=1, source_target_pairs={{0,2},{1,3},{2,0},{3,1},{4,6},{5,7},{6,4},{7,5},{8,10},{9,11},{10,... | collective-permute-start | bytes 196616 | tf_op jit(solution)/shard_map/ppermute | solution.py:25
  99.3 0.3 collective-permute-start.17
  99.5 0.0 collective-permute-done.15.refs_1_
  99.5 2.6 %collective-permute-done.16.refs_2_ = f32[128,128]{1,0:T(8,128)S(1)} collective-permute-done((f32[128,128]{1,0:T(8,128)S(1)}, f32[128,128]{1,0:T(8,128)S(1)}, u32[]{:S(2)}, u32[]{:S(2)}) %collective-permute-start.16) | collective-permute-done | bytes 65568 | tf_op jit(solution)/shard_map/ppermute | solution.py:25
  102.2 1.1 %collective-permute-done.17.refs_3_ = f32[128,128]{1,0:T(8,128)S(1)} collective-permute-done((f32[128,128]{1,0:T(8,128)S(1)}, f32[128,128]{1,0:T(8,128)S(1)}, u32[]{:S(2)}, u32[]{:S(2)}) %collective-permute-start.17) | collective-permute-done | bytes 65568 | tf_op jit(solution)/shard_map/ppermute | solution.py:25
  103.3 0.0 copy-done
  103.3 0.0 copy-done.5
  103.3 0.0 copy-done.6
  103.3 0.0 copy-start.7
  103.3 0.6 copy-done.7
  103.9 1.7 %top_columns.1 = f32[1,128,512]{2,1,0:T(8,128)} custom-call(f32[128,128]{1,0:T(8,128)} %copy-done, f32[128,128]{1,0:T(8,128)} %copy-done.5, f32[128,128]{1,0:T(8,128)} %copy-done.6, f32[128,128]{1,0:T(8,128)} %copy-done.7), custom_call_target="tpu_custom_call" | custom-call | tf_op jit(solution)/shard_map/top_columns/pallas_call | solution.py:470
  105.6 0.0 copy-done.8
  (9 shorter events, 0.1 us)
Async XLA Ops:
  0.6 1.0 copy-start.1
  1.6 0.9 copy-start.2
  2.5 0.7 copy-start.4
  15.7 6.2 %collective-permute-start.2 = (f32[512,512]{1,0:T(8,128)S(1)}, f32[512,512]{1,0:T(8,128)S(1)}, u32[]{:S(2)}, u32[]{:S(2)}) collective-permute-start(f32[512,512]{1,0:T(8,128)S(1)} %get-tuple-element.33), channel_id=1, source_target_pairs={{0,1},{1,0},{2,3},{3,2},{4,5},{5,4},{6,7},{7,6},{8,9},{9,8},{10,11... | collective-permute-start | bytes 3145736 | tf_op jit(solution)/shard_map/ppermute | solution.py:25
  16.2 2.7 %collective-permute-start = (f32[512,128]{1,0:T(8,128)S(1)}, f32[512,128]{1,0:T(8,128)S(1)}, u32[]{:S(2)}, u32[]{:S(2)}) collective-permute-start(f32[512,128]{1,0:T(8,128)S(1)} %get-tuple-element.30), channel_id=1, source_target_pairs={{0,1},{1,0},{2,3},{3,2},{4,5},{5,4},{6,7},{7,6},{8,9},{9,8},{10,11... | collective-permute-start | bytes 786440 | tf_op jit(solution)/shard_map/ppermute | solution.py:25
  18.9 6.8 %collective-permute-start.1 = (f32[256,128]{1,0:T(8,128)S(1)}, f32[256,128]{1,0:T(8,128)S(1)}, u32[]{:S(2)}, u32[]{:S(2)}) collective-permute-start(f32[256,128]{1,0:T(8,128)S(1)} %slice_add_fusion.1), channel_id=1, source_target_pairs={{0,2},{1,3},{2,0},{3,1},{4,6},{5,7},{6,4},{7,5},{8,10},{9,11},{10,... | collective-permute-start | bytes 393224 | tf_op jit(solution)/shard_map/ppermute | solution.py:25
  25.6 8.1 %copy-start.3 = (bf16[1,5,128,128]{3,2,1,0:T(8,128)(2,1)S(1)}, bf16[1,5,128,128]{3,2,1,0:T(8,128)(2,1)}, u32[]{:S(2)}) copy-start(bf16[1,5,128,128]{3,2,1,0:T(8,128)(2,1)} %coupling_ref.1) | copy-start | bytes 491524
  32.0 1.7 %collective-permute-start.3 = (f32[256,128]{1,0:T(8,128)S(1)}, f32[256,128]{1,0:T(8,128)S(1)}, u32[]{:S(2)}, u32[]{:S(2)}) collective-permute-start(f32[256,128]{1,0:T(8,128)S(1)} %get-tuple-element.35.refs_0_), channel_id=1, source_target_pairs={{0,1},{1,0},{2,3},{3,2},{4,5},{5,4},{6,7},{7,6},{8,9},{9,8},{10,11... | collective-permute-start | bytes 393224 | tf_op jit(solution)/shard_map/ppermute | solution.py:25
  32.0 17.1 %collective-permute-start.5 = (f32[256,512]{1,0:T(8,128)S(1)}, f32[256,512]{1,0:T(8,128)S(1)}, u32[]{:S(2)}, u32[]{:S(2)}) collective-permute-start(f32[256,512]{1,0:T(8,128)S(1)} %slice_add_fusion._), channel_id=1, source_target_pairs={{0,2},{1,3},{2,0},{3,1},{4,6},{5,7},{6,4},{7,5},{8,10},{9,11},{10,... | collective-permute-start | bytes 1572872 | tf_op jit(solution)/shard_map/ppermute | solution.py:25
  39.9 9.3 %collective-permute-start.4 = (f32[256,128]{1,0:T(8,128)S(1)}, f32[256,128]{1,0:T(8,128)S(1)}, u32[]{:S(2)}, u32[]{:S(2)}) collective-permute-start(f32[256,128]{1,0:T(8,128)S(1)} %get-tuple-element.37.refs_0_), channel_id=1, source_target_pairs={{0,2},{1,3},{2,0},{3,1},{4,6},{5,7},{6,4},{7,5},{8,10},{9,11},{10,... | collective-permute-start | bytes 393224 | tf_op jit(solution)/shard_map/ppermute | solution.py:25
  55.4 5.8 %collective-permute-start.6 = (f32[256,128]{1,0:T(8,128)S(1)}, f32[256,128]{1,0:T(8,128)S(1)}, u32[]{:S(2)}, u32[]{:S(2)}) collective-permute-start(f32[256,128]{1,0:T(8,128)S(1)} %get-tuple-element.39.refs_0_), channel_id=1, source_target_pairs={{0,4},{1,5},{2,6},{3,7},{4,0},{5,1},{6,2},{7,3},{8,12},{9,13},{10,... | collective-permute-start | bytes 393224 | tf_op jit(solution)/shard_map/ppermute | solution.py:25
  59.0 10.0 %collective-permute-start.10 = (f32[256,128]{1,0:T(8,128)S(1)}, f32[256,128]{1,0:T(8,128)S(1)}, u32[]{:S(2)}, u32[]{:S(2)}) collective-permute-start(f32[256,128]{1,0:T(8,128)S(1)} %get-tuple-element.48), channel_id=1, source_target_pairs={{0,3},{1,2},{2,1},{3,0},{4,7},{5,6},{6,5},{7,4},{8,11},{9,10},{10,... | collective-permute-start | bytes 393224 | tf_op jit(solution)/shard_map/ppermute | solution.py:25
  59.7 9.3 %collective-permute-start.8 = (f32[256,128]{1,0:T(8,128)S(1)}, f32[256,128]{1,0:T(8,128)S(1)}, u32[]{:S(2)}, u32[]{:S(2)}) collective-permute-start(f32[256,128]{1,0:T(8,128)S(1)} %get-tuple-element.46), channel_id=1, source_target_pairs={{0,1},{1,0},{2,3},{3,2},{4,5},{5,4},{6,7},{7,6},{8,9},{9,8},{10,11... | collective-permute-start | bytes 393224 | tf_op jit(solution)/shard_map/ppermute | solution.py:25
  60.7 8.3 %collective-permute-start.9 = (f32[256,128]{1,0:T(8,128)S(1)}, f32[256,128]{1,0:T(8,128)S(1)}, u32[]{:S(2)}, u32[]{:S(2)}) collective-permute-start(f32[256,128]{1,0:T(8,128)S(1)} %get-tuple-element.47), channel_id=1, source_target_pairs={{0,2},{1,3},{2,0},{3,1},{4,6},{5,7},{6,4},{7,5},{8,10},{9,11},{10,... | collective-permute-start | bytes 393224 | tf_op jit(solution)/shard_map/ppermute | solution.py:25
  67.3 5.2 %collective-permute-start.7 = (f32[256,128]{1,0:T(8,128)S(1)}, f32[256,128]{1,0:T(8,128)S(1)}, u32[]{:S(2)}, u32[]{:S(2)}) collective-permute-start(f32[256,128]{1,0:T(8,128)S(1)} %get-tuple-element.45.refs_0_), channel_id=1, source_target_pairs={{0,8},{1,9},{2,10},{3,11},{4,12},{5,13},{6,14},{7,15},{8,0},{9,1},... | collective-permute-start | bytes 393224 | tf_op jit(solution)/shard_map/ppermute | solution.py:25
  69.3 9.5 %collective-permute-start.12 = (f32[256,128]{1,0:T(8,128)S(1)}, f32[256,128]{1,0:T(8,128)S(1)}, u32[]{:S(2)}, u32[]{:S(2)}) collective-permute-start(f32[256,128]{1,0:T(8,128)S(1)} %upper_maps_2.1.refs_3_.refs_0_), channel_id=1, source_target_pairs={{0,4},{1,5},{2,6},{3,7},{4,0},{5,1},{6,2},{7,3},{8,12},{9,13},{10,... | collective-permute-start | bytes 393224 | tf_op jit(solution)/shard_map/ppermute | solution.py:25
  79.2 6.7 %collective-permute-start.13 = (f32[256,128]{1,0:T(8,128)S(1)}, f32[256,128]{1,0:T(8,128)S(1)}, u32[]{:S(2)}, u32[]{:S(2)}) collective-permute-start(f32[256,128]{1,0:T(8,128)S(1)} %upper_maps_3.1), channel_id=1, source_target_pairs={{0,8},{1,9},{2,10},{3,11},{4,12},{5,13},{6,14},{7,15},{8,0},{9,1},... | collective-permute-start | bytes 393224 | tf_op jit(solution)/shard_map/ppermute | solution.py:25
  80.8 10.2 %collective-permute-start.11 = (f32[256,128]{1,0:T(8,128)S(1)}, f32[256,128]{1,0:T(8,128)S(1)}, u32[]{:S(2)}, u32[]{:S(2)}) collective-permute-start(f32[256,128]{1,0:T(8,128)S(1)} %get-tuple-element.51), channel_id=1, source_target_pairs={{0,16},{1,17},{2,18},{3,19},{4,20},{5,21},{6,22},{7,23},{8,24},{9,... | collective-permute-start | bytes 393224 | tf_op jit(solution)/shard_map/ppermute | solution.py:25
  85.9 11.1 %collective-permute-start.14 = (f32[256,128]{1,0:T(8,128)S(1)}, f32[256,128]{1,0:T(8,128)S(1)}, u32[]{:S(2)}, u32[]{:S(2)}) collective-permute-start(f32[256,128]{1,0:T(8,128)S(1)} %add.11.own_ref), channel_id=1, source_target_pairs={{0,16},{1,17},{2,18},{3,19},{4,20},{5,21},{6,22},{7,23},{8,24},{9,... | collective-permute-start | bytes 393224 | tf_op jit(solution)/shard_map/ppermute | solution.py:25
  97.0 8.7 %copy-start.8 = (f32[5,128,128]{2,1,0:T(8,128)}, f32[5,128,128]{2,1,0:T(8,128)S(1)}, u32[]{:S(2)}) copy-start(f32[5,128,128]{2,1,0:T(8,128)S(1)} %get-tuple-element.58) | copy-start | bytes 983044
  97.6 5.7 %copy-start = (f32[128,128]{1,0:T(8,128)}, f32[128,128]{1,0:T(8,128)S(1)}, u32[]{:S(2)}) copy-start(f32[128,128]{1,0:T(8,128)S(1)} %top_sample.1.refs_0_) | copy-start | bytes 196612
  97.6 1.9 %collective-permute-start.15 = (f32[128,128]{1,0:T(8,128)S(1)}, f32[128,128]{1,0:T(8,128)S(1)}, u32[]{:S(2)}, u32[]{:S(2)}) collective-permute-start(f32[128,128]{1,0:T(8,128)S(1)} %top_sample.1.refs_0_), channel_id=1, source_target_pairs={{0,1},{1,0},{2,3},{3,2},{4,5},{5,4},{6,7},{7,6},{8,9},{9,8},{10,11... | collective-permute-start | bytes 196616 | tf_op jit(solution)/shard_map/ppermute | solution.py:25
  97.7 4.5 %collective-permute-start.16 = (f32[128,128]{1,0:T(8,128)S(1)}, f32[128,128]{1,0:T(8,128)S(1)}, u32[]{:S(2)}, u32[]{:S(2)}) collective-permute-start(f32[128,128]{1,0:T(8,128)S(1)} %top_sample.1.refs_0_), channel_id=1, source_target_pairs={{0,2},{1,3},{2,0},{3,1},{4,6},{5,7},{6,4},{7,5},{8,10},{9,11},{10,... | collective-permute-start | bytes 196616 | tf_op jit(solution)/shard_map/ppermute | solution.py:25
  99.3 4.0 %collective-permute-start.17 = (f32[128,128]{1,0:T(8,128)S(1)}, f32[128,128]{1,0:T(8,128)S(1)}, u32[]{:S(2)}, u32[]{:S(2)}) collective-permute-start(f32[128,128]{1,0:T(8,128)S(1)} %top_sample.1.refs_0_), channel_id=1, source_target_pairs={{0,3},{1,2},{2,1},{3,0},{4,7},{5,6},{6,5},{7,4},{8,11},{9,10},{10,... | collective-permute-start | bytes 196616 | tf_op jit(solution)/shard_map/ppermute | solution.py:25
  99.5 3.8 %copy-start.5 = (f32[128,128]{1,0:T(8,128)}, f32[128,128]{1,0:T(8,128)S(1)}, u32[]{:S(2)}) copy-start(f32[128,128]{1,0:T(8,128)S(1)} %collective-permute-done.15.refs_1_) | copy-start | bytes 196612
  102.2 1.1 %copy-start.6 = (f32[128,128]{1,0:T(8,128)}, f32[128,128]{1,0:T(8,128)S(1)}, u32[]{:S(2)}) copy-start(f32[128,128]{1,0:T(8,128)S(1)} %collective-permute-done.16.refs_2_) | copy-start | bytes 196612
  103.3 0.6 copy-start.7

commit v2 on v1

--- a/solution.py
+++ b/solution.py
@@ -119,53 +119,41 @@
     slots_ref,
     tiles_ref,
     sketch_ref,
-    sub_ref,
-    leaf_sketch_ref,
     keep_ref,
     send_ref,
-    keep_red_ref,
-    send_red_ref,
-    sketch_red_ref,
     dense,
     held,
     slots,
-    sub,
-    leaf_sketch,
     tile_sem,
     sketch_sems,
-    small_sems,
+    slots_sem,
+    *,
+    leaves,
 ):
     tile_count, tile_size, _ = tiles_ref.shape
     depth = sketch_ref.shape[0]
     rows = dense.shape[0]
     half = rows // 2
-    rank = sub.shape[1]
     col_tiles = depth // tile_size
     chunks = sketch_sems.shape[0]
     chunk = depth // chunks
-    leaf_tiles = leaf_sketch_ref.shape[0] // tile_size
-    leaves = rows // leaf_sketch_ref.shape[0]
+    leaf_tiles = rows // leaves // tile_size
     me = lax.axis_index("col")
-    small = [
-        pltpu.make_async_copy(source, target, small_sems.at[k])
-        for k, (source, target) in enumerate(
-            ((slots_ref, slots), (sub_ref, sub), (leaf_sketch_ref, leaf_sketch))
-        )
-    ]
+    slots_load = pltpu.make_async_copy(slots_ref, slots, slots_sem)
     loads = [
         pltpu.make_async_copy(
             sketch_ref.at[pl.ds(k * chunk, chunk)], held.at[pl.ds(k * chunk, chunk)], sketch_sems.at[k]
         )
         for k in range(chunks)
     ]
-    for load in small + loads:
+    for load in [slots_load] + loads:
         load.start()
 
     @pl.loop(0, rows // 64)
     def _(i):
         dense[pl.ds(pl.multiple_of(i * 64, 64), 64), :] = jnp.zeros((64, depth), dense.dtype)
 
-    small[0].wait()
+    slots_load.wait()
     together = math.gcd(tile_count, 8)
 
     @pl.loop(0, tile_count // together)
@@ -184,14 +172,6 @@
                 tiles_ref.at[t], dense.at[pl.ds(row, tile_size), pl.ds(col, tile_size)], tile_sem
             ).start()
 
-    small[1].wait()
-    small[2].wait()
-    high, middle, low = in_parts(sub[...])
-    two = jnp.concatenate([high, middle], axis=1)
-    sketch_two = short_dot(leaf_sketch[...], two)
-    sketch_red_ref[...] = sketch_two[:, :rank] + (
-        sketch_two[:, rank:] + short_dot(leaf_sketch[...], low)
-    )
     pltpu.make_async_copy(tiles_ref, tiles_ref, tile_sem).wait()
     for k in range(chunks):
         loads[k].wait()
@@ -205,42 +185,27 @@
                 ref[...] = part
             else:
                 ref[...] += part
-    for ref, red_ref in ((send_ref, send_red_ref), (keep_ref, keep_red_ref)):
-        first, second, third = in_parts(ref[...])
-        wide = short_dot(second, two) + short_dot(first, two)
-        rest = short_dot(third, high) + short_dot(first, low)
-        red_ref[...] = wide[:, :rank] + (wide[:, rank:] + rest)
-
-
-def sample_rows(tiles, tile_slots, sketch, subsketch, row_sketch):
+
+
+def sample_rows(tiles, tile_slots, sketch, leaf):
     tile_size = tiles.shape[1]
     depth, width = sketch.shape
-    rank = subsketch.shape[1]
-    leaf = row_sketch.shape[0]
-    rows = leaf * lax.axis_size("col")
+    leaves = lax.axis_size("col")
+    rows = leaf * leaves
     half = rows // 2
     chunks = math.gcd(depth // tile_size, 4)
-    f32 = jnp.float32
-    return pl.pallas_call(
-        spmm_body,
-        out_shape=[
-            jax.ShapeDtypeStruct((half, width), f32),
-            jax.ShapeDtypeStruct((half, width), f32),
-            jax.ShapeDtypeStruct((half, rank), f32),
-            jax.ShapeDtypeStruct((half, rank), f32),
-            jax.ShapeDtypeStruct((leaf, rank), f32),
-        ],
-        in_specs=[HBM] * 5,
-        out_specs=[VMEM] * 5,
+    return pl.pallas_call(
+        functools.partial(spmm_body, leaves=leaves),
+        out_shape=[jax.ShapeDtypeStruct((half, width), jnp.float32)] * 2,
+        in_specs=[HBM] * 3,
+        out_specs=[VMEM] * 2,
         scratch_shapes=[
             pltpu.VMEM((rows, depth), jnp.bfloat16),
             pltpu.VMEM((depth, width), jnp.bfloat16),
             pltpu.SMEM(tile_slots.shape, jnp.int32),
-            pltpu.VMEM(subsketch.shape, f32),
-            pltpu.VMEM(row_sketch.shape, jnp.bfloat16),
             pltpu.SemaphoreType.DMA,
             pltpu.SemaphoreType.DMA((chunks,)),
-            pltpu.SemaphoreType.DMA((3,)),
+            pltpu.SemaphoreType.DMA,
         ],
         compiler_params=pltpu.CompilerParams(vmem_limit_bytes=48 * 2**20),
         cost_estimate=pl.CostEstimate(
@@ -249,7 +214,36 @@
             transcendentals=0,
         ),
         name="spmm",
-    )(tile_slots, tiles, sketch, subsketch, row_sketch)
+    )(tile_slots, tiles, sketch)
+
+
+def reduce_body(*refs):
+    sub_ref, ref = refs[:2]
+    outs = refs[len(refs) // 2 + 1 :]
+    rank = sub_ref.shape[1]
+    high, middle, low = in_parts(sub_ref[...])
+    two = jnp.concatenate([high, middle], axis=1)
+    first, second, third = in_parts(ref[...])
+    wide = short_dot(second, two) + short_dot(first, two)
+    rest = short_dot(third, high) + short_dot(first, low)
+    outs[0][...] = wide[:, :rank] + (wide[:, rank:] + rest)
+    if len(outs) > 1:
+        exact = refs[2][...]
+        wide = short_dot(exact, two)
+        outs[1][...] = wide[:, :rank] + (wide[:, rank:] + short_dot(exact, low))
+
+
+def reduce_step(subsketch, *blocks):
+    rank = subsketch.shape[1]
+    return pl.pallas_call(
+        reduce_body,
+        out_shape=[jax.ShapeDtypeStruct((block.shape[0], rank), jnp.float32) for block in blocks],
+        in_specs=[VMEM] * (1 + len(blocks)),
+        out_specs=[VMEM] * len(blocks),
+        compiler_params=small_params(),
+        cost_estimate=small_cost(1),
+        name="reduced_" + str(len(blocks)),
+    )(subsketch, *blocks)
 
 
 def leaf_body(keep_ref, first_ref, second_ref, sketch_red_ref, _, basis_ref, basis_t_ref, pair_ref):
@@ -270,7 +264,7 @@
 
 
 def small_cost(micros):
-    return pl.CostEstimate(flops=micros * 10**9, bytes_accessed=micros * 3 * 10**6, transcendentals=0)
+    return pl.CostEstimate(flops=micros * 10**7, bytes_accessed=micros * 3 * 10**4, transcendentals=0)
 
 
 def leaf_step(keep, first, second, sketch_red, after):
@@ -481,18 +475,22 @@
     ways = lax.axis_size("col")
     col_bits = ways.bit_length() - 1
     leaf = row_sketch.shape[0]
-    keep, send, keep_red, send_red, sketch_red = sample_rows(
-        tiles, tile_slots, sketch, subsketch, row_sketch
-    )
+    keep, send = sample_rows(tiles, tile_slots, sketch, leaf)
+    (send_red,) = reduce_step(subsketch, send)
     first_red = from_partner(send_red, "col", 1)
+    keep_red, sketch_red = reduce_step(subsketch, keep, row_sketch)
+    passed_red, send = lax.optimization_barrier((keep_red[leaf:] + first_red[leaf:], send))
+    second_red = from_partner(passed_red, "col", 2)
     first = from_partner(send, "col", 1)
-    second_red = from_partner(keep_red[leaf:] + first_red[leaf:], "col", 2)
-    passed = keep[leaf:] + first[leaf:]
+    passed, second_red = lax.optimization_barrier((keep[leaf:] + first[leaf:], second_red))
     second = from_partner(passed, "col", 2)
     leaf_basis, basis_t, pair = leaf_step(keep_red, first_red, second_red, sketch_red, passed)
     blocks, low_maps, after, parts = [], [], [], []
     for tree_level in range(LEVELS):
-        other = from_partner(pair, ROW_COL, 2**tree_level)
+        if tree_level < LEVELS - 1:
+            other = from_partner(pair, ROW_COL, 2**tree_level)
+        else:
+            other = waiting
         if tree_level == col_bits - 1:
             after = [second]
         block, maps, pair = merge_step(tree_level, pair, other, couplings, after)
@@ -510,7 +508,8 @@
             parts = [cut[0]] + [from_partner(cut[away], "col", away) for away in range(1, ways)]
             after = [cut[0]]
         if tree_level == LEVELS - 2:
-            whole = parts[0] + parts[1]
+            waiting = from_partner(pair, ROW_COL, 2 ** (LEVELS - 1))
+            whole, waiting = lax.optimization_barrier((parts[0] + parts[1], waiting))
             far = from_partner(whole, ROW_COL, 2 ** (LEVELS - 1))
             after = [whole]
     top = top_step(whole, far, couplings, pair)

time: 106 us -> 98.8 us (0.932)
  waiting for transfers between devices: 26 us -> 22 us
  starting transfers between devices: 21.3 us -> 19.3 us
  local copies, waits for them, and re-layouts: 3.23 us -> 1.51 us
    ppermute x18, waiting for transfers between devices: 26 us -> 22 us  [from_partner(): return lax.ppermute(block, axis, route)]
    ppermute x18, starting transfers between devices: 21.3 us -> 19.3 us  [from_partner(): return lax.ppermute(block, axis, route)]
    unnamed x22, local copies, waits for them, and re-layouts: 3.23 us -> 1.51 us
    pallas_call x1 -> x3, Pallas kernels: 12.4 us -> 12.8 us  [the longest x1 11.2 us: sample_rows(): pl.pallas_call(functools.partial(spmm_body, leaves=leaves), out_shape=[ja...]
  transfers between devices with their start and end apart: 18 -> 18, of which waited for: 8 -> 10; matrix products, arithmetic and copies ran while one was open for 6% -> 6% of each run, Pallas kernels for 20% -> 28%
where the time goes in v2:
time: 98.8 us; the launch traced here: 98.6 us
  Pallas kernels  48.7 us (49%)
  waiting for transfers between devices  22 us (22%)
  starting transfers between devices  19.3 us (20%)
  other arithmetic  6 us (6%)
  local copies, waits for them, and re-layouts  1.51 us (2%)
  between operations  1.02 us (1%)
    pallas_call x4, Pallas kernels, merge_step(): pl.pallas_call(functools.partial(merge_body, tree_level), grid=(1,), out_...  24.8 us
    ppermute x18, waiting for transfers between devices, from_partner(): return lax.ppermute(block, axis, route)  22 us
    ppermute x18, starting transfers between devices, from_partner(): return lax.ppermute(block, axis, route)  19.3 us
    pallas_call x1, Pallas kernels, sample_rows(): pl.pallas_call(functools.partial(spmm_body, leaves=leaves), out_shape=[ja...  11.2 us
    pallas_call x1, Pallas kernels, leaf_step(): pl.pallas_call(leaf_body, grid=(1,), out_shape=[jax.ShapeDtypeStruct((lea...  6.39 us
    pallas_call x1, other arithmetic, merge_step(): pl.pallas_call(functools.partial(merge_body, tree_level), grid=(1,), out_...  5.89 us
  transfers between devices with their start and end apart: 18, of which 10 were waited for; matrix products, arithmetic and copies ran while one was open for 6% of the time, Pallas kernels for 28%

profile of v2, /device:TPU:0, one launch (start us, length us, event | category | flops | bytes accessed | tf_op | source)
XLA Modules:
  0.0 98.6 jit_solution(4144791286783096205)
XLA Ops:
  0.6 0.0 copy-start.2
  0.6 0.0 copy-start.1
  0.7 0.0 copy-start.4
  0.7 0.7 copy-done.4
  1.4 11.2 %spmm.1 = (f32[512,512]{1,0:T(8,128)S(1)}, f32[512,512]{1,0:T(8,128)S(1)}) custom-call(s32[168]{0:T(256)S(1)} %copy-done.4, bf16[168,128,128]{2,1,0:T(8,128)(2,1)} %tiles_ref.1, bf16[6144,512]{1,0:T(8,128)(2,1)} %sketch_ref.1), custom_call_target="tpu_custom_call" | custom-call | flops 6442450944 | bytes 13893632 | tf_op jit(solution)/shard_map/spmm/pallas_call | solution.py:197
  12.6 0.0 copy-start
  12.6 0.0 copy-done.2
  12.6 0.7 reduced_1.1
  13.3 0.5 collective-permute-start
  13.9 0.0 copy-done.1
  13.9 0.9 reduced_2.1
  14.7 0.3 collective-permute-done.first_ref
  15.0 0.4 collective-permute-start.1
  15.5 2.7 %collective-permute-start.2 = (f32[256,128]{1,0:T(8,128)S(1)}, f32[256,128]{1,0:T(8,128)S(1)}, u32[]{:S(2)}, u32[]{:S(2)}) collective-permute-start(f32[256,128]{1,0:T(8,128)S(1)} %slice_add_fusion.1), channel_id=1, source_target_pairs={{0,2},{1,3},{2,0},{3,1},{4,6},{5,7},{6,4},{7,5},{8,10},{9,11},{10,... | collective-permute-start | bytes 393224 | tf_op jit(solution)/shard_map/ppermute | solution.py:25
  18.1 0.0 collective-permute-done.1.refs_1_
  18.1 0.1 slice_add_fusion._
  18.2 3.9 %collective-permute-done.2.second_ref = f32[256,128]{1,0:T(8,128)S(1)} collective-permute-done((f32[256,128]{1,0:T(8,128)S(1)}, f32[256,128]{1,0:T(8,128)S(1)}, u32[]{:S(2)}, u32[]{:S(2)}) %collective-permute-start.2) | collective-permute-done | bytes 131104 | tf_op jit(solution)/shard_map/ppermute | solution.py:25
  22.2 1.7 %collective-permute-start.5 = (f32[256,512]{1,0:T(8,128)S(1)}, f32[256,512]{1,0:T(8,128)S(1)}, u32[]{:S(2)}, u32[]{:S(2)}) collective-permute-start(f32[256,512]{1,0:T(8,128)S(1)} %slice_add_fusion._), channel_id=1, source_target_pairs={{0,2},{1,3},{2,0},{3,1},{4,6},{5,7},{6,4},{7,5},{8,10},{9,11},{10,... | collective-permute-start | bytes 1572872 | tf_op jit(solution)/shard_map/ppermute | solution.py:25
  23.9 6.4 %leaf_orth.1 = (f32[256,128]{1,0:T(8,128)}, f32[128,256]{1,0:T(8,128)S(1)}, f32[256,128]{1,0:T(8,128)S(1)}) custom-call(f32[512,128]{1,0:T(8,128)S(1)} %get-tuple-element.35.keep_ref, f32[512,128]{1,0:T(8,128)S(1)} %collective-permute-done.first_ref, f32[256,128]{1,0:T(8,128)S(1)} %collective-permute-done.2.second_ref, ...), custom_call_target="tpu_custom_call" | custom-call | flops 80000000 | bytes 240000 | tf_op jit(solution)/shard_map/leaf_orth/pallas_call | solution.py:274
  30.3 0.0 collective-permute-start.3
  30.3 1.3 %collective-permute-done.3.refs_1_ = f32[256,128]{1,0:T(8,128)S(1)} collective-permute-done((f32[256,128]{1,0:T(8,128)S(1)}, f32[256,128]{1,0:T(8,128)S(1)}, u32[]{:S(2)}, u32[]{:S(2)}) %collective-permute-start.3) | collective-permute-done | bytes 131104 | tf_op jit(solution)/shard_map/ppermute | solution.py:25
  31.6 0.0 copy-done
  31.6 6.3 %merge_orth_0.1 = (f32[128,128]{1,0:T(8,128)S(1)}, f32[2,128,128]{2,1,0:T(8,128)S(1)}, f32[256,128]{1,0:T(8,128)S(1)}) custom-call(f32[256,128]{1,0:T(8,128)S(1)} %get-tuple-element.43.refs_0_, f32[256,128]{1,0:T(8,128)S(1)} %collective-permute-done.3.refs_1_, bf16[1,5,128,128]{3,2,1,0:T(8,128)(2,1)S(1)} %copy-done), custom_call_target="tpu_custom_call" | custom-call | flops 80000000 | bytes 240000 | tf_op jit(solution)/shard_map/merge_orth_0/pallas_call | solution.py:338
  37.9 0.3 collective-permute-start.4
  38.3 5.3 %collective-permute-done.4.refs_1_ = f32[256,128]{1,0:T(8,128)S(1)} collective-permute-done((f32[256,128]{1,0:T(8,128)S(1)}, f32[256,128]{1,0:T(8,128)S(1)}, u32[]{:S(2)}, u32[]{:S(2)}) %collective-permute-start.4) | collective-permute-done | bytes 131104 | tf_op jit(solution)/shard_map/ppermute | solution.py:25
  43.5 0.0 collective-permute-done.5.refs_3_.refs_2_
  43.5 6.1 %merge_orth_1.1 = (f32[128,128]{1,0:T(8,128)S(1)}, f32[2,128,128]{2,1,0:T(8,128)S(1)}, f32[256,128]{1,0:T(8,128)S(1)}) custom-call(f32[256,128]{1,0:T(8,128)S(1)} %get-tuple-element.45.refs_0_, f32[256,128]{1,0:T(8,128)S(1)} %collective-permute-done.4.refs_1_, bf16[1,5,128,128]{3,2,1,0:T(8,128)(2,1)S(1)} %copy-done, ...), custom_call_target="tpu_custom_call" | custom-call | flops 80000000 | bytes 240000 | tf_op jit(solution)/shard_map/merge_orth_1/pallas_call | solution.py:338
  49.7 1.6 %collective-permute-start.6 = (f32[256,128]{1,0:T(8,128)S(1)}, f32[256,128]{1,0:T(8,128)S(1)}, u32[]{:S(2)}, u32[]{:S(2)}) collective-permute-start(f32[256,128]{1,0:T(8,128)S(1)} %get-tuple-element.47.refs_0_), channel_id=1, source_target_pairs={{0,4},{1,5},{2,6},{3,7},{4,0},{5,1},{6,2},{7,3},{8,12},{9,13},{10,... | collective-permute-start | bytes 393224 | tf_op jit(solution)/shard_map/ppermute | solution.py:25
  51.2 1.8 %lower_maps.1 = (f32[256,128]{1,0:T(8,128)S(1)}, f32[256,128]{1,0:T(8,128)S(1)}, f32[256,128]{1,0:T(8,128)S(1)}, f32[256,128]{1,0:T(8,128)S(1)}) custom-call(f32[512,512]{1,0:T(8,128)S(1)} %get-tuple-element.34.refs_1_.refs_0_, f32[512,512]{1,0:T(8,128)S(1)} %collective-permute-done.1.refs_1_, f32[256,512]{1,0:T(8,128)S(1)} %collective-permute-done.5.refs_3_.refs_2_, ...), custom_call_target="tpu_custom_call" | custom-call | flops 20000000 | bytes 60000 | tf_op jit(solution)/shard_map/lower_maps/pallas_call | solution.py:382
  53.0 0.1 collective-permute-start.10
  53.1 0.6 collective-permute-start.8
  53.7 1.5 %collective-permute-start.9 = (f32[256,128]{1,0:T(8,128)S(1)}, f32[256,128]{1,0:T(8,128)S(1)}, u32[]{:S(2)}, u32[]{:S(2)}) collective-permute-start(f32[256,128]{1,0:T(8,128)S(1)} %get-tuple-element.55), channel_id=1, source_target_pairs={{0,2},{1,3},{2,0},{3,1},{4,6},{5,7},{6,4},{7,5},{8,10},{9,11},{10,... | collective-permute-start | bytes 393224 | tf_op jit(solution)/shard_map/ppermute | solution.py:25
  55.2 0.0 collective-permute-done.6.refs_1_
  55.2 6.1 %merge_orth_2.1 = (f32[128,128]{1,0:T(8,128)S(1)}, f32[2,128,128]{2,1,0:T(8,128)S(1)}, f32[256,128]{1,0:T(8,128)S(1)}) custom-call(f32[256,128]{1,0:T(8,128)S(1)} %get-tuple-element.47.refs_0_, f32[256,128]{1,0:T(8,128)S(1)} %collective-permute-done.6.refs_1_, bf16[1,5,128,128]{3,2,1,0:T(8,128)(2,1)S(1)} %copy-done, ...), custom_call_target="tpu_custom_call" | custom-call | flops 80000000 | bytes 240000 | tf_op jit(solution)/shard_map/merge_orth_2/pallas_call | solution.py:338
  61.4 1.6 %collective-permute-start.7 = (f32[256,128]{1,0:T(8,128)S(1)}, f32[256,128]{1,0:T(8,128)S(1)}, u32[]{:S(2)}, u32[]{:S(2)}) collective-permute-start(f32[256,128]{1,0:T(8,128)S(1)} %get-tuple-element.53.refs_0_), channel_id=1, source_target_pairs={{0,8},{1,9},{2,10},{3,11},{4,12},{5,13},{6,14},{7,15},{8,0},{9,1},... | collective-permute-start | bytes 393224 | tf_op jit(solution)/shard_map/ppermute | solution.py:25
  63.0 0.0 collective-permute-done.10.refs_3_
  63.0 0.0 collective-permute-done.8.refs_1_
  63.0 0.0 collective-permute-done.9.refs_2_
  63.0 0.3 upper_maps_2.1.refs_3_.refs_0_
  63.3 1.0 %collective-permute-start.11 = (f32[256,128]{1,0:T(8,128)S(1)}, f32[256,128]{1,0:T(8,128)S(1)}, u32[]{:S(2)}, u32[]{:S(2)}) collective-permute-start(f32[256,128]{1,0:T(8,128)S(1)} %upper_maps_2.1.refs_3_.refs_0_), channel_id=1, source_target_pairs={{0,4},{1,5},{2,6},{3,7},{4,0},{5,1},{6,2},{7,3},{8,12},{9,13},{10,... | collective-permute-start | bytes 393224 | tf_op jit(solution)/shard_map/ppermute | solution.py:25
  64.3 2.2 %collective-permute-done.7.refs_1_ = f32[256,128]{1,0:T(8,128)S(1)} collective-permute-done((f32[256,128]{1,0:T(8,128)S(1)}, f32[256,128]{1,0:T(8,128)S(1)}, u32[]{:S(2)}, u32[]{:S(2)}) %collective-permute-start.7) | collective-permute-done | bytes 131104 | tf_op jit(solution)/shard_map/ppermute | solution.py:25
  66.6 6.3 %merge_orth_3.1 = (f32[128,128]{1,0:T(8,128)S(1)}, f32[2,128,128]{2,1,0:T(8,128)S(1)}, f32[256,128]{1,0:T(8,128)S(1)}) custom-call(f32[256,128]{1,0:T(8,128)S(1)} %get-tuple-element.53.refs_0_, f32[256,128]{1,0:T(8,128)S(1)} %collective-permute-done.7.refs_1_, bf16[1,5,128,128]{3,2,1,0:T(8,128)(2,1)S(1)} %copy-done, f32[256,128]{1,0:T(8,128)S(1)} %upper_maps_2.1.refs_3_.refs_0_), custom_call_target="tpu_custom_call" | custom-call | flops 80000000 | bytes 240000 | tf_op jit(solution)/shard_map/merge_orth_3/pallas_call | solution.py:338
  72.9 0.0 collective-permute-done.11.refs_1_
  72.9 0.3 upper_maps_3.1
  73.2 1.6 %collective-permute-start.12 = (f32[256,128]{1,0:T(8,128)S(1)}, f32[256,128]{1,0:T(8,128)S(1)}, u32[]{:S(2)}, u32[]{:S(2)}) collective-permute-start(f32[256,128]{1,0:T(8,128)S(1)} %upper_maps_3.1), channel_id=1, source_target_pairs={{0,8},{1,9},{2,10},{3,11},{4,12},{5,13},{6,14},{7,15},{8,0},{9,1},... | collective-permute-start | bytes 393224 | tf_op jit(solution)/shard_map/ppermute | solution.py:25
  74.8 2.6 %collective-permute-start.13 = (f32[256,128]{1,0:T(8,128)S(1)}, f32[256,128]{1,0:T(8,128)S(1)}, u32[]{:S(2)}, u32[]{:S(2)}) collective-permute-start(f32[256,128]{1,0:T(8,128)S(1)} %get-tuple-element.59), channel_id=1, source_target_pairs={{0,16},{1,17},{2,18},{3,19},{4,20},{5,21},{6,22},{7,23},{8,24},{9,... | collective-permute-start | bytes 393224 | tf_op jit(solution)/shard_map/ppermute | solution.py:25
  77.4 2.5 %collective-permute-done.12 = f32[256,128]{1,0:T(8,128)S(1)} collective-permute-done((f32[256,128]{1,0:T(8,128)S(1)}, f32[256,128]{1,0:T(8,128)S(1)}, u32[]{:S(2)}, u32[]{:S(2)}) %collective-permute-start.12) | collective-permute-done | bytes 131104 | tf_op jit(solution)/shard_map/ppermute | solution.py:25
  79.9 2.6 %collective-permute-done.13 = f32[256,128]{1,0:T(8,128)S(1)} collective-permute-done((f32[256,128]{1,0:T(8,128)S(1)}, f32[256,128]{1,0:T(8,128)S(1)}, u32[]{:S(2)}, u32[]{:S(2)}) %collective-permute-start.13) | collective-permute-done | bytes 131104 | tf_op jit(solution)/shard_map/ppermute | solution.py:25
  82.6 1.1 %collective-permute-start.14 = (f32[256,128]{1,0:T(8,128)S(1)}, f32[256,128]{1,0:T(8,128)S(1)}, u32[]{:S(2)}, u32[]{:S(2)}) collective-permute-start(f32[256,128]{1,0:T(8,128)S(1)} %add.11.own_ref), channel_id=1, source_target_pairs={{0,16},{1,17},{2,18},{3,19},{4,20},{5,21},{6,22},{7,23},{8,24},{9,... | collective-permute-start | bytes 393224 | tf_op jit(solution)/shard_map/ppermute | solution.py:25
  83.6 5.9 %merge_orth_4.1 = (f32[5,128,128]{2,1,0:T(8,128)S(1)}, f32[128,256]{1,0:T(8,128)S(1)}, f32[8,128]{1,0:T(8,128)}) fusion(f32[5,128,128]{2,1,0:T(8,128)S(1)} %bitcast_dynamic-update-slice_fusion.1, f32[256,128]{1,0:T(8,128)S(1)} %get-tuple-element.59, f32[256,128]{1,0:T(8,128)S(1)} %collective-permute-done.13, bf16[1,5,128,128]{3,2,1,0:T(8,128)(2,1)S(1)} %copy-done, ...), kind=kCustom, calls=%fused_computation.2 | custom fusion | flops 80000000 | bytes 757760 | tf_op jit(solution)/shard_map/merge_orth_4/pallas_call | solution.py:338
  89.5 0.0 copy-start.8
  89.5 0.3 collective-permute-done.14.other_ref
  89.8 0.6 top_sample.1.refs_0_
  90.4 0.0 copy-start.3
  90.4 0.1 collective-permute-start.15
  90.5 0.6 collective-permute-start.16
  91.1 1.3 %collective-permute-start.17 = (f32[128,128]{1,0:T(8,128)S(1)}, f32[128,128]{1,0:T(8,128)S(1)}, u32[]{:S(2)}, u32[]{:S(2)}) collective-permute-start(f32[128,128]{1,0:T(8,128)S(1)} %top_sample.1.refs_0_), channel_id=1, source_target_pairs={{0,3},{1,2},{2,1},{3,0},{4,7},{5,6},{6,5},{7,4},{8,11},{9,10},{10,... | collective-permute-start | bytes 196616 | tf_op jit(solution)/shard_map/ppermute | solution.py:25
  92.4 0.0 collective-permute-done.15.refs_1_
  92.4 3.1 %collective-permute-done.16.refs_2_ = f32[128,128]{1,0:T(8,128)S(1)} collective-permute-done((f32[128,128]{1,0:T(8,128)S(1)}, f32[128,128]{1,0:T(8,128)S(1)}, u32[]{:S(2)}, u32[]{:S(2)}) %collective-permute-start.16) | collective-permute-done | bytes 65568 | tf_op jit(solution)/shard_map/ppermute | solution.py:25
  95.5 0.5 collective-permute-done.17.refs_3_
  96.0 0.0 copy-done.3
  96.0 0.1 copy-done.6
  96.1 0.6 copy-done.7
  96.7 1.7 %top_columns.1 = f32[1,128,512]{2,1,0:T(8,128)} custom-call(f32[128,128]{1,0:T(8,128)} %copy-done.3, f32[128,128]{1,0:T(8,128)} %copy-done.5, f32[128,128]{1,0:T(8,128)} %copy-done.6, f32[128,128]{1,0:T(8,128)} %copy-done.7), custom_call_target="tpu_custom_call" | custom-call | tf_op jit(solution)/shard_map/top_columns/pallas_call | solution.py:464
  (11 shorter events, 0.1 us)
Async XLA Ops:
  0.6 12.0 %copy-start.2 = (f32[512,128]{1,0:T(8,128)S(1)}, f32[512,128]{1,0:T(8,128)}, u32[]{:S(2)}) copy-start(f32[512,128]{1,0:T(8,128)} %refs_0_.3) | copy-start | bytes 786436
  0.6 13.2 %copy-start.1 = (bf16[256,512]{1,0:T(8,128)(2,1)S(1)}, bf16[256,512]{1,0:T(8,128)(2,1)}, u32[]{:S(2)}) copy-start(bf16[256,512]{1,0:T(8,128)(2,1)} %refs_3_.1) | copy-start | bytes 786436
  0.7 0.7 copy-start.4
  12.6 19.1 %copy-start = (bf16[1,5,128,128]{3,2,1,0:T(8,128)(2,1)S(1)}, bf16[1,5,128,128]{3,2,1,0:T(8,128)(2,1)}, u32[]{:S(2)}) copy-start(bf16[1,5,128,128]{3,2,1,0:T(8,128)(2,1)} %coupling_ref.1) | copy-start | bytes 491524
  13.3 1.7 %collective-permute-start = (f32[512,128]{1,0:T(8,128)S(1)}, f32[512,128]{1,0:T(8,128)S(1)}, u32[]{:S(2)}, u32[]{:S(2)}) collective-permute-start(f32[512,128]{1,0:T(8,128)S(1)} %reduced_1.1), channel_id=1, source_target_pairs={{0,1},{1,0},{2,3},{3,2},{4,5},{5,4},{6,7},{7,6},{8,9},{9,8},{10,11... | collective-permute-start | bytes 786440 | tf_op jit(solution)/shard_map/ppermute | solution.py:25
  15.0 3.1 %collective-permute-start.1 = (f32[512,512]{1,0:T(8,128)S(1)}, f32[512,512]{1,0:T(8,128)S(1)}, u32[]{:S(2)}, u32[]{:S(2)}) collective-permute-start(f32[512,512]{1,0:T(8,128)S(1)} %get-tuple-element.37.refs_1_), channel_id=1, source_target_pairs={{0,1},{1,0},{2,3},{3,2},{4,5},{5,4},{6,7},{7,6},{8,9},{9,8},{10,11... | collective-permute-start | bytes 3145736 | tf_op jit(solution)/shard_map/ppermute | solution.py:25
  15.5 6.7 %collective-permute-start.2 = (f32[256,128]{1,0:T(8,128)S(1)}, f32[256,128]{1,0:T(8,128)S(1)}, u32[]{:S(2)}, u32[]{:S(2)}) collective-permute-start(f32[256,128]{1,0:T(8,128)S(1)} %slice_add_fusion.1), channel_id=1, source_target_pairs={{0,2},{1,3},{2,0},{3,1},{4,6},{5,7},{6,4},{7,5},{8,10},{9,11},{10,... | collective-permute-start | bytes 393224 | tf_op jit(solution)/shard_map/ppermute | solution.py:25
  22.2 21.4 %collective-permute-start.5 = (f32[256,512]{1,0:T(8,128)S(1)}, f32[256,512]{1,0:T(8,128)S(1)}, u32[]{:S(2)}, u32[]{:S(2)}) collective-permute-start(f32[256,512]{1,0:T(8,128)S(1)} %slice_add_fusion._), channel_id=1, source_target_pairs={{0,2},{1,3},{2,0},{3,1},{4,6},{5,7},{6,4},{7,5},{8,10},{9,11},{10,... | collective-permute-start | bytes 1572872 | tf_op jit(solution)/shard_map/ppermute | solution.py:25
  30.3 1.3 %collective-permute-start.3 = (f32[256,128]{1,0:T(8,128)S(1)}, f32[256,128]{1,0:T(8,128)S(1)}, u32[]{:S(2)}, u32[]{:S(2)}) collective-permute-start(f32[256,128]{1,0:T(8,128)S(1)} %get-tuple-element.43.refs_0_), channel_id=1, source_target_pairs={{0,1},{1,0},{2,3},{3,2},{4,5},{5,4},{6,7},{7,6},{8,9},{9,8},{10,11... | collective-permute-start | bytes 393224 | tf_op jit(solution)/shard_map/ppermute | solution.py:25
  37.9 5.6 %collective-permute-start.4 = (f32[256,128]{1,0:T(8,128)S(1)}, f32[256,128]{1,0:T(8,128)S(1)}, u32[]{:S(2)}, u32[]{:S(2)}) collective-permute-start(f32[256,128]{1,0:T(8,128)S(1)} %get-tuple-element.45.refs_0_), channel_id=1, source_target_pairs={{0,2},{1,3},{2,0},{3,1},{4,6},{5,7},{6,4},{7,5},{8,10},{9,11},{10,... | collective-permute-start | bytes 393224 | tf_op jit(solution)/shard_map/ppermute | solution.py:25
  49.7 5.6 %collective-permute-start.6 = (f32[256,128]{1,0:T(8,128)S(1)}, f32[256,128]{1,0:T(8,128)S(1)}, u32[]{:S(2)}, u32[]{:S(2)}) collective-permute-start(f32[256,128]{1,0:T(8,128)S(1)} %get-tuple-element.47.refs_0_), channel_id=1, source_target_pairs={{0,4},{1,5},{2,6},{3,7},{4,0},{5,1},{6,2},{7,3},{8,12},{9,13},{10,... | collective-permute-start | bytes 393224 | tf_op jit(solution)/shard_map/ppermute | solution.py:25
  53.0 10.0 %collective-permute-start.10 = (f32[256,128]{1,0:T(8,128)S(1)}, f32[256,128]{1,0:T(8,128)S(1)}, u32[]{:S(2)}, u32[]{:S(2)}) collective-permute-start(f32[256,128]{1,0:T(8,128)S(1)} %get-tuple-element.56), channel_id=1, source_target_pairs={{0,3},{1,2},{2,1},{3,0},{4,7},{5,6},{6,5},{7,4},{8,11},{9,10},{10,... | collective-permute-start | bytes 393224 | tf_op jit(solution)/shard_map/ppermute | solution.py:25
  53.1 9.9 %collective-permute-start.8 = (f32[256,128]{1,0:T(8,128)S(1)}, f32[256,128]{1,0:T(8,128)S(1)}, u32[]{:S(2)}, u32[]{:S(2)}) collective-permute-start(f32[256,128]{1,0:T(8,128)S(1)} %get-tuple-element.54), channel_id=1, source_target_pairs={{0,1},{1,0},{2,3},{3,2},{4,5},{5,4},{6,7},{7,6},{8,9},{9,8},{10,11... | collective-permute-start | bytes 393224 | tf_op jit(solution)/shard_map/ppermute | solution.py:25
  53.7 9.3 %collective-permute-start.9 = (f32[256,128]{1,0:T(8,128)S(1)}, f32[256,128]{1,0:T(8,128)S(1)}, u32[]{:S(2)}, u32[]{:S(2)}) collective-permute-start(f32[256,128]{1,0:T(8,128)S(1)} %get-tuple-element.55), channel_id=1, source_target_pairs={{0,2},{1,3},{2,0},{3,1},{4,6},{5,7},{6,4},{7,5},{8,10},{9,11},{10,... | collective-permute-start | bytes 393224 | tf_op jit(solution)/shard_map/ppermute | solution.py:25
  61.4 5.2 %collective-permute-start.7 = (f32[256,128]{1,0:T(8,128)S(1)}, f32[256,128]{1,0:T(8,128)S(1)}, u32[]{:S(2)}, u32[]{:S(2)}) collective-permute-start(f32[256,128]{1,0:T(8,128)S(1)} %get-tuple-element.53.refs_0_), channel_id=1, source_target_pairs={{0,8},{1,9},{2,10},{3,11},{4,12},{5,13},{6,14},{7,15},{8,0},{9,1},... | collective-permute-start | bytes 393224 | tf_op jit(solution)/shard_map/ppermute | solution.py:25
  63.3 9.5 %collective-permute-start.11 = (f32[256,128]{1,0:T(8,128)S(1)}, f32[256,128]{1,0:T(8,128)S(1)}, u32[]{:S(2)}, u32[]{:S(2)}) collective-permute-start(f32[256,128]{1,0:T(8,128)S(1)} %upper_maps_2.1.refs_3_.refs_0_), channel_id=1, source_target_pairs={{0,4},{1,5},{2,6},{3,7},{4,0},{5,1},{6,2},{7,3},{8,12},{9,13},{10,... | collective-permute-start | bytes 393224 | tf_op jit(solution)/shard_map/ppermute | solution.py:25
  73.2 6.7 %collective-permute-start.12 = (f32[256,128]{1,0:T(8,128)S(1)}, f32[256,128]{1,0:T(8,128)S(1)}, u32[]{:S(2)}, u32[]{:S(2)}) collective-permute-start(f32[256,128]{1,0:T(8,128)S(1)} %upper_maps_3.1), channel_id=1, source_target_pairs={{0,8},{1,9},{2,10},{3,11},{4,12},{5,13},{6,14},{7,15},{8,0},{9,1},... | collective-permute-start | bytes 393224 | tf_op jit(solution)/shard_map/ppermute | solution.py:25
  74.8 7.7 %collective-permute-start.13 = (f32[256,128]{1,0:T(8,128)S(1)}, f32[256,128]{1,0:T(8,128)S(1)}, u32[]{:S(2)}, u32[]{:S(2)}) collective-permute-start(f32[256,128]{1,0:T(8,128)S(1)} %get-tuple-element.59), channel_id=1, source_target_pairs={{0,16},{1,17},{2,18},{3,19},{4,20},{5,21},{6,22},{7,23},{8,24},{9,... | collective-permute-start | bytes 393224 | tf_op jit(solution)/shard_map/ppermute | solution.py:25
  82.6 7.3 %collective-permute-start.14 = (f32[256,128]{1,0:T(8,128)S(1)}, f32[256,128]{1,0:T(8,128)S(1)}, u32[]{:S(2)}, u32[]{:S(2)}) collective-permute-start(f32[256,128]{1,0:T(8,128)S(1)} %add.11.own_ref), channel_id=1, source_target_pairs={{0,16},{1,17},{2,18},{3,19},{4,20},{5,21},{6,22},{7,23},{8,24},{9,... | collective-permute-start | bytes 393224 | tf_op jit(solution)/shard_map/ppermute | solution.py:25
  89.5 8.8 %copy-start.8 = (f32[5,128,128]{2,1,0:T(8,128)}, f32[5,128,128]{2,1,0:T(8,128)S(1)}, u32[]{:S(2)}) copy-start(f32[5,128,128]{2,1,0:T(8,128)S(1)} %get-tuple-element.68) | copy-start | bytes 983044
  90.4 5.5 %copy-start.3 = (f32[128,128]{1,0:T(8,128)}, f32[128,128]{1,0:T(8,128)S(1)}, u32[]{:S(2)}) copy-start(f32[128,128]{1,0:T(8,128)S(1)} %top_sample.1.refs_0_) | copy-start | bytes 196612
  90.4 1.9 %collective-permute-start.15 = (f32[128,128]{1,0:T(8,128)S(1)}, f32[128,128]{1,0:T(8,128)S(1)}, u32[]{:S(2)}, u32[]{:S(2)}) collective-permute-start(f32[128,128]{1,0:T(8,128)S(1)} %top_sample.1.refs_0_), channel_id=1, source_target_pairs={{0,1},{1,0},{2,3},{3,2},{4,5},{5,4},{6,7},{7,6},{8,9},{9,8},{10,11... | collective-permute-start | bytes 196616 | tf_op jit(solution)/shard_map/ppermute | solution.py:25
  90.5 5.0 %collective-permute-start.16 = (f32[128,128]{1,0:T(8,128)S(1)}, f32[128,128]{1,0:T(8,128)S(1)}, u32[]{:S(2)}, u32[]{:S(2)}) collective-permute-start(f32[128,128]{1,0:T(8,128)S(1)} %top_sample.1.refs_0_), channel_id=1, source_target_pairs={{0,2},{1,3},{2,0},{3,1},{4,6},{5,7},{6,4},{7,5},{8,10},{9,11},{10,... | collective-permute-start | bytes 196616 | tf_op jit(solution)/shard_map/ppermute | solution.py:25
  91.1 4.9 %collective-permute-start.17 = (f32[128,128]{1,0:T(8,128)S(1)}, f32[128,128]{1,0:T(8,128)S(1)}, u32[]{:S(2)}, u32[]{:S(2)}) collective-permute-start(f32[128,128]{1,0:T(8,128)S(1)} %top_sample.1.refs_0_), channel_id=1, source_target_pairs={{0,3},{1,2},{2,1},{3,0},{4,7},{5,6},{6,5},{7,4},{8,11},{9,10},{10,... | collective-permute-start | bytes 196616 | tf_op jit(solution)/shard_map/ppermute | solution.py:25
  92.4 3.6 %copy-start.5 = (f32[128,128]{1,0:T(8,128)}, f32[128,128]{1,0:T(8,128)S(1)}, u32[]{:S(2)}) copy-start(f32[128,128]{1,0:T(8,128)S(1)} %collective-permute-done.15.refs_1_) | copy-start | bytes 196612
  95.5 0.6 copy-start.6
  96.1 0.6 copy-start.7

commit v3 on v2

--- a/solution.py
+++ b/solution.py
@@ -39,60 +39,68 @@
     )
 
 
-def inverse_factor(gram):
+def square_sum(block):
+    squares = block * block
+    return jnp.sum(jnp.sum(squares, axis=0, keepdims=True), axis=1, keepdims=True)
+
+
+def inverse_factor(gram, trace):
     size = gram.shape[0]
     high = 8
     count = size // high
-    lane_all = lax.broadcasted_iota(jnp.int32, (size, size), 1)
-    diag = lane_all == lax.broadcasted_iota(jnp.int32, (size, size), 0)
-    trace = jnp.sum(
-        jnp.sum(jnp.where(diag, gram, 0.0), axis=0, keepdims=True), axis=1, keepdims=True
-    )
-    shift = 0.0001 * trace / size + 1e-06
-    gram = jnp.where(diag, gram + shift, gram)
+    square = (size, size)
+    diag = lax.broadcasted_iota(jnp.int32, square, 1) == lax.broadcasted_iota(jnp.int32, square, 0)
+    gram = jnp.where(diag, gram + (0.0001 * trace / size + 1e-06), gram)
     rows = [gram[high * g : high * g + high, :] for g in range(count)]
     shape = (high, size)
     lane = lax.broadcasted_iota(jnp.int32, shape, 1)
     sub = lax.broadcasted_iota(jnp.int32, shape, 0)
 
-    def along_lanes(block, at):
-        return jnp.broadcast_to(block[:, at : at + 1], shape)
+    def along_lanes(block, first):
+        return [jnp.broadcast_to(block[:, first + k : first + k + 1], shape) for k in range(high)]
 
     def along_rows(block, at):
         return jnp.broadcast_to(block[at : at + 1, :], shape)
 
     found = []
+    here = along_lanes(rows[0], 0)
     for b in range(count):
-        first = b * high
-        panel = rows[b]
-        columns = [along_lanes(panel, first + k) for k in range(high)]
-        inside = (lane >= first) & (lane < first + high)
-        panel = jnp.where(inside, jnp.where(lane - first == sub, 1.0, 0.0), panel)
-        forward, full = panel, panel
-        forward_scale = jnp.zeros(shape, jnp.float32)
-        full_scale = jnp.zeros(shape, jnp.float32)
+        first, after = b * high, (b + 1) * high
+        more = b + 1 < count
+        inside = (lane >= first) & (lane < after)
+        full = jnp.where(inside, jnp.where(lane - first == sub, 1.0, 0.0), rows[b])
+        done = jnp.zeros(shape, jnp.float32)
+        if more:
+            under = along_lanes(rows[b + 1], first)
+            right = along_lanes(rows[b], after)
+            corner = along_lanes(rows[b + 1], after)
         for i in range(high):
-            pivot = along_rows(columns[i], i)
-            inverse = 1.0 / pivot
-            others = jnp.where(sub == i, 0.0, columns[i])
-            below = jnp.where(sub > i, columns[i], 0.0)
+            root = lax.rsqrt(along_rows(here[i], i))
+            inverse = root * root
+            below = jnp.where(sub > i, here[i], 0.0)
+            scaled = below * inverse
+            if more:
+                low = under[i] * inverse
             for k in range(i + 1, high):
-                columns[k] = columns[k] - others * along_rows(columns[k], i) * inverse
-            row = along_rows(forward, i) * inverse
-            forward = forward - below * row
-            full = full - others * row
-            forward_scale = jnp.where(sub == i, lax.rsqrt(pivot), forward_scale)
-            full_scale = jnp.where(sub == i, inverse, full_scale)
-        found.append(jnp.where(lane < first + high, forward * forward_scale, 0.0))
-        if b + 1 == count:
+                x = along_rows(here[k], i)
+                here[k] = here[k] - ((below * x) * inverse if k < i + 3 else scaled * x)
+                if more:
+                    under[k] = under[k] - low * x
+            if more:
+                for k in range(high):
+                    x = along_rows(right[k], i)
+                    right[k] = right[k] - scaled * x
+                    corner[k] = corner[k] - low * x
+            x = along_rows(full, i)
+            done = jnp.where(sub == i, x * root, done)
+            full = full - scaled * x
+        found.append(jnp.where(lane < after, done, 0.0))
+        if not more:
             break
-        full = full * full_scale
-        full_rows = [along_rows(full, k) for k in range(high)]
+        change = dot(done.T, done)
         for g in range(b + 1, count):
-            terms = [along_lanes(rows[g], first + k) * full_rows[k] for k in range(high)]
-            while len(terms) > 1:
-                terms = [terms[t] + terms[t + 1] for t in range(0, len(terms), 2)]
-            rows[g] = jnp.where(inside, 0.0, rows[g]) - terms[0]
+            rows[g] = jnp.where(inside, 0.0, rows[g]) - change[high * g : high * g + high]
+        here = corner
     return jnp.concatenate(found, axis=0)
 
 
@@ -251,12 +259,12 @@
     reduced = keep_ref[...] + first_ref[...] + second_ref[...]
     reduced_t = reduced.T
     both = dot(reduced_t, jnp.concatenate([reduced, sketch_red_ref[...]], axis=1))
-    inverse = inverse_factor(both[:, :rank])
-    moved = dot(inverse, both)
+    inverse = inverse_factor(both[:, :rank], square_sum(reduced))
+    moved = dot(inverse, jnp.concatenate([both, reduced_t], axis=1))
     pair_ref[:rank, :] = moved[:, :rank]
-    pair_ref[rank:, :] = moved[:, rank:]
+    pair_ref[rank:, :] = moved[:, rank : 2 * rank]
+    basis_t_ref[...] = moved[:, 2 * rank :]
     basis_ref[...] = dot_nt(reduced, inverse)
-    basis_t_ref[...] = dot(inverse, reduced_t)
 
 
 def small_params():
@@ -307,24 +315,23 @@
     other = other_sample - dot(back, own_sketch)
     own_t, other_t = own.T, other.T
     stacked_t = jnp.concatenate([own_t, other_t], axis=1)
+    stacked = jnp.concatenate([own, other], axis=0)
     right = jnp.concatenate(
-        [
-            jnp.concatenate([own, own_sketch], axis=1),
-            jnp.concatenate([other, other_sketch], axis=1),
-        ],
-        axis=0,
+        [stacked, jnp.concatenate([own_sketch, other_sketch], axis=0)], axis=1
     )
-    both = dot(stacked_t, right)
-    inverse = inverse_factor(both[:, :rank])
+    both = dot(stacked_t, stacked if last else right)
+    if not last:
+        crossed = dot(other_t, back)
+    inverse = inverse_factor(both[:, :rank], square_sum(own) + square_sum(other))
     block_ref[...] = dot_nt(own, inverse)
     if last:
         pair_ref[...] = dot(inverse, stacked_t)
         return
-    moved = dot(inverse, both)
+    moved = dot(inverse, jnp.concatenate([both, own_t, crossed], axis=1))
     pair_ref[:rank, :] = moved[:, :rank]
-    pair_ref[rank:, :] = moved[:, rank:]
-    maps_ref[0] = dot(inverse, own_t)
-    maps_ref[1] = dot(inverse, dot(other_t, back))
+    pair_ref[rank:, :] = moved[:, rank : 2 * rank]
+    maps_ref[0] = moved[:, 2 * rank : 3 * rank]
+    maps_ref[1] = moved[:, 3 * rank :]
 
 
 def coupling_spec(couplings, tree_level):

time: 98.8 us -> 103 us (1.043)
  Pallas kernels: 48.7 us -> 52.1 us
    pallas_call x4, Pallas kernels: 24.8 us -> 27.5 us  [merge_step(): pl.pallas_call(functools.partial(merge_body, tree_level), grid=(1,), out_...]
  transfers between devices with their start and end apart: 18 -> 18, of which waited for: 10 -> 9; matrix products, arithmetic and copies ran while one was open for 6% -> 7% of each run, Pallas kernels for 28% -> 30%
where the time goes in v3:
time: 103 us; the launch traced here: 102 us
  Pallas kernels  52.1 us (51%)
  waiting for transfers between devices  21.7 us (21%)
  starting transfers between devices  19.3 us (19%)
  other arithmetic  6.71 us (7%)
  local copies, waits for them, and re-layouts  1.51 us (1%)
    pallas_call x4, Pallas kernels, merge_step(): pl.pallas_call(functools.partial(merge_body, tree_level), grid=(1,), out_...  27.5 us
    ppermute x18, waiting for transfers between devices, from_partner(): return lax.ppermute(block, axis, route)  21.7 us
    ppermute x18, starting transfers between devices, from_partner(): return lax.ppermute(block, axis, route)  19.3 us
    pallas_call x1, Pallas kernels, sample_rows(): pl.pallas_call(functools.partial(spmm_body, leaves=leaves), out_shape=[ja...  11.2 us
    pallas_call x1, Pallas kernels, leaf_step(): pl.pallas_call(leaf_body, grid=(1,), out_shape=[jax.ShapeDtypeStruct((lea...  7.19 us
    pallas_call x1, other arithmetic, merge_step(): pl.pallas_call(functools.partial(merge_body, tree_level), grid=(1,), out_...  6.6 us
  transfers between devices with their start and end apart: 18, of which 9 were waited for; matrix products, arithmetic and copies ran while one was open for 7% of the time, Pallas kernels for 30%

profile of v3, /device:TPU:0, one launch (start us, length us, event | category | flops | bytes accessed | tf_op | source)
XLA Modules:
  0.0 102.4 jit_solution(3448595633634824243)
XLA Ops:
  0.6 0.0 copy-start.2
  0.6 0.0 copy-start.1
  0.7 0.0 copy-start.4
  0.7 0.7 copy-done.4
  1.4 11.2 %spmm.1 = (f32[512,512]{1,0:T(8,128)S(1)}, f32[512,512]{1,0:T(8,128)S(1)}) custom-call(s32[168]{0:T(256)S(1)} %copy-done.4, bf16[168,128,128]{2,1,0:T(8,128)(2,1)} %tiles_ref.1, bf16[6144,512]{1,0:T(8,128)(2,1)} %sketch_ref.1), custom_call_target="tpu_custom_call" | custom-call | flops 6442450944 | bytes 13893632 | tf_op jit(solution)/shard_map/spmm/pallas_call | solution.py:205
  12.6 0.0 copy-start
  12.6 0.0 copy-done.2
  12.6 0.7 reduced_1.1
  13.3 0.5 collective-permute-start
  13.9 0.0 copy-done.1
  13.9 0.9 reduced_2.1
  14.7 0.3 collective-permute-done.first_ref
  15.0 0.4 collective-permute-start.1
  15.5 2.7 %collective-permute-start.2 = (f32[256,128]{1,0:T(8,128)S(1)}, f32[256,128]{1,0:T(8,128)S(1)}, u32[]{:S(2)}, u32[]{:S(2)}) collective-permute-start(f32[256,128]{1,0:T(8,128)S(1)} %slice_add_fusion.1), channel_id=1, source_target_pairs={{0,2},{1,3},{2,0},{3,1},{4,6},{5,7},{6,4},{7,5},{8,10},{9,11},{10,... | collective-permute-start | bytes 393224 | tf_op jit(solution)/shard_map/ppermute | solution.py:25
  18.1 0.0 collective-permute-done.1.refs_1_
  18.1 0.1 slice_add_fusion._
  18.2 3.9 %collective-permute-done.2.second_ref = f32[256,128]{1,0:T(8,128)S(1)} collective-permute-done((f32[256,128]{1,0:T(8,128)S(1)}, f32[256,128]{1,0:T(8,128)S(1)}, u32[]{:S(2)}, u32[]{:S(2)}) %collective-permute-start.2) | collective-permute-done | bytes 131104 | tf_op jit(solution)/shard_map/ppermute | solution.py:25
  22.2 1.7 %collective-permute-start.5 = (f32[256,512]{1,0:T(8,128)S(1)}, f32[256,512]{1,0:T(8,128)S(1)}, u32[]{:S(2)}, u32[]{:S(2)}) collective-permute-start(f32[256,512]{1,0:T(8,128)S(1)} %slice_add_fusion._), channel_id=1, source_target_pairs={{0,2},{1,3},{2,0},{3,1},{4,6},{5,7},{6,4},{7,5},{8,10},{9,11},{10,... | collective-permute-start | bytes 1572872 | tf_op jit(solution)/shard_map/ppermute | solution.py:25
  23.9 7.2 %leaf_orth.1 = (f32[256,128]{1,0:T(8,128)}, f32[128,256]{1,0:T(8,128)S(1)}, f32[256,128]{1,0:T(8,128)S(1)}) custom-call(f32[512,128]{1,0:T(8,128)S(1)} %get-tuple-element.35.keep_ref, f32[512,128]{1,0:T(8,128)S(1)} %collective-permute-done.first_ref, f32[256,128]{1,0:T(8,128)S(1)} %collective-permute-done.2.second_ref, ...), custom_call_target="tpu_custom_call" | custom-call | flops 80000000 | bytes 240000 | tf_op jit(solution)/shard_map/leaf_orth/pallas_call | solution.py:282
  31.1 0.0 collective-permute-start.3
  31.1 1.3 %collective-permute-done.3.refs_1_ = f32[256,128]{1,0:T(8,128)S(1)} collective-permute-done((f32[256,128]{1,0:T(8,128)S(1)}, f32[256,128]{1,0:T(8,128)S(1)}, u32[]{:S(2)}, u32[]{:S(2)}) %collective-permute-start.3) | collective-permute-done | bytes 131104 | tf_op jit(solution)/shard_map/ppermute | solution.py:25
  32.4 0.0 copy-done
  32.4 6.9 %merge_orth_0.1 = (f32[128,128]{1,0:T(8,128)S(1)}, f32[2,128,128]{2,1,0:T(8,128)S(1)}, f32[256,128]{1,0:T(8,128)S(1)}) custom-call(f32[256,128]{1,0:T(8,128)S(1)} %get-tuple-element.43.refs_0_, f32[256,128]{1,0:T(8,128)S(1)} %collective-permute-done.3.refs_1_, bf16[1,5,128,128]{3,2,1,0:T(8,128)(2,1)S(1)} %copy-done), custom_call_target="tpu_custom_call" | custom-call | flops 80000000 | bytes 240000 | tf_op jit(solution)/shard_map/merge_orth_0/pallas_call | solution.py:345
  39.4 0.3 collective-permute-start.4
  39.7 5.3 %collective-permute-done.4.refs_1_ = f32[256,128]{1,0:T(8,128)S(1)} collective-permute-done((f32[256,128]{1,0:T(8,128)S(1)}, f32[256,128]{1,0:T(8,128)S(1)}, u32[]{:S(2)}, u32[]{:S(2)}) %collective-permute-start.4) | collective-permute-done | bytes 131104 | tf_op jit(solution)/shard_map/ppermute | solution.py:25
  45.0 0.0 collective-permute-done.5.refs_3_.refs_2_
  45.0 6.8 %merge_orth_1.1 = (f32[128,128]{1,0:T(8,128)S(1)}, f32[2,128,128]{2,1,0:T(8,128)S(1)}, f32[256,128]{1,0:T(8,128)S(1)}) custom-call(f32[256,128]{1,0:T(8,128)S(1)} %get-tuple-element.45.refs_0_, f32[256,128]{1,0:T(8,128)S(1)} %collective-permute-done.4.refs_1_, bf16[1,5,128,128]{3,2,1,0:T(8,128)(2,1)S(1)} %copy-done, ...), custom_call_target="tpu_custom_call" | custom-call | flops 80000000 | bytes 240000 | tf_op jit(solution)/shard_map/merge_orth_1/pallas_call | solution.py:345
  51.8 1.6 %collective-permute-start.6 = (f32[256,128]{1,0:T(8,128)S(1)}, f32[256,128]{1,0:T(8,128)S(1)}, u32[]{:S(2)}, u32[]{:S(2)}) collective-permute-start(f32[256,128]{1,0:T(8,128)S(1)} %get-tuple-element.47.refs_0_), channel_id=1, source_target_pairs={{0,4},{1,5},{2,6},{3,7},{4,0},{5,1},{6,2},{7,3},{8,12},{9,13},{10,... | collective-permute-start | bytes 393224 | tf_op jit(solution)/shard_map/ppermute | solution.py:25
  53.3 1.8 %lower_maps.1 = (f32[256,128]{1,0:T(8,128)S(1)}, f32[256,128]{1,0:T(8,128)S(1)}, f32[256,128]{1,0:T(8,128)S(1)}, f32[256,128]{1,0:T(8,128)S(1)}) custom-call(f32[512,512]{1,0:T(8,128)S(1)} %get-tuple-element.34.refs_1_.refs_0_, f32[512,512]{1,0:T(8,128)S(1)} %collective-permute-done.1.refs_1_, f32[256,512]{1,0:T(8,128)S(1)} %collective-permute-done.5.refs_3_.refs_2_, ...), custom_call_target="tpu_custom_call" | custom-call | flops 20000000 | bytes 60000 | tf_op jit(solution)/shard_map/lower_maps/pallas_call | solution.py:389
  55.2 0.1 collective-permute-start.10
  55.2 0.6 collective-permute-start.8
  55.9 1.5 %collective-permute-start.9 = (f32[256,128]{1,0:T(8,128)S(1)}, f32[256,128]{1,0:T(8,128)S(1)}, u32[]{:S(2)}, u32[]{:S(2)}) collective-permute-start(f32[256,128]{1,0:T(8,128)S(1)} %get-tuple-element.55), channel_id=1, source_target_pairs={{0,2},{1,3},{2,0},{3,1},{4,6},{5,7},{6,4},{7,5},{8,10},{9,11},{10,... | collective-permute-start | bytes 393224 | tf_op jit(solution)/shard_map/ppermute | solution.py:25
  57.4 0.0 collective-permute-done.6.refs_1_
  57.4 6.8 %merge_orth_2.1 = (f32[128,128]{1,0:T(8,128)S(1)}, f32[2,128,128]{2,1,0:T(8,128)S(1)}, f32[256,128]{1,0:T(8,128)S(1)}) custom-call(f32[256,128]{1,0:T(8,128)S(1)} %get-tuple-element.47.refs_0_, f32[256,128]{1,0:T(8,128)S(1)} %collective-permute-done.6.refs_1_, bf16[1,5,128,128]{3,2,1,0:T(8,128)(2,1)S(1)} %copy-done, ...), custom_call_target="tpu_custom_call" | custom-call | flops 80000000 | bytes 240000 | tf_op jit(solution)/shard_map/merge_orth_2/pallas_call | solution.py:345
  64.1 1.6 %collective-permute-start.7 = (f32[256,128]{1,0:T(8,128)S(1)}, f32[256,128]{1,0:T(8,128)S(1)}, u32[]{:S(2)}, u32[]{:S(2)}) collective-permute-start(f32[256,128]{1,0:T(8,128)S(1)} %get-tuple-element.53.refs_0_), channel_id=1, source_target_pairs={{0,8},{1,9},{2,10},{3,11},{4,12},{5,13},{6,14},{7,15},{8,0},{9,1},... | collective-permute-start | bytes 393224 | tf_op jit(solution)/shard_map/ppermute | solution.py:25
  65.8 0.0 collective-permute-done.10.refs_3_
  65.8 0.0 collective-permute-done.8.refs_1_
  65.8 0.0 collective-permute-done.9.refs_2_
  65.8 0.3 upper_maps_2.1.refs_3_.refs_0_
  66.1 1.0 collective-permute-start.11
  67.1 2.2 %collective-permute-done.7.refs_1_ = f32[256,128]{1,0:T(8,128)S(1)} collective-permute-done((f32[256,128]{1,0:T(8,128)S(1)}, f32[256,128]{1,0:T(8,128)S(1)}, u32[]{:S(2)}, u32[]{:S(2)}) %collective-permute-start.7) | collective-permute-done | bytes 131104 | tf_op jit(solution)/shard_map/ppermute | solution.py:25
  69.3 7.0 %merge_orth_3.1 = (f32[128,128]{1,0:T(8,128)S(1)}, f32[2,128,128]{2,1,0:T(8,128)S(1)}, f32[256,128]{1,0:T(8,128)S(1)}) custom-call(f32[256,128]{1,0:T(8,128)S(1)} %get-tuple-element.53.refs_0_, f32[256,128]{1,0:T(8,128)S(1)} %collective-permute-done.7.refs_1_, bf16[1,5,128,128]{3,2,1,0:T(8,128)(2,1)S(1)} %copy-done, f32[256,128]{1,0:T(8,128)S(1)} %upper_maps_2.1.refs_3_.refs_0_), custom_call_target="tpu_custom_call" | custom-call | flops 80000000 | bytes 240000 | tf_op jit(solution)/shard_map/merge_orth_3/pallas_call | solution.py:345
  76.3 0.0 collective-permute-done.11.refs_1_
  76.3 0.3 upper_maps_3.1
  76.6 1.6 %collective-permute-start.12 = (f32[256,128]{1,0:T(8,128)S(1)}, f32[256,128]{1,0:T(8,128)S(1)}, u32[]{:S(2)}, u32[]{:S(2)}) collective-permute-start(f32[256,128]{1,0:T(8,128)S(1)} %upper_maps_3.1), channel_id=1, source_target_pairs={{0,8},{1,9},{2,10},{3,11},{4,12},{5,13},{6,14},{7,15},{8,0},{9,1},... | collective-permute-start | bytes 393224 | tf_op jit(solution)/shard_map/ppermute | solution.py:25
  78.3 2.6 %collective-permute-start.13 = (f32[256,128]{1,0:T(8,128)S(1)}, f32[256,128]{1,0:T(8,128)S(1)}, u32[]{:S(2)}, u32[]{:S(2)}) collective-permute-start(f32[256,128]{1,0:T(8,128)S(1)} %get-tuple-element.59), channel_id=1, source_target_pairs={{0,16},{1,17},{2,18},{3,19},{4,20},{5,21},{6,22},{7,23},{8,24},{9,... | collective-permute-start | bytes 393224 | tf_op jit(solution)/shard_map/ppermute | solution.py:25
  80.9 2.5 %collective-permute-done.12 = f32[256,128]{1,0:T(8,128)S(1)} collective-permute-done((f32[256,128]{1,0:T(8,128)S(1)}, f32[256,128]{1,0:T(8,128)S(1)}, u32[]{:S(2)}, u32[]{:S(2)}) %collective-permute-start.12) | collective-permute-done | bytes 131104 | tf_op jit(solution)/shard_map/ppermute | solution.py:25
  83.4 2.6 %collective-permute-done.13 = f32[256,128]{1,0:T(8,128)S(1)} collective-permute-done((f32[256,128]{1,0:T(8,128)S(1)}, f32[256,128]{1,0:T(8,128)S(1)}, u32[]{:S(2)}, u32[]{:S(2)}) %collective-permute-start.13) | collective-permute-done | bytes 131104 | tf_op jit(solution)/shard_map/ppermute | solution.py:25
  86.0 1.1 %collective-permute-start.14 = (f32[256,128]{1,0:T(8,128)S(1)}, f32[256,128]{1,0:T(8,128)S(1)}, u32[]{:S(2)}, u32[]{:S(2)}) collective-permute-start(f32[256,128]{1,0:T(8,128)S(1)} %add.11.own_ref), channel_id=1, source_target_pairs={{0,16},{1,17},{2,18},{3,19},{4,20},{5,21},{6,22},{7,23},{8,24},{9,... | collective-permute-start | bytes 393224 | tf_op jit(solution)/shard_map/ppermute | solution.py:25
  87.1 6.6 %merge_orth_4.1 = (f32[5,128,128]{2,1,0:T(8,128)S(1)}, f32[128,256]{1,0:T(8,128)S(1)}, f32[8,128]{1,0:T(8,128)}) fusion(f32[5,128,128]{2,1,0:T(8,128)S(1)} %bitcast_dynamic-update-slice_fusion.1, f32[256,128]{1,0:T(8,128)S(1)} %get-tuple-element.59, f32[256,128]{1,0:T(8,128)S(1)} %collective-permute-done.13, bf16[1,5,128,128]{3,2,1,0:T(8,128)(2,1)S(1)} %copy-done, ...), kind=kCustom, calls=%fused_computation.2 | custom fusion | flops 80000000 | bytes 757760 | tf_op jit(solution)/shard_map/merge_orth_4/pallas_call | solution.py:345
  93.7 0.0 copy-start.8
  93.7 0.0 collective-permute-done.14.other_ref
  93.7 0.6 top_sample.1.refs_0_
  94.3 0.0 copy-start.3
  94.3 0.1 collective-permute-start.15
  94.4 0.5 collective-permute-start.16
  94.9 1.4 %collective-permute-start.17 = (f32[128,128]{1,0:T(8,128)S(1)}, f32[128,128]{1,0:T(8,128)S(1)}, u32[]{:S(2)}, u32[]{:S(2)}) collective-permute-start(f32[128,128]{1,0:T(8,128)S(1)} %top_sample.1.refs_0_), channel_id=1, source_target_pairs={{0,3},{1,2},{2,1},{3,0},{4,7},{5,6},{6,5},{7,4},{8,11},{9,10},{10,... | collective-permute-start | bytes 196616 | tf_op jit(solution)/shard_map/ppermute | solution.py:25
  96.2 0.0 collective-permute-done.15.refs_1_
  96.2 3.1 %collective-permute-done.16.refs_2_ = f32[128,128]{1,0:T(8,128)S(1)} collective-permute-done((f32[128,128]{1,0:T(8,128)S(1)}, f32[128,128]{1,0:T(8,128)S(1)}, u32[]{:S(2)}, u32[]{:S(2)}) %collective-permute-start.16) | collective-permute-done | bytes 65568 | tf_op jit(solution)/shard_map/ppermute | solution.py:25
  99.3 0.5 collective-permute-done.17.refs_3_
  99.8 0.0 copy-done.3
  99.8 0.1 copy-done.6
  100.0 0.6 copy-done.7
  100.6 1.7 %top_columns.1 = f32[1,128,512]{2,1,0:T(8,128)} custom-call(f32[128,128]{1,0:T(8,128)} %copy-done.3, f32[128,128]{1,0:T(8,128)} %copy-done.5, f32[128,128]{1,0:T(8,128)} %copy-done.6, f32[128,128]{1,0:T(8,128)} %copy-done.7), custom_call_target="tpu_custom_call" | custom-call | tf_op jit(solution)/shard_map/top_columns/pallas_call | solution.py:471
  (11 shorter events, 0.1 us)
Async XLA Ops:
  0.6 12.0 %copy-start.2 = (f32[512,128]{1,0:T(8,128)S(1)}, f32[512,128]{1,0:T(8,128)}, u32[]{:S(2)}) copy-start(f32[512,128]{1,0:T(8,128)} %refs_0_.3) | copy-start | bytes 786436
  0.6 13.2 %copy-start.1 = (bf16[256,512]{1,0:T(8,128)(2,1)S(1)}, bf16[256,512]{1,0:T(8,128)(2,1)}, u32[]{:S(2)}) copy-start(bf16[256,512]{1,0:T(8,128)(2,1)} %refs_3_.1) | copy-start | bytes 786436
  0.7 0.7 copy-start.4
  12.6 19.9 %copy-start = (bf16[1,5,128,128]{3,2,1,0:T(8,128)(2,1)S(1)}, bf16[1,5,128,128]{3,2,1,0:T(8,128)(2,1)}, u32[]{:S(2)}) copy-start(bf16[1,5,128,128]{3,2,1,0:T(8,128)(2,1)} %coupling_ref.1) | copy-start | bytes 491524
  13.3 1.7 %collective-permute-start = (f32[512,128]{1,0:T(8,128)S(1)}, f32[512,128]{1,0:T(8,128)S(1)}, u32[]{:S(2)}, u32[]{:S(2)}) collective-permute-start(f32[512,128]{1,0:T(8,128)S(1)} %reduced_1.1), channel_id=1, source_target_pairs={{0,1},{1,0},{2,3},{3,2},{4,5},{5,4},{6,7},{7,6},{8,9},{9,8},{10,11... | collective-permute-start | bytes 786440 | tf_op jit(solution)/shard_map/ppermute | solution.py:25
  15.0 3.1 %collective-permute-start.1 = (f32[512,512]{1,0:T(8,128)S(1)}, f32[512,512]{1,0:T(8,128)S(1)}, u32[]{:S(2)}, u32[]{:S(2)}) collective-permute-start(f32[512,512]{1,0:T(8,128)S(1)} %get-tuple-element.37.refs_1_), channel_id=1, source_target_pairs={{0,1},{1,0},{2,3},{3,2},{4,5},{5,4},{6,7},{7,6},{8,9},{9,8},{10,11... | collective-permute-start | bytes 3145736 | tf_op jit(solution)/shard_map/ppermute | solution.py:25
  15.5 6.7 %collective-permute-start.2 = (f32[256,128]{1,0:T(8,128)S(1)}, f32[256,128]{1,0:T(8,128)S(1)}, u32[]{:S(2)}, u32[]{:S(2)}) collective-permute-start(f32[256,128]{1,0:T(8,128)S(1)} %slice_add_fusion.1), channel_id=1, source_target_pairs={{0,2},{1,3},{2,0},{3,1},{4,6},{5,7},{6,4},{7,5},{8,10},{9,11},{10,... | collective-permute-start | bytes 393224 | tf_op jit(solution)/shard_map/ppermute | solution.py:25
  22.2 22.9 %collective-permute-start.5 = (f32[256,512]{1,0:T(8,128)S(1)}, f32[256,512]{1,0:T(8,128)S(1)}, u32[]{:S(2)}, u32[]{:S(2)}) collective-permute-start(f32[256,512]{1,0:T(8,128)S(1)} %slice_add_fusion._), channel_id=1, source_target_pairs={{0,2},{1,3},{2,0},{3,1},{4,6},{5,7},{6,4},{7,5},{8,10},{9,11},{10,... | collective-permute-start | bytes 1572872 | tf_op jit(solution)/shard_map/ppermute | solution.py:25
  31.1 1.3 %collective-permute-start.3 = (f32[256,128]{1,0:T(8,128)S(1)}, f32[256,128]{1,0:T(8,128)S(1)}, u32[]{:S(2)}, u32[]{:S(2)}) collective-permute-start(f32[256,128]{1,0:T(8,128)S(1)} %get-tuple-element.43.refs_0_), channel_id=1, source_target_pairs={{0,1},{1,0},{2,3},{3,2},{4,5},{5,4},{6,7},{7,6},{8,9},{9,8},{10,11... | collective-permute-start | bytes 393224 | tf_op jit(solution)/shard_map/ppermute | solution.py:25
  39.4 5.6 %collective-permute-start.4 = (f32[256,128]{1,0:T(8,128)S(1)}, f32[256,128]{1,0:T(8,128)S(1)}, u32[]{:S(2)}, u32[]{:S(2)}) collective-permute-start(f32[256,128]{1,0:T(8,128)S(1)} %get-tuple-element.45.refs_0_), channel_id=1, source_target_pairs={{0,2},{1,3},{2,0},{3,1},{4,6},{5,7},{6,4},{7,5},{8,10},{9,11},{10,... | collective-permute-start | bytes 393224 | tf_op jit(solution)/shard_map/ppermute | solution.py:25
  51.8 5.6 %collective-permute-start.6 = (f32[256,128]{1,0:T(8,128)S(1)}, f32[256,128]{1,0:T(8,128)S(1)}, u32[]{:S(2)}, u32[]{:S(2)}) collective-permute-start(f32[256,128]{1,0:T(8,128)S(1)} %get-tuple-element.47.refs_0_), channel_id=1, source_target_pairs={{0,4},{1,5},{2,6},{3,7},{4,0},{5,1},{6,2},{7,3},{8,12},{9,13},{10,... | collective-permute-start | bytes 393224 | tf_op jit(solution)/shard_map/ppermute | solution.py:25
  55.2 10.6 %collective-permute-start.10 = (f32[256,128]{1,0:T(8,128)S(1)}, f32[256,128]{1,0:T(8,128)S(1)}, u32[]{:S(2)}, u32[]{:S(2)}) collective-permute-start(f32[256,128]{1,0:T(8,128)S(1)} %get-tuple-element.56), channel_id=1, source_target_pairs={{0,3},{1,2},{2,1},{3,0},{4,7},{5,6},{6,5},{7,4},{8,11},{9,10},{10,... | collective-permute-start | bytes 393224 | tf_op jit(solution)/shard_map/ppermute | solution.py:25
  55.2 10.6 %collective-permute-start.8 = (f32[256,128]{1,0:T(8,128)S(1)}, f32[256,128]{1,0:T(8,128)S(1)}, u32[]{:S(2)}, u32[]{:S(2)}) collective-permute-start(f32[256,128]{1,0:T(8,128)S(1)} %get-tuple-element.54), channel_id=1, source_target_pairs={{0,1},{1,0},{2,3},{3,2},{4,5},{5,4},{6,7},{7,6},{8,9},{9,8},{10,11... | collective-permute-start | bytes 393224 | tf_op jit(solution)/shard_map/ppermute | solution.py:25
  55.9 9.9 %collective-permute-start.9 = (f32[256,128]{1,0:T(8,128)S(1)}, f32[256,128]{1,0:T(8,128)S(1)}, u32[]{:S(2)}, u32[]{:S(2)}) collective-permute-start(f32[256,128]{1,0:T(8,128)S(1)} %get-tuple-element.55), channel_id=1, source_target_pairs={{0,2},{1,3},{2,0},{3,1},{4,6},{5,7},{6,4},{7,5},{8,10},{9,11},{10,... | collective-permute-start | bytes 393224 | tf_op jit(solution)/shard_map/ppermute | solution.py:25
  64.1 5.2 %collective-permute-start.7 = (f32[256,128]{1,0:T(8,128)S(1)}, f32[256,128]{1,0:T(8,128)S(1)}, u32[]{:S(2)}, u32[]{:S(2)}) collective-permute-start(f32[256,128]{1,0:T(8,128)S(1)} %get-tuple-element.53.refs_0_), channel_id=1, source_target_pairs={{0,8},{1,9},{2,10},{3,11},{4,12},{5,13},{6,14},{7,15},{8,0},{9,1},... | collective-permute-start | bytes 393224 | tf_op jit(solution)/shard_map/ppermute | solution.py:25
  66.1 10.2 %collective-permute-start.11 = (f32[256,128]{1,0:T(8,128)S(1)}, f32[256,128]{1,0:T(8,128)S(1)}, u32[]{:S(2)}, u32[]{:S(2)}) collective-permute-start(f32[256,128]{1,0:T(8,128)S(1)} %upper_maps_2.1.refs_3_.refs_0_), channel_id=1, source_target_pairs={{0,4},{1,5},{2,6},{3,7},{4,0},{5,1},{6,2},{7,3},{8,12},{9,13},{10,... | collective-permute-start | bytes 393224 | tf_op jit(solution)/shard_map/ppermute | solution.py:25
  76.6 6.7 %collective-permute-start.12 = (f32[256,128]{1,0:T(8,128)S(1)}, f32[256,128]{1,0:T(8,128)S(1)}, u32[]{:S(2)}, u32[]{:S(2)}) collective-permute-start(f32[256,128]{1,0:T(8,128)S(1)} %upper_maps_3.1), channel_id=1, source_target_pairs={{0,8},{1,9},{2,10},{3,11},{4,12},{5,13},{6,14},{7,15},{8,0},{9,1},... | collective-permute-start | bytes 393224 | tf_op jit(solution)/shard_map/ppermute | solution.py:25
  78.3 7.7 %collective-permute-start.13 = (f32[256,128]{1,0:T(8,128)S(1)}, f32[256,128]{1,0:T(8,128)S(1)}, u32[]{:S(2)}, u32[]{:S(2)}) collective-permute-start(f32[256,128]{1,0:T(8,128)S(1)} %get-tuple-element.59), channel_id=1, source_target_pairs={{0,16},{1,17},{2,18},{3,19},{4,20},{5,21},{6,22},{7,23},{8,24},{9,... | collective-permute-start | bytes 393224 | tf_op jit(solution)/shard_map/ppermute | solution.py:25
  86.0 7.7 %collective-permute-start.14 = (f32[256,128]{1,0:T(8,128)S(1)}, f32[256,128]{1,0:T(8,128)S(1)}, u32[]{:S(2)}, u32[]{:S(2)}) collective-permute-start(f32[256,128]{1,0:T(8,128)S(1)} %add.11.own_ref), channel_id=1, source_target_pairs={{0,16},{1,17},{2,18},{3,19},{4,20},{5,21},{6,22},{7,23},{8,24},{9,... | collective-permute-start | bytes 393224 | tf_op jit(solution)/shard_map/ppermute | solution.py:25
  93.7 8.6 %copy-start.8 = (f32[5,128,128]{2,1,0:T(8,128)}, f32[5,128,128]{2,1,0:T(8,128)S(1)}, u32[]{:S(2)}) copy-start(f32[5,128,128]{2,1,0:T(8,128)S(1)} %get-tuple-element.68) | copy-start | bytes 983044
  94.3 5.5 %copy-start.3 = (f32[128,128]{1,0:T(8,128)}, f32[128,128]{1,0:T(8,128)S(1)}, u32[]{:S(2)}) copy-start(f32[128,128]{1,0:T(8,128)S(1)} %top_sample.1.refs_0_) | copy-start | bytes 196612
  94.3 1.9 %collective-permute-start.15 = (f32[128,128]{1,0:T(8,128)S(1)}, f32[128,128]{1,0:T(8,128)S(1)}, u32[]{:S(2)}, u32[]{:S(2)}) collective-permute-start(f32[128,128]{1,0:T(8,128)S(1)} %top_sample.1.refs_0_), channel_id=1, source_target_pairs={{0,1},{1,0},{2,3},{3,2},{4,5},{5,4},{6,7},{7,6},{8,9},{9,8},{10,11... | collective-permute-start | bytes 196616 | tf_op jit(solution)/shard_map/ppermute | solution.py:25
  94.4 5.0 %collective-permute-start.16 = (f32[128,128]{1,0:T(8,128)S(1)}, f32[128,128]{1,0:T(8,128)S(1)}, u32[]{:S(2)}, u32[]{:S(2)}) collective-permute-start(f32[128,128]{1,0:T(8,128)S(1)} %top_sample.1.refs_0_), channel_id=1, source_target_pairs={{0,2},{1,3},{2,0},{3,1},{4,6},{5,7},{6,4},{7,5},{8,10},{9,11},{10,... | collective-permute-start | bytes 196616 | tf_op jit(solution)/shard_map/ppermute | solution.py:25
  94.9 5.0 %collective-permute-start.17 = (f32[128,128]{1,0:T(8,128)S(1)}, f32[128,128]{1,0:T(8,128)S(1)}, u32[]{:S(2)}, u32[]{:S(2)}) collective-permute-start(f32[128,128]{1,0:T(8,128)S(1)} %top_sample.1.refs_0_), channel_id=1, source_target_pairs={{0,3},{1,2},{2,1},{3,0},{4,7},{5,6},{6,5},{7,4},{8,11},{9,10},{10,... | collective-permute-start | bytes 196616 | tf_op jit(solution)/shard_map/ppermute | solution.py:25
  96.2 3.6 %copy-start.5 = (f32[128,128]{1,0:T(8,128)}, f32[128,128]{1,0:T(8,128)S(1)}, u32[]{:S(2)}) copy-start(f32[128,128]{1,0:T(8,128)S(1)} %collective-permute-done.15.refs_1_) | copy-start | bytes 196612
  99.3 0.6 copy-start.6
  100.0 0.6 copy-start.7

commit v4 on v3

--- a/solution.py
+++ b/solution.py
@@ -70,36 +70,46 @@
         inside = (lane >= first) & (lane < after)
         full = jnp.where(inside, jnp.where(lane - first == sub, 1.0, 0.0), rows[b])
         done = jnp.zeros(shape, jnp.float32)
+        steps = []
         if more:
             under = along_lanes(rows[b + 1], first)
             right = along_lanes(rows[b], after)
             corner = along_lanes(rows[b + 1], after)
+            below_row = jnp.where(inside, 0.0, rows[b + 1])
         for i in range(high):
             root = lax.rsqrt(along_rows(here[i], i))
             inverse = root * root
             below = jnp.where(sub > i, here[i], 0.0)
             scaled = below * inverse
-            if more:
-                low = under[i] * inverse
-            for k in range(i + 1, high):
-                x = along_rows(here[k], i)
+            entries = {k: along_rows(here[k], i) for k in range(i + 1, high)}
+            for k, x in entries.items():
                 here[k] = here[k] - ((below * x) * inverse if k < i + 3 else scaled * x)
-                if more:
-                    under[k] = under[k] - low * x
-            if more:
-                for k in range(high):
-                    x = along_rows(right[k], i)
-                    right[k] = right[k] - scaled * x
-                    corner[k] = corner[k] - low * x
             x = along_rows(full, i)
             done = jnp.where(sub == i, x * root, done)
             full = full - scaled * x
+            if not more:
+                continue
+            steps.append(({k: entry * inverse for k, entry in entries.items()}, x * inverse))
+            low = under[i] * inverse
+            for k, entry in entries.items():
+                under[k] = under[k] - low * entry
+            for k in range(high):
+                entry = along_rows(right[k], i)
+                right[k] = right[k] - scaled * entry
+                corner[k] = corner[k] - low * entry
+            below_row = below_row - low * x
         found.append(jnp.where(lane < after, done, 0.0))
         if not more:
             break
-        change = dot(done.T, done)
-        for g in range(b + 1, count):
-            rows[g] = jnp.where(inside, 0.0, rows[g]) - change[high * g : high * g + high]
+        rows[b + 1] = below_row
+        for g in range(b + 2, count):
+            columns = along_lanes(rows[g], first)
+            row = jnp.where(inside, 0.0, rows[g])
+            for i, (entries, x) in enumerate(steps):
+                for k, entry in entries.items():
+                    columns[k] = columns[k] - columns[i] * entry
+                row = row - columns[i] * x
+            rows[g] = row
         here = corner
     return jnp.concatenate(found, axis=0)
 

time: 103 us -> 91.3 us (0.89)
  Pallas kernels: 52.1 us -> 41.2 us
  other arithmetic: 6.71 us -> 4.51 us
  waiting for transfers between devices: 21.7 us -> 23.5 us
    pallas_call x4, Pallas kernels: 27.5 us -> 18.2 us  [merge_step(): pl.pallas_call(functools.partial(merge_body, tree_level), grid=(1,), out_...]
    pallas_call x1, other arithmetic: 6.6 us -> 4.4 us  [merge_step(): pl.pallas_call(functools.partial(merge_body, tree_level), grid=(1,), out_...]
    ppermute x18, waiting for transfers between devices: 21.7 us -> 23.5 us  [from_partner(): return lax.ppermute(block, axis, route)]
    pallas_call x1, Pallas kernels: 7.19 us -> 5.56 us  [leaf_step(): pl.pallas_call(leaf_body, grid=(1,), out_shape=[jax.ShapeDtypeStruct((lea...]
  transfers between devices with their start and end apart: 18 -> 18, of which waited for: 9 -> 10; matrix products, arithmetic and copies ran while one was open for 7% -> 5% of each run, Pallas kernels for 30% -> 24%
where the time goes in v4:
time: 91.3 us; the launch traced here: 91.1 us
  Pallas kernels  41.2 us (45%)
  waiting for transfers between devices  23.5 us (26%)
  starting transfers between devices  19.3 us (21%)
  other arithmetic  4.51 us (5%)
  local copies, waits for them, and re-layouts  1.51 us (2%)
  between operations  1.03 us (1%)
    ppermute x18, waiting for transfers between devices, from_partner(): return lax.ppermute(block, axis, route)  23.5 us
    ppermute x18, starting transfers between devices, from_partner(): return lax.ppermute(block, axis, route)  19.3 us
    pallas_call x4, Pallas kernels, merge_step(): pl.pallas_call(functools.partial(merge_body, tree_level), grid=(1,), out_...  18.2 us
    pallas_call x1, Pallas kernels, sample_rows(): pl.pallas_call(functools.partial(spmm_body, leaves=leaves), out_shape=[ja...  11.2 us
    pallas_call x1, Pallas kernels, leaf_step(): pl.pallas_call(leaf_body, grid=(1,), out_shape=[jax.ShapeDtypeStruct((lea...  5.56 us
    pallas_call x1, other arithmetic, merge_step(): pl.pallas_call(functools.partial(merge_body, tree_level), grid=(1,), out_...  4.4 us
  transfers between devices with their start and end apart: 18, of which 10 were waited for; matrix products, arithmetic and copies ran while one was open for 5% of the time, Pallas kernels for 24%

profile of v4, /device:TPU:0, one launch (start us, length us, event | category | flops | bytes accessed | tf_op | source)
XLA Modules:
  0.0 91.1 jit_solution(14300591035879265678)
XLA Ops:
  0.6 0.0 copy-start.2
  0.6 0.0 copy-start.1
  0.7 0.0 copy-start.4
  0.7 0.7 copy-done.4
  1.4 11.2 %spmm.1 = (f32[512,512]{1,0:T(8,128)S(1)}, f32[512,512]{1,0:T(8,128)S(1)}) custom-call(s32[168]{0:T(256)S(1)} %copy-done.4, bf16[168,128,128]{2,1,0:T(8,128)(2,1)} %tiles_ref.1, bf16[6144,512]{1,0:T(8,128)(2,1)} %sketch_ref.1), custom_call_target="tpu_custom_call" | custom-call | flops 6442450944 | bytes 13893632 | tf_op jit(solution)/shard_map/spmm/pallas_call | solution.py:215
  12.6 0.0 copy-start
  12.6 0.0 copy-done.2
  12.6 0.7 reduced_1.1
  13.3 0.5 collective-permute-start
  13.9 0.0 copy-done.1
  13.9 0.9 reduced_2.1
  14.7 0.3 collective-permute-done.first_ref
  15.0 0.4 collective-permute-start.1
  15.5 2.7 %collective-permute-start.2 = (f32[256,128]{1,0:T(8,128)S(1)}, f32[256,128]{1,0:T(8,128)S(1)}, u32[]{:S(2)}, u32[]{:S(2)}) collective-permute-start(f32[256,128]{1,0:T(8,128)S(1)} %slice_add_fusion.1), channel_id=1, source_target_pairs={{0,2},{1,3},{2,0},{3,1},{4,6},{5,7},{6,4},{7,5},{8,10},{9,11},{10,... | collective-permute-start | bytes 393224 | tf_op jit(solution)/shard_map/ppermute | solution.py:25
  18.1 0.0 collective-permute-done.1.refs_1_
  18.1 0.1 slice_add_fusion._
  18.2 3.9 %collective-permute-done.2.second_ref = f32[256,128]{1,0:T(8,128)S(1)} collective-permute-done((f32[256,128]{1,0:T(8,128)S(1)}, f32[256,128]{1,0:T(8,128)S(1)}, u32[]{:S(2)}, u32[]{:S(2)}) %collective-permute-start.2) | collective-permute-done | bytes 131104 | tf_op jit(solution)/shard_map/ppermute | solution.py:25
  22.2 1.7 %collective-permute-start.5 = (f32[256,512]{1,0:T(8,128)S(1)}, f32[256,512]{1,0:T(8,128)S(1)}, u32[]{:S(2)}, u32[]{:S(2)}) collective-permute-start(f32[256,512]{1,0:T(8,128)S(1)} %slice_add_fusion._), channel_id=1, source_target_pairs={{0,2},{1,3},{2,0},{3,1},{4,6},{5,7},{6,4},{7,5},{8,10},{9,11},{10,... | collective-permute-start | bytes 1572872 | tf_op jit(solution)/shard_map/ppermute | solution.py:25
  23.9 5.6 %leaf_orth.1 = (f32[256,128]{1,0:T(8,128)}, f32[128,256]{1,0:T(8,128)S(1)}, f32[256,128]{1,0:T(8,128)S(1)}) custom-call(f32[512,128]{1,0:T(8,128)S(1)} %get-tuple-element.35.keep_ref, f32[512,128]{1,0:T(8,128)S(1)} %collective-permute-done.first_ref, f32[256,128]{1,0:T(8,128)S(1)} %collective-permute-done.2.second_ref, ...), custom_call_target="tpu_custom_call" | custom-call | flops 80000000 | bytes 240000 | tf_op jit(solution)/shard_map/leaf_orth/pallas_call | solution.py:292
  29.5 0.0 collective-permute-start.3
  29.5 1.3 %collective-permute-done.3.refs_1_ = f32[256,128]{1,0:T(8,128)S(1)} collective-permute-done((f32[256,128]{1,0:T(8,128)S(1)}, f32[256,128]{1,0:T(8,128)S(1)}, u32[]{:S(2)}, u32[]{:S(2)}) %collective-permute-start.3) | collective-permute-done | bytes 131104 | tf_op jit(solution)/shard_map/ppermute | solution.py:25
  30.8 0.0 copy-done
  30.8 4.6 %merge_orth_0.1 = (f32[128,128]{1,0:T(8,128)S(1)}, f32[2,128,128]{2,1,0:T(8,128)S(1)}, f32[256,128]{1,0:T(8,128)S(1)}) custom-call(f32[256,128]{1,0:T(8,128)S(1)} %get-tuple-element.43.refs_0_, f32[256,128]{1,0:T(8,128)S(1)} %collective-permute-done.3.refs_1_, bf16[1,5,128,128]{3,2,1,0:T(8,128)(2,1)S(1)} %copy-done), custom_call_target="tpu_custom_call" | custom-call | flops 80000000 | bytes 240000 | tf_op jit(solution)/shard_map/merge_orth_0/pallas_call | solution.py:355
  35.4 0.3 collective-permute-start.4
  35.8 5.3 %collective-permute-done.4.refs_1_ = f32[256,128]{1,0:T(8,128)S(1)} collective-permute-done((f32[256,128]{1,0:T(8,128)S(1)}, f32[256,128]{1,0:T(8,128)S(1)}, u32[]{:S(2)}, u32[]{:S(2)}) %collective-permute-start.4) | collective-permute-done | bytes 131104 | tf_op jit(solution)/shard_map/ppermute | solution.py:25
  41.1 0.0 collective-permute-done.5.refs_3_.refs_2_
  41.1 4.4 %merge_orth_1.1 = (f32[128,128]{1,0:T(8,128)S(1)}, f32[2,128,128]{2,1,0:T(8,128)S(1)}, f32[256,128]{1,0:T(8,128)S(1)}) custom-call(f32[256,128]{1,0:T(8,128)S(1)} %get-tuple-element.45.refs_0_, f32[256,128]{1,0:T(8,128)S(1)} %collective-permute-done.4.refs_1_, bf16[1,5,128,128]{3,2,1,0:T(8,128)(2,1)S(1)} %copy-done, ...), custom_call_target="tpu_custom_call" | custom-call | flops 80000000 | bytes 240000 | tf_op jit(solution)/shard_map/merge_orth_1/pallas_call | solution.py:355
  45.5 1.6 %collective-permute-start.6 = (f32[256,128]{1,0:T(8,128)S(1)}, f32[256,128]{1,0:T(8,128)S(1)}, u32[]{:S(2)}, u32[]{:S(2)}) collective-permute-start(f32[256,128]{1,0:T(8,128)S(1)} %get-tuple-element.47.refs_0_), channel_id=1, source_target_pairs={{0,4},{1,5},{2,6},{3,7},{4,0},{5,1},{6,2},{7,3},{8,12},{9,13},{10,... | collective-permute-start | bytes 393224 | tf_op jit(solution)/shard_map/ppermute | solution.py:25
  47.1 1.8 %lower_maps.1 = (f32[256,128]{1,0:T(8,128)S(1)}, f32[256,128]{1,0:T(8,128)S(1)}, f32[256,128]{1,0:T(8,128)S(1)}, f32[256,128]{1,0:T(8,128)S(1)}) custom-call(f32[512,512]{1,0:T(8,128)S(1)} %get-tuple-element.34.refs_1_.refs_0_, f32[512,512]{1,0:T(8,128)S(1)} %collective-permute-done.1.refs_1_, f32[256,512]{1,0:T(8,128)S(1)} %collective-permute-done.5.refs_3_.refs_2_, ...), custom_call_target="tpu_custom_call" | custom-call | flops 20000000 | bytes 60000 | tf_op jit(solution)/shard_map/lower_maps/pallas_call | solution.py:399
  48.9 0.1 collective-permute-start.10
  49.0 0.6 collective-permute-start.8
  49.6 1.5 %collective-permute-start.9 = (f32[256,128]{1,0:T(8,128)S(1)}, f32[256,128]{1,0:T(8,128)S(1)}, u32[]{:S(2)}, u32[]{:S(2)}) collective-permute-start(f32[256,128]{1,0:T(8,128)S(1)} %get-tuple-element.55), channel_id=1, source_target_pairs={{0,2},{1,3},{2,0},{3,1},{4,6},{5,7},{6,4},{7,5},{8,10},{9,11},{10,... | collective-permute-start | bytes 393224 | tf_op jit(solution)/shard_map/ppermute | solution.py:25
  51.1 0.0 collective-permute-done.6.refs_1_
  51.1 4.4 %merge_orth_2.1 = (f32[128,128]{1,0:T(8,128)S(1)}, f32[2,128,128]{2,1,0:T(8,128)S(1)}, f32[256,128]{1,0:T(8,128)S(1)}) custom-call(f32[256,128]{1,0:T(8,128)S(1)} %get-tuple-element.47.refs_0_, f32[256,128]{1,0:T(8,128)S(1)} %collective-permute-done.6.refs_1_, bf16[1,5,128,128]{3,2,1,0:T(8,128)(2,1)S(1)} %copy-done, ...), custom_call_target="tpu_custom_call" | custom-call | flops 80000000 | bytes 240000 | tf_op jit(solution)/shard_map/merge_orth_2/pallas_call | solution.py:355
  55.5 1.6 %collective-permute-start.7 = (f32[256,128]{1,0:T(8,128)S(1)}, f32[256,128]{1,0:T(8,128)S(1)}, u32[]{:S(2)}, u32[]{:S(2)}) collective-permute-start(f32[256,128]{1,0:T(8,128)S(1)} %get-tuple-element.53.refs_0_), channel_id=1, source_target_pairs={{0,8},{1,9},{2,10},{3,11},{4,12},{5,13},{6,14},{7,15},{8,0},{9,1},... | collective-permute-start | bytes 393224 | tf_op jit(solution)/shard_map/ppermute | solution.py:25
  57.2 0.0 collective-permute-done.10.refs_3_
  57.2 0.0 collective-permute-done.8.refs_1_
  57.2 0.0 collective-permute-done.9.refs_2_
  57.2 0.3 upper_maps_2.1.refs_3_.refs_0_
  57.5 1.0 %collective-permute-start.11 = (f32[256,128]{1,0:T(8,128)S(1)}, f32[256,128]{1,0:T(8,128)S(1)}, u32[]{:S(2)}, u32[]{:S(2)}) collective-permute-start(f32[256,128]{1,0:T(8,128)S(1)} %upper_maps_2.1.refs_3_.refs_0_), channel_id=1, source_target_pairs={{0,4},{1,5},{2,6},{3,7},{4,0},{5,1},{6,2},{7,3},{8,12},{9,13},{10,... | collective-permute-start | bytes 393224 | tf_op jit(solution)/shard_map/ppermute | solution.py:25
  58.5 2.2 %collective-permute-done.7.refs_1_ = f32[256,128]{1,0:T(8,128)S(1)} collective-permute-done((f32[256,128]{1,0:T(8,128)S(1)}, f32[256,128]{1,0:T(8,128)S(1)}, u32[]{:S(2)}, u32[]{:S(2)}) %collective-permute-start.7) | collective-permute-done | bytes 131104 | tf_op jit(solution)/shard_map/ppermute | solution.py:25
  60.7 4.7 %merge_orth_3.1 = (f32[128,128]{1,0:T(8,128)S(1)}, f32[2,128,128]{2,1,0:T(8,128)S(1)}, f32[256,128]{1,0:T(8,128)S(1)}) custom-call(f32[256,128]{1,0:T(8,128)S(1)} %get-tuple-element.53.refs_0_, f32[256,128]{1,0:T(8,128)S(1)} %collective-permute-done.7.refs_1_, bf16[1,5,128,128]{3,2,1,0:T(8,128)(2,1)S(1)} %copy-done, f32[256,128]{1,0:T(8,128)S(1)} %upper_maps_2.1.refs_3_.refs_0_), custom_call_target="tpu_custom_call" | custom-call | flops 80000000 | bytes 240000 | tf_op jit(solution)/shard_map/merge_orth_3/pallas_call | solution.py:355
  65.4 0.0 collective-permute-done.11.refs_1_
  65.4 0.3 upper_maps_3.1
  65.7 1.6 %collective-permute-start.12 = (f32[256,128]{1,0:T(8,128)S(1)}, f32[256,128]{1,0:T(8,128)S(1)}, u32[]{:S(2)}, u32[]{:S(2)}) collective-permute-start(f32[256,128]{1,0:T(8,128)S(1)} %upper_maps_3.1), channel_id=1, source_target_pairs={{0,8},{1,9},{2,10},{3,11},{4,12},{5,13},{6,14},{7,15},{8,0},{9,1},... | collective-permute-start | bytes 393224 | tf_op jit(solution)/shard_map/ppermute | solution.py:25
  67.4 2.6 %collective-permute-start.13 = (f32[256,128]{1,0:T(8,128)S(1)}, f32[256,128]{1,0:T(8,128)S(1)}, u32[]{:S(2)}, u32[]{:S(2)}) collective-permute-start(f32[256,128]{1,0:T(8,128)S(1)} %get-tuple-element.59), channel_id=1, source_target_pairs={{0,16},{1,17},{2,18},{3,19},{4,20},{5,21},{6,22},{7,23},{8,24},{9,... | collective-permute-start | bytes 393224 | tf_op jit(solution)/shard_map/ppermute | solution.py:25
  70.0 2.5 %collective-permute-done.12 = f32[256,128]{1,0:T(8,128)S(1)} collective-permute-done((f32[256,128]{1,0:T(8,128)S(1)}, f32[256,128]{1,0:T(8,128)S(1)}, u32[]{:S(2)}, u32[]{:S(2)}) %collective-permute-start.12) | collective-permute-done | bytes 131104 | tf_op jit(solution)/shard_map/ppermute | solution.py:25
  72.5 2.6 %collective-permute-done.13 = f32[256,128]{1,0:T(8,128)S(1)} collective-permute-done((f32[256,128]{1,0:T(8,128)S(1)}, f32[256,128]{1,0:T(8,128)S(1)}, u32[]{:S(2)}, u32[]{:S(2)}) %collective-permute-start.13) | collective-permute-done | bytes 131104 | tf_op jit(solution)/shard_map/ppermute | solution.py:25
  75.1 1.1 %collective-permute-start.14 = (f32[256,128]{1,0:T(8,128)S(1)}, f32[256,128]{1,0:T(8,128)S(1)}, u32[]{:S(2)}, u32[]{:S(2)}) collective-permute-start(f32[256,128]{1,0:T(8,128)S(1)} %add.11.own_ref), channel_id=1, source_target_pairs={{0,16},{1,17},{2,18},{3,19},{4,20},{5,21},{6,22},{7,23},{8,24},{9,... | collective-permute-start | bytes 393224 | tf_op jit(solution)/shard_map/ppermute | solution.py:25
  76.2 4.4 %merge_orth_4.1 = (f32[5,128,128]{2,1,0:T(8,128)S(1)}, f32[128,256]{1,0:T(8,128)S(1)}, f32[8,128]{1,0:T(8,128)}) fusion(f32[5,128,128]{2,1,0:T(8,128)S(1)} %bitcast_dynamic-update-slice_fusion.1, f32[256,128]{1,0:T(8,128)S(1)} %get-tuple-element.59, f32[256,128]{1,0:T(8,128)S(1)} %collective-permute-done.13, bf16[1,5,128,128]{3,2,1,0:T(8,128)(2,1)S(1)} %copy-done, ...), kind=kCustom, calls=%fused_computation.2 | custom fusion | flops 80000000 | bytes 757760 | tf_op jit(solution)/shard_map/merge_orth_4/pallas_call | solution.py:355
  80.6 0.0 copy-start.8
  80.6 1.8 %collective-permute-done.14.other_ref = f32[256,128]{1,0:T(8,128)S(1)} collective-permute-done((f32[256,128]{1,0:T(8,128)S(1)}, f32[256,128]{1,0:T(8,128)S(1)}, u32[]{:S(2)}, u32[]{:S(2)}) %collective-permute-start.14) | collective-permute-done | bytes 131104 | tf_op jit(solution)/shard_map/ppermute | solution.py:25
  82.4 0.6 top_sample.1.refs_0_
  83.0 0.0 copy-start.3
  83.0 0.1 collective-permute-start.15
  83.1 0.6 collective-permute-start.16
  83.6 1.3 %collective-permute-start.17 = (f32[128,128]{1,0:T(8,128)S(1)}, f32[128,128]{1,0:T(8,128)S(1)}, u32[]{:S(2)}, u32[]{:S(2)}) collective-permute-start(f32[128,128]{1,0:T(8,128)S(1)} %top_sample.1.refs_0_), channel_id=1, source_target_pairs={{0,3},{1,2},{2,1},{3,0},{4,7},{5,6},{6,5},{7,4},{8,11},{9,10},{10,... | collective-permute-start | bytes 196616 | tf_op jit(solution)/shard_map/ppermute | solution.py:25
  84.9 0.0 collective-permute-done.15.refs_1_
  84.9 3.1 %collective-permute-done.16.refs_2_ = f32[128,128]{1,0:T(8,128)S(1)} collective-permute-done((f32[128,128]{1,0:T(8,128)S(1)}, f32[128,128]{1,0:T(8,128)S(1)}, u32[]{:S(2)}, u32[]{:S(2)}) %collective-permute-start.16) | collective-permute-done | bytes 65568 | tf_op jit(solution)/shard_map/ppermute | solution.py:25
  88.0 0.5 collective-permute-done.17.refs_3_
  88.5 0.0 copy-done.3
  88.5 0.1 copy-done.6
  88.6 0.6 copy-done.7
  89.2 1.7 %top_columns.1 = f32[1,128,512]{2,1,0:T(8,128)} custom-call(f32[128,128]{1,0:T(8,128)} %copy-done.3, f32[128,128]{1,0:T(8,128)} %copy-done.5, f32[128,128]{1,0:T(8,128)} %copy-done.6, f32[128,128]{1,0:T(8,128)} %copy-done.7), custom_call_target="tpu_custom_call" | custom-call | tf_op jit(solution)/shard_map/top_columns/pallas_call | solution.py:481
  (11 shorter events, 0.1 us)
Async XLA Ops:
  0.6 12.0 %copy-start.2 = (f32[512,128]{1,0:T(8,128)S(1)}, f32[512,128]{1,0:T(8,128)}, u32[]{:S(2)}) copy-start(f32[512,128]{1,0:T(8,128)} %refs_0_.3) | copy-start | bytes 786436
  0.6 13.2 %copy-start.1 = (bf16[256,512]{1,0:T(8,128)(2,1)S(1)}, bf16[256,512]{1,0:T(8,128)(2,1)}, u32[]{:S(2)}) copy-start(bf16[256,512]{1,0:T(8,128)(2,1)} %refs_3_.1) | copy-start | bytes 786436
  0.7 0.7 copy-start.4
  12.6 18.2 %copy-start = (bf16[1,5,128,128]{3,2,1,0:T(8,128)(2,1)S(1)}, bf16[1,5,128,128]{3,2,1,0:T(8,128)(2,1)}, u32[]{:S(2)}) copy-start(bf16[1,5,128,128]{3,2,1,0:T(8,128)(2,1)} %coupling_ref.1) | copy-start | bytes 491524
  13.3 1.7 %collective-permute-start = (f32[512,128]{1,0:T(8,128)S(1)}, f32[512,128]{1,0:T(8,128)S(1)}, u32[]{:S(2)}, u32[]{:S(2)}) collective-permute-start(f32[512,128]{1,0:T(8,128)S(1)} %reduced_1.1), channel_id=1, source_target_pairs={{0,1},{1,0},{2,3},{3,2},{4,5},{5,4},{6,7},{7,6},{8,9},{9,8},{10,11... | collective-permute-start | bytes 786440 | tf_op jit(solution)/shard_map/ppermute | solution.py:25
  15.0 3.1 %collective-permute-start.1 = (f32[512,512]{1,0:T(8,128)S(1)}, f32[512,512]{1,0:T(8,128)S(1)}, u32[]{:S(2)}, u32[]{:S(2)}) collective-permute-start(f32[512,512]{1,0:T(8,128)S(1)} %get-tuple-element.37.refs_1_), channel_id=1, source_target_pairs={{0,1},{1,0},{2,3},{3,2},{4,5},{5,4},{6,7},{7,6},{8,9},{9,8},{10,11... | collective-permute-start | bytes 3145736 | tf_op jit(solution)/shard_map/ppermute | solution.py:25
  15.5 6.7 %collective-permute-start.2 = (f32[256,128]{1,0:T(8,128)S(1)}, f32[256,128]{1,0:T(8,128)S(1)}, u32[]{:S(2)}, u32[]{:S(2)}) collective-permute-start(f32[256,128]{1,0:T(8,128)S(1)} %slice_add_fusion.1), channel_id=1, source_target_pairs={{0,2},{1,3},{2,0},{3,1},{4,6},{5,7},{6,4},{7,5},{8,10},{9,11},{10,... | collective-permute-start | bytes 393224 | tf_op jit(solution)/shard_map/ppermute | solution.py:25
  22.2 18.9 %collective-permute-start.5 = (f32[256,512]{1,0:T(8,128)S(1)}, f32[256,512]{1,0:T(8,128)S(1)}, u32[]{:S(2)}, u32[]{:S(2)}) collective-permute-start(f32[256,512]{1,0:T(8,128)S(1)} %slice_add_fusion._), channel_id=1, source_target_pairs={{0,2},{1,3},{2,0},{3,1},{4,6},{5,7},{6,4},{7,5},{8,10},{9,11},{10,... | collective-permute-start | bytes 1572872 | tf_op jit(solution)/shard_map/ppermute | solution.py:25
  29.5 1.3 %collective-permute-start.3 = (f32[256,128]{1,0:T(8,128)S(1)}, f32[256,128]{1,0:T(8,128)S(1)}, u32[]{:S(2)}, u32[]{:S(2)}) collective-permute-start(f32[256,128]{1,0:T(8,128)S(1)} %get-tuple-element.43.refs_0_), channel_id=1, source_target_pairs={{0,1},{1,0},{2,3},{3,2},{4,5},{5,4},{6,7},{7,6},{8,9},{9,8},{10,11... | collective-permute-start | bytes 393224 | tf_op jit(solution)/shard_map/ppermute | solution.py:25
  35.4 5.6 %collective-permute-start.4 = (f32[256,128]{1,0:T(8,128)S(1)}, f32[256,128]{1,0:T(8,128)S(1)}, u32[]{:S(2)}, u32[]{:S(2)}) collective-permute-start(f32[256,128]{1,0:T(8,128)S(1)} %get-tuple-element.45.refs_0_), channel_id=1, source_target_pairs={{0,2},{1,3},{2,0},{3,1},{4,6},{5,7},{6,4},{7,5},{8,10},{9,11},{10,... | collective-permute-start | bytes 393224 | tf_op jit(solution)/shard_map/ppermute | solution.py:25
  45.5 5.6 %collective-permute-start.6 = (f32[256,128]{1,0:T(8,128)S(1)}, f32[256,128]{1,0:T(8,128)S(1)}, u32[]{:S(2)}, u32[]{:S(2)}) collective-permute-start(f32[256,128]{1,0:T(8,128)S(1)} %get-tuple-element.47.refs_0_), channel_id=1, source_target_pairs={{0,4},{1,5},{2,6},{3,7},{4,0},{5,1},{6,2},{7,3},{8,12},{9,13},{10,... | collective-permute-start | bytes 393224 | tf_op jit(solution)/shard_map/ppermute | solution.py:25
  48.9 8.3 %collective-permute-start.10 = (f32[256,128]{1,0:T(8,128)S(1)}, f32[256,128]{1,0:T(8,128)S(1)}, u32[]{:S(2)}, u32[]{:S(2)}) collective-permute-start(f32[256,128]{1,0:T(8,128)S(1)} %get-tuple-element.56), channel_id=1, source_target_pairs={{0,3},{1,2},{2,1},{3,0},{4,7},{5,6},{6,5},{7,4},{8,11},{9,10},{10,... | collective-permute-start | bytes 393224 | tf_op jit(solution)/shard_map/ppermute | solution.py:25
  49.0 8.2 %collective-permute-start.8 = (f32[256,128]{1,0:T(8,128)S(1)}, f32[256,128]{1,0:T(8,128)S(1)}, u32[]{:S(2)}, u32[]{:S(2)}) collective-permute-start(f32[256,128]{1,0:T(8,128)S(1)} %get-tuple-element.54), channel_id=1, source_target_pairs={{0,1},{1,0},{2,3},{3,2},{4,5},{5,4},{6,7},{7,6},{8,9},{9,8},{10,11... | collective-permute-start | bytes 393224 | tf_op jit(solution)/shard_map/ppermute | solution.py:25
  49.6 7.6 %collective-permute-start.9 = (f32[256,128]{1,0:T(8,128)S(1)}, f32[256,128]{1,0:T(8,128)S(1)}, u32[]{:S(2)}, u32[]{:S(2)}) collective-permute-start(f32[256,128]{1,0:T(8,128)S(1)} %get-tuple-element.55), channel_id=1, source_target_pairs={{0,2},{1,3},{2,0},{3,1},{4,6},{5,7},{6,4},{7,5},{8,10},{9,11},{10,... | collective-permute-start | bytes 393224 | tf_op jit(solution)/shard_map/ppermute | solution.py:25
  55.5 5.2 %collective-permute-start.7 = (f32[256,128]{1,0:T(8,128)S(1)}, f32[256,128]{1,0:T(8,128)S(1)}, u32[]{:S(2)}, u32[]{:S(2)}) collective-permute-start(f32[256,128]{1,0:T(8,128)S(1)} %get-tuple-element.53.refs_0_), channel_id=1, source_target_pairs={{0,8},{1,9},{2,10},{3,11},{4,12},{5,13},{6,14},{7,15},{8,0},{9,1},... | collective-permute-start | bytes 393224 | tf_op jit(solution)/shard_map/ppermute | solution.py:25
  57.5 7.9 %collective-permute-start.11 = (f32[256,128]{1,0:T(8,128)S(1)}, f32[256,128]{1,0:T(8,128)S(1)}, u32[]{:S(2)}, u32[]{:S(2)}) collective-permute-start(f32[256,128]{1,0:T(8,128)S(1)} %upper_maps_2.1.refs_3_.refs_0_), channel_id=1, source_target_pairs={{0,4},{1,5},{2,6},{3,7},{4,0},{5,1},{6,2},{7,3},{8,12},{9,13},{10,... | collective-permute-start | bytes 393224 | tf_op jit(solution)/shard_map/ppermute | solution.py:25
  65.7 6.7 %collective-permute-start.12 = (f32[256,128]{1,0:T(8,128)S(1)}, f32[256,128]{1,0:T(8,128)S(1)}, u32[]{:S(2)}, u32[]{:S(2)}) collective-permute-start(f32[256,128]{1,0:T(8,128)S(1)} %upper_maps_3.1), channel_id=1, source_target_pairs={{0,8},{1,9},{2,10},{3,11},{4,12},{5,13},{6,14},{7,15},{8,0},{9,1},... | collective-permute-start | bytes 393224 | tf_op jit(solution)/shard_map/ppermute | solution.py:25
  67.4 7.7 %collective-permute-start.13 = (f32[256,128]{1,0:T(8,128)S(1)}, f32[256,128]{1,0:T(8,128)S(1)}, u32[]{:S(2)}, u32[]{:S(2)}) collective-permute-start(f32[256,128]{1,0:T(8,128)S(1)} %get-tuple-element.59), channel_id=1, source_target_pairs={{0,16},{1,17},{2,18},{3,19},{4,20},{5,21},{6,22},{7,23},{8,24},{9,... | collective-permute-start | bytes 393224 | tf_op jit(solution)/shard_map/ppermute | solution.py:25
  75.1 7.3 %collective-permute-start.14 = (f32[256,128]{1,0:T(8,128)S(1)}, f32[256,128]{1,0:T(8,128)S(1)}, u32[]{:S(2)}, u32[]{:S(2)}) collective-permute-start(f32[256,128]{1,0:T(8,128)S(1)} %add.11.own_ref), channel_id=1, source_target_pairs={{0,16},{1,17},{2,18},{3,19},{4,20},{5,21},{6,22},{7,23},{8,24},{9,... | collective-permute-start | bytes 393224 | tf_op jit(solution)/shard_map/ppermute | solution.py:25
  80.6 10.3 %copy-start.8 = (f32[5,128,128]{2,1,0:T(8,128)}, f32[5,128,128]{2,1,0:T(8,128)S(1)}, u32[]{:S(2)}) copy-start(f32[5,128,128]{2,1,0:T(8,128)S(1)} %get-tuple-element.68) | copy-start | bytes 983044
  83.0 5.5 %copy-start.3 = (f32[128,128]{1,0:T(8,128)}, f32[128,128]{1,0:T(8,128)S(1)}, u32[]{:S(2)}) copy-start(f32[128,128]{1,0:T(8,128)S(1)} %top_sample.1.refs_0_) | copy-start | bytes 196612
  83.0 1.9 %collective-permute-start.15 = (f32[128,128]{1,0:T(8,128)S(1)}, f32[128,128]{1,0:T(8,128)S(1)}, u32[]{:S(2)}, u32[]{:S(2)}) collective-permute-start(f32[128,128]{1,0:T(8,128)S(1)} %top_sample.1.refs_0_), channel_id=1, source_target_pairs={{0,1},{1,0},{2,3},{3,2},{4,5},{5,4},{6,7},{7,6},{8,9},{9,8},{10,11... | collective-permute-start | bytes 196616 | tf_op jit(solution)/shard_map/ppermute | solution.py:25
  83.1 5.0 %collective-permute-start.16 = (f32[128,128]{1,0:T(8,128)S(1)}, f32[128,128]{1,0:T(8,128)S(1)}, u32[]{:S(2)}, u32[]{:S(2)}) collective-permute-start(f32[128,128]{1,0:T(8,128)S(1)} %top_sample.1.refs_0_), channel_id=1, source_target_pairs={{0,2},{1,3},{2,0},{3,1},{4,6},{5,7},{6,4},{7,5},{8,10},{9,11},{10,... | collective-permute-start | bytes 196616 | tf_op jit(solution)/shard_map/ppermute | solution.py:25
  83.6 4.9 %collective-permute-start.17 = (f32[128,128]{1,0:T(8,128)S(1)}, f32[128,128]{1,0:T(8,128)S(1)}, u32[]{:S(2)}, u32[]{:S(2)}) collective-permute-start(f32[128,128]{1,0:T(8,128)S(1)} %top_sample.1.refs_0_), channel_id=1, source_target_pairs={{0,3},{1,2},{2,1},{3,0},{4,7},{5,6},{6,5},{7,4},{8,11},{9,10},{10,... | collective-permute-start | bytes 196616 | tf_op jit(solution)/shard_map/ppermute | solution.py:25
  84.9 3.6 %copy-start.5 = (f32[128,128]{1,0:T(8,128)}, f32[128,128]{1,0:T(8,128)S(1)}, u32[]{:S(2)}) copy-start(f32[128,128]{1,0:T(8,128)S(1)} %collective-permute-done.15.refs_1_) | copy-start | bytes 196612
  88.0 0.6 copy-start.6
  88.6 0.6 copy-start.7

commit v5 on v4

--- a/solution.py
+++ b/solution.py
@@ -264,7 +264,7 @@
     )(subsketch, *blocks)
 
 
-def leaf_body(keep_ref, first_ref, second_ref, sketch_red_ref, _, basis_ref, basis_t_ref, pair_ref):
+def leaf_body(keep_ref, first_ref, second_ref, sketch_red_ref, _, basis_t_ref, pair_ref):
     rank = keep_ref.shape[-1]
     reduced = keep_ref[...] + first_ref[...] + second_ref[...]
     reduced_t = reduced.T
@@ -274,7 +274,6 @@
     pair_ref[:rank, :] = moved[:, :rank]
     pair_ref[rank:, :] = moved[:, rank : 2 * rank]
     basis_t_ref[...] = moved[:, 2 * rank :]
-    basis_ref[...] = dot_nt(reduced, inverse)
 
 
 def small_params():
@@ -293,34 +292,64 @@
         leaf_body,
         grid=(1,),
         out_shape=[
-            jax.ShapeDtypeStruct((leaf, rank), f32),
             jax.ShapeDtypeStruct((rank, leaf), f32),
             jax.ShapeDtypeStruct((2 * rank, rank), f32),
         ],
         in_specs=[part, part, VMEM, VMEM, ANY],
-        out_specs=[VMEM] * 3,
+        out_specs=[VMEM] * 2,
         compiler_params=small_params(),
         cost_estimate=small_cost(8),
         name="leaf_orth",
     )(keep, first, second, sketch_red, after)
 
 
+def basis_body(basis_t_ref, basis_ref, mark_ref):
+    basis_ref[...] = basis_t_ref[...].T
+    mark_ref[...] = jnp.zeros_like(mark_ref)
+
+
+def basis_step(basis_t):
+    return pl.pallas_call(
+        basis_body,
+        out_shape=[
+            jax.ShapeDtypeStruct(basis_t.shape[::-1], jnp.float32),
+            jax.ShapeDtypeStruct((8, 128), jnp.float32),
+        ],
+        in_specs=[VMEM],
+        out_specs=[VMEM] * 2,
+        compiler_params=small_params(),
+        cost_estimate=small_cost(1),
+        name="leaf_basis",
+    )(basis_t)
+
+
+def position():
+    return lax.axis_index("row") * lax.axis_size("col") + lax.axis_index("col")
+
+
 def turned(coupling_ref, tree_level):
-    position = lax.axis_index("row") * lax.axis_size("col") + lax.axis_index("col")
-    upper = position // 2**tree_level % 2 == 1
+    upper = position() // 2**tree_level % 2 == 1
     coupling = coupling_ref[0, 0].astype(jnp.float32)
     coupling_t = coupling.T
     return jnp.where(upper, coupling_t, coupling), jnp.where(upper, coupling, coupling_t)
 
 
 def merge_body(tree_level, *refs):
-    own_ref, other_ref, coupling_ref = refs[:3]
-    block_ref, maps_ref, pair_ref = refs[-3:]
     last = tree_level == LEVELS - 1
+    coupling_ref, own_ref, other_ref = refs[:3]
+    if tree_level == LEVELS - 2:
+        block_ref, maps_ref, pair_ref, half_ref = refs[-4:]
+    else:
+        block_ref, maps_ref, pair_ref = refs[-3:]
+    odd = position() % 2 == 1
     rank = own_ref.shape[-1]
     ahead, back = turned(coupling_ref, tree_level)
     own_sample, own_sketch = own_ref[:rank], own_ref[rank:]
-    other_sample, other_sketch = other_ref[:rank], other_ref[rank:]
+    if last:
+        other_sample = jnp.where(odd, refs[3][...], other_ref[...])
+        other_sketch = jnp.where(odd, other_ref[...], refs[3][...])
+    else:
+        other_sample, other_sketch = other_ref[:rank], other_ref[rank:]
     own = own_sample - dot(ahead, other_sketch)
     other = other_sample - dot(back, own_sketch)
     own_t, other_t = own.T, other.T
@@ -340,6 +369,8 @@
     moved = dot(inverse, jnp.concatenate([both, own_t, crossed], axis=1))
     pair_ref[:rank, :] = moved[:, :rank]
     pair_ref[rank:, :] = moved[:, rank : 2 * rank]
+    if tree_level == LEVELS - 2:
+        half_ref[...] = jnp.where(odd, moved[:, rank : 2 * rank], moved[:, :rank])
     maps_ref[0] = moved[:, 2 * rank : 3 * rank]
     maps_ref[1] = moved[:, 3 * rank :]
 
@@ -348,10 +379,11 @@
     return pl.BlockSpec((1, 1) + couplings.shape[2:], lambda step: (0, tree_level, 0, 0))
 
 
-def merge_step(tree_level, own, other, couplings, after):
+def merge_step(tree_level, own, others, couplings, after):
     rank = own.shape[1]
     f32 = jnp.float32
     last = tree_level == LEVELS - 1
+    split = tree_level == LEVELS - 2
     return pl.pallas_call(
         functools.partial(merge_body, tree_level),
         grid=(1,),
@@ -359,13 +391,14 @@
             jax.ShapeDtypeStruct((rank, rank), f32),
             jax.ShapeDtypeStruct((8, rank) if last else (2, rank, rank), f32),
             jax.ShapeDtypeStruct((rank, 2 * rank) if last else (2 * rank, rank), f32),
-        ],
-        in_specs=[VMEM, VMEM, coupling_spec(couplings, tree_level)] + [ANY] * len(after),
-        out_specs=[VMEM, ANY if last else VMEM, VMEM],
+        ]
+        + [jax.ShapeDtypeStruct((rank, rank), f32)] * split,
+        in_specs=[coupling_spec(couplings, tree_level)] + [VMEM] * (1 + len(others)) + [ANY] * len(after),
+        out_specs=[VMEM, ANY if last else VMEM, VMEM] + [VMEM] * split,
         compiler_params=small_params(),
         cost_estimate=small_cost(8),
         name=f"merge_orth_{tree_level}",
-    )(own, other, couplings, *after)
+    )(couplings, own, *others, *after)
 
 
 def lower_body(*refs):
@@ -428,7 +461,7 @@
         in_specs=[VMEM] * (len(parts) + 1),
         out_specs=VMEM,
         compiler_params=small_params(),
-        cost_estimate=small_cost(1),
+        cost_estimate=small_cost(200),
         name=f"upper_maps_{tree_level}",
     )(*parts, maps)
 
@@ -484,6 +517,7 @@
         in_specs=[VMEM] * ways,
         out_specs=ANY,
         scratch_shapes=[pltpu.SemaphoreType.DMA((ways,))],
+        compiler_params=small_params(),
         name="top_columns",
     )(*pieces)
 
@@ -501,16 +535,17 @@
     first = from_partner(send, "col", 1)
     passed, second_red = lax.optimization_barrier((keep[leaf:] + first[leaf:], second_red))
     second = from_partner(passed, "col", 2)
-    leaf_basis, basis_t, pair = leaf_step(keep_red, first_red, second_red, sketch_red, passed)
+    basis_t, pair = leaf_step(keep_red, first_red, second_red, sketch_red, passed)
     blocks, low_maps, after, parts = [], [], [], []
     for tree_level in range(LEVELS):
         if tree_level < LEVELS - 1:
-            other = from_partner(pair, ROW_COL, 2**tree_level)
+            others = [from_partner(pair, ROW_COL, 2**tree_level)]
         else:
-            other = waiting
+            others = [waiting, from_partner(waiting, ROW_COL, 1)]
         if tree_level == col_bits - 1:
-            after = [second]
-        block, maps, pair = merge_step(tree_level, pair, other, couplings, after)
+            leaf_basis, mark = basis_step(basis_t)
+            after = [second, mark]
+        block, maps, pair, *half = merge_step(tree_level, pair, others, couplings, after)
         blocks.append(block)
         if tree_level == LEVELS - 1:
             break
@@ -525,7 +560,7 @@
             parts = [cut[0]] + [from_partner(cut[away], "col", away) for away in range(1, ways)]
             after = [cut[0]]
         if tree_level == LEVELS - 2:
-            waiting = from_partner(pair, ROW_COL, 2 ** (LEVELS - 1))
+            waiting = from_partner(half[0], ROW_COL, 2 ** (LEVELS - 1))
             whole, waiting = lax.optimization_barrier((parts[0] + parts[1], waiting))
             far = from_partner(whole, ROW_COL, 2 ** (LEVELS - 1))
             after = [whole]

time: 91.3 us -> 86.9 us (0.952)
  Pallas kernels: 41.2 us -> 35.3 us
  other arithmetic: 4.51 us -> 9.16 us
  waiting for transfers between devices: 23.5 us -> 19.6 us
  starting transfers between devices: 19.3 us -> 20.9 us
    pallas_call x4 -> x3, Pallas kernels: 18.2 us -> 13.5 us  [merge_step(): pl.pallas_call(functools.partial(merge_body, tree_level), grid=(1,), out_...]
    pallas_call x1 -> x2, other arithmetic: 4.4 us -> 9.05 us  [merge_step(): pl.pallas_call(functools.partial(merge_body, tree_level), grid=(1,), out_...]
    ppermute x18 -> x19, waiting for transfers between devices: 23.5 us -> 19.6 us  [from_partner(): return lax.ppermute(block, axis, route)]
    ppermute x18 -> x19, starting transfers between devices: 19.3 us -> 20.9 us  [from_partner(): return lax.ppermute(block, axis, route)]
    pallas_call x1, Pallas kernels: 1.66 us -> 0.73 us  [columns_step(): pl.pallas_call(columns_body, out_shape=jax.ShapeDtypeStruct((1, rank, par...]
    pallas_call x1 -> x2, Pallas kernels: 5.56 us -> 5.25 us  [the longest x1 4.49 us: leaf_step(): pl.pallas_call(leaf_body, grid=(1,), out_shape=[jax.ShapeDtypeStruct((ran...]
  transfers between devices with their start and end apart: 18 -> 19, of which waited for: 10 -> 10; matrix products, arithmetic and copies ran while one was open for 5% -> 11% of each run, Pallas kernels for 24% -> 20%
where the time goes in v5:
time: 86.9 us; the launch traced here: 86.7 us
  Pallas kernels  35.3 us (41%)
  starting transfers between devices  20.9 us (24%)
  waiting for transfers between devices  19.6 us (23%)
  other arithmetic  9.16 us (11%)
  between operations  1.03 us (1%)
    ppermute x19, starting transfers between devices, from_partner(): return lax.ppermute(block, axis, route)  20.9 us
    ppermute x19, waiting for transfers between devices, from_partner(): return lax.ppermute(block, axis, route)  19.6 us
    pallas_call x3, Pallas kernels, merge_step(): pl.pallas_call(functools.partial(merge_body, tree_level), grid=(1,), out_...  13.5 us
    pallas_call x1, Pallas kernels, sample_rows(): pl.pallas_call(functools.partial(spmm_body, leaves=leaves), out_shape=[ja...  11.2 us
    pallas_call x2, other arithmetic, merge_step(): pl.pallas_call(functools.partial(merge_body, tree_level), grid=(1,), out_...  9.05 us
    pallas_call x1, Pallas kernels, leaf_step(): pl.pallas_call(leaf_body, grid=(1,), out_shape=[jax.ShapeDtypeStruct((ran...  4.49 us
    pallas_call x1, Pallas kernels, lower_step(): pl.pallas_call(lower_body, grid=(1,), out_shape=[jax.ShapeDtypeStruct((2...  1.8 us
  transfers between devices with their start and end apart: 19, of which 10 were waited for; matrix products, arithmetic and copies ran while one was open for 11% of the time, Pallas kernels for 20%

profile of v5, /device:TPU:0, one launch (start us, length us, event | category | flops | bytes accessed | tf_op | source)
XLA Modules:
  0.0 86.7 jit_solution(10569219090013163458)
XLA Ops:
  0.6 0.0 copy-start.2
  0.6 0.0 copy-start.1
  0.7 0.0 copy-start.3
  0.7 0.7 copy-done.3
  1.4 11.2 %spmm.1 = (f32[512,512]{1,0:T(8,128)S(1)}, f32[512,512]{1,0:T(8,128)S(1)}) custom-call(s32[168]{0:T(256)S(1)} %copy-done.3, bf16[168,128,128]{2,1,0:T(8,128)(2,1)} %tiles_ref.1, bf16[6144,512]{1,0:T(8,128)(2,1)} %sketch_ref.1), custom_call_target="tpu_custom_call" | custom-call | flops 6442450944 | bytes 13893632 | tf_op jit(solution)/shard_map/spmm/pallas_call | solution.py:215
  12.6 0.0 copy-start
  12.6 0.0 copy-done.2
  12.6 0.7 reduced_1.1
  13.3 0.5 collective-permute-start
  13.9 0.0 copy-done.1
  13.9 0.9 %reduced_2.1 = (f32[512,128]{1,0:T(8,128)S(1)}, f32[256,128]{1,0:T(8,128)S(1)}) custom-call(f32[512,128]{1,0:T(8,128)S(1)} %copy-done.2, f32[512,512]{1,0:T(8,128)S(1)} %get-tuple-element.36.refs_1_.refs_0_, bf16[256,512]{1,0:T(8,128)(2,1)S(1)} %copy-done.1), custom_call_target="tpu_custom_call" | custom-call | flops 10000000 | bytes 30000 | tf_op jit(solution)/shard_map/reduced_2/pallas_call | solution.py:256
  14.7 0.3 collective-permute-done.first_ref
  15.0 0.4 collective-permute-start.1
  15.5 2.7 %collective-permute-start.2 = (f32[256,128]{1,0:T(8,128)S(1)}, f32[256,128]{1,0:T(8,128)S(1)}, u32[]{:S(2)}, u32[]{:S(2)}) collective-permute-start(f32[256,128]{1,0:T(8,128)S(1)} %slice_add_fusion.1), channel_id=1, source_target_pairs={{0,2},{1,3},{2,0},{3,1},{4,6},{5,7},{6,4},{7,5},{8,10},{9,11},{10,... | collective-permute-start | bytes 393224 | tf_op jit(solution)/shard_map/ppermute | solution.py:25
  18.1 0.0 collective-permute-done.1.refs_1_
  18.1 0.1 slice_add_fusion._
  18.2 3.9 %collective-permute-done.2.second_ref = f32[256,128]{1,0:T(8,128)S(1)} collective-permute-done((f32[256,128]{1,0:T(8,128)S(1)}, f32[256,128]{1,0:T(8,128)S(1)}, u32[]{:S(2)}, u32[]{:S(2)}) %collective-permute-start.2) | collective-permute-done | bytes 131104 | tf_op jit(solution)/shard_map/ppermute | solution.py:25
  22.2 1.7 %collective-permute-start.5 = (f32[256,512]{1,0:T(8,128)S(1)}, f32[256,512]{1,0:T(8,128)S(1)}, u32[]{:S(2)}, u32[]{:S(2)}) collective-permute-start(f32[256,512]{1,0:T(8,128)S(1)} %slice_add_fusion._), channel_id=1, source_target_pairs={{0,2},{1,3},{2,0},{3,1},{4,6},{5,7},{6,4},{7,5},{8,10},{9,11},{10,... | collective-permute-start | bytes 1572872 | tf_op jit(solution)/shard_map/ppermute | solution.py:25
  23.9 4.5 %leaf_orth.1 = (f32[128,256]{1,0:T(8,128)S(1)}, f32[256,128]{1,0:T(8,128)S(1)}) custom-call(f32[512,128]{1,0:T(8,128)S(1)} %get-tuple-element.37.keep_ref, f32[512,128]{1,0:T(8,128)S(1)} %collective-permute-done.first_ref, f32[256,128]{1,0:T(8,128)S(1)} %collective-permute-done.2.second_ref, f32[256,128]{1,0:T(8,128)S(1)} %get-tuple-element.42.sketch_red_ref, ...), custom_call_target="tpu_custom_call" | custom-call | flops 80000000 | bytes 240000 | tf_op jit(solution)/shard_map/leaf_orth/pallas_call | solution.py:291
  28.4 0.1 collective-permute-start.3
  28.5 0.8 leaf_basis.1
  29.2 0.6 collective-permute-done.3.refs_2_
  29.8 0.0 copy-done
  29.8 4.6 %merge_orth_0.1 = (f32[128,128]{1,0:T(8,128)S(1)}, f32[2,128,128]{2,1,0:T(8,128)S(1)}, f32[256,128]{1,0:T(8,128)S(1)}) custom-call(bf16[1,5,128,128]{3,2,1,0:T(8,128)(2,1)S(1)} %copy-done, f32[256,128]{1,0:T(8,128)S(1)} %get-tuple-element.46.refs_1_, f32[256,128]{1,0:T(8,128)S(1)} %collective-permute-done.3.refs_2_), custom_call_target="tpu_custom_call" | custom-call | flops 80000000 | bytes 240000 | tf_op jit(solution)/shard_map/merge_orth_0/pallas_call | solution.py:387
  34.4 0.3 collective-permute-start.4
  34.8 5.3 %collective-permute-done.4.refs_2_ = f32[256,128]{1,0:T(8,128)S(1)} collective-permute-done((f32[256,128]{1,0:T(8,128)S(1)}, f32[256,128]{1,0:T(8,128)S(1)}, u32[]{:S(2)}, u32[]{:S(2)}) %collective-permute-start.4) | collective-permute-done | bytes 131104 | tf_op jit(solution)/shard_map/ppermute | solution.py:25
  40.1 0.0 collective-permute-done.5.refs_3_.refs_2_
  40.1 4.4 %merge_orth_1.1 = (f32[128,128]{1,0:T(8,128)S(1)}, f32[2,128,128]{2,1,0:T(8,128)S(1)}, f32[256,128]{1,0:T(8,128)S(1)}) custom-call(bf16[1,5,128,128]{3,2,1,0:T(8,128)(2,1)S(1)} %copy-done, f32[256,128]{1,0:T(8,128)S(1)} %get-tuple-element.48.refs_1_, f32[256,128]{1,0:T(8,128)S(1)} %collective-permute-done.4.refs_2_, ...), custom_call_target="tpu_custom_call" | custom-call | flops 80000000 | bytes 240000 | tf_op jit(solution)/shard_map/merge_orth_1/pallas_call | solution.py:387
  44.5 1.6 %collective-permute-start.6 = (f32[256,128]{1,0:T(8,128)S(1)}, f32[256,128]{1,0:T(8,128)S(1)}, u32[]{:S(2)}, u32[]{:S(2)}) collective-permute-start(f32[256,128]{1,0:T(8,128)S(1)} %get-tuple-element.51.refs_1_), channel_id=1, source_target_pairs={{0,4},{1,5},{2,6},{3,7},{4,0},{5,1},{6,2},{7,3},{8,12},{9,13},{10,... | collective-permute-start | bytes 393224 | tf_op jit(solution)/shard_map/ppermute | solution.py:25
  46.1 1.8 %lower_maps.1 = (f32[256,128]{1,0:T(8,128)S(1)}, f32[256,128]{1,0:T(8,128)S(1)}, f32[256,128]{1,0:T(8,128)S(1)}, f32[256,128]{1,0:T(8,128)S(1)}) custom-call(f32[512,512]{1,0:T(8,128)S(1)} %get-tuple-element.36.refs_1_.refs_0_, f32[512,512]{1,0:T(8,128)S(1)} %collective-permute-done.1.refs_1_, f32[256,512]{1,0:T(8,128)S(1)} %collective-permute-done.5.refs_3_.refs_2_, ...), custom_call_target="tpu_custom_call" | custom-call | flops 20000000 | bytes 60000 | tf_op jit(solution)/shard_map/lower_maps/pallas_call | solution.py:432
  47.9 0.1 collective-permute-start.10
  48.0 0.6 collective-permute-start.8
  48.6 1.5 %collective-permute-start.9 = (f32[256,128]{1,0:T(8,128)S(1)}, f32[256,128]{1,0:T(8,128)S(1)}, u32[]{:S(2)}, u32[]{:S(2)}) collective-permute-start(f32[256,128]{1,0:T(8,128)S(1)} %get-tuple-element.58), channel_id=1, source_target_pairs={{0,2},{1,3},{2,0},{3,1},{4,6},{5,7},{6,4},{7,5},{8,10},{9,11},{10,... | collective-permute-start | bytes 393224 | tf_op jit(solution)/shard_map/ppermute | solution.py:25
  50.1 0.0 collective-permute-done.6.refs_2_
  50.1 4.4 %merge_orth_2.1 = (f32[128,128]{1,0:T(8,128)S(1)}, f32[2,128,128]{2,1,0:T(8,128)S(1)}, f32[256,128]{1,0:T(8,128)S(1)}) custom-call(bf16[1,5,128,128]{3,2,1,0:T(8,128)(2,1)S(1)} %copy-done, f32[256,128]{1,0:T(8,128)S(1)} %get-tuple-element.51.refs_1_, f32[256,128]{1,0:T(8,128)S(1)} %collective-permute-done.6.refs_2_, ...), custom_call_target="tpu_custom_call" | custom-call | flops 80000000 | bytes 240000 | tf_op jit(solution)/shard_map/merge_orth_2/pallas_call | solution.py:387
  54.6 1.6 %collective-permute-start.7 = (f32[256,128]{1,0:T(8,128)S(1)}, f32[256,128]{1,0:T(8,128)S(1)}, u32[]{:S(2)}, u32[]{:S(2)}) collective-permute-start(f32[256,128]{1,0:T(8,128)S(1)} %get-tuple-element.56), channel_id=1, source_target_pairs={{0,8},{1,9},{2,10},{3,11},{4,12},{5,13},{6,14},{7,15},{8,0},{9,1},... | collective-permute-start | bytes 393224 | tf_op jit(solution)/shard_map/ppermute | solution.py:25
  56.2 0.0 collective-permute-done.10.refs_3_
  56.2 0.0 collective-permute-done.8.refs_1_
  56.2 0.0 collective-permute-done.9.refs_2_
  56.2 0.3 upper_maps_2.1.refs_0_
  56.5 1.0 %collective-permute-start.11 = (f32[256,128]{1,0:T(8,128)S(1)}, f32[256,128]{1,0:T(8,128)S(1)}, u32[]{:S(2)}, u32[]{:S(2)}) collective-permute-start(f32[256,128]{1,0:T(8,128)S(1)} %upper_maps_2.1.refs_0_), channel_id=1, source_target_pairs={{0,4},{1,5},{2,6},{3,7},{4,0},{5,1},{6,2},{7,3},{8,12},{9,13},{10,... | collective-permute-start | bytes 393224 | tf_op jit(solution)/shard_map/ppermute | solution.py:25
  57.5 2.2 %collective-permute-done.7 = f32[256,128]{1,0:T(8,128)S(1)} collective-permute-done((f32[256,128]{1,0:T(8,128)S(1)}, f32[256,128]{1,0:T(8,128)S(1)}, u32[]{:S(2)}, u32[]{:S(2)}) %collective-permute-start.7) | collective-permute-done | bytes 131104 | tf_op jit(solution)/shard_map/ppermute | solution.py:25
  59.7 4.7 %merge_orth_3.1 = (f32[5,128,128]{2,1,0:T(8,128)S(1)}, f32[256,128]{1,0:T(8,128)S(1)}, f32[2,128,128]{2,1,0:T(8,128)S(1)}, f32[128,128]{1,0:T(8,128)S(1)}) fusion(f32[5,128,128]{2,1,0:T(8,128)S(1)} %bitcast_dynamic-update-slice_fusion.2, bf16[1,5,128,128]{3,2,1,0:T(8,128)(2,1)S(1)} %copy-done, f32[256,128]{1,0:T(8,128)S(1)} %get-tuple-element.56, ...), kind=kCustom, calls=%fused_computation.3 | custom fusion | flops 80000000 | bytes 950272 | tf_op jit(solution)/shard_map/merge_orth_3/pallas_call | solution.py:387
  64.4 0.0 collective-permute-done.11.refs_1_
  64.4 0.3 upper_maps_3.1
  64.7 1.6 %collective-permute-start.12 = (f32[256,128]{1,0:T(8,128)S(1)}, f32[256,128]{1,0:T(8,128)S(1)}, u32[]{:S(2)}, u32[]{:S(2)}) collective-permute-start(f32[256,128]{1,0:T(8,128)S(1)} %upper_maps_3.1), channel_id=1, source_target_pairs={{0,8},{1,9},{2,10},{3,11},{4,12},{5,13},{6,14},{7,15},{8,0},{9,1},... | collective-permute-start | bytes 393224 | tf_op jit(solution)/shard_map/ppermute | solution.py:25
  66.4 2.6 %collective-permute-start.13 = (f32[128,128]{1,0:T(8,128)S(1)}, f32[128,128]{1,0:T(8,128)S(1)}, u32[]{:S(2)}, u32[]{:S(2)}) collective-permute-start(f32[128,128]{1,0:T(8,128)S(1)} %get-tuple-element.83), channel_id=1, source_target_pairs={{0,16},{1,17},{2,18},{3,19},{4,20},{5,21},{6,22},{7,23},{8,24},{9,... | collective-permute-start | bytes 196616 | tf_op jit(solution)/shard_map/ppermute | solution.py:25
  69.0 1.5 %collective-permute-done.12 = f32[256,128]{1,0:T(8,128)S(1)} collective-permute-done((f32[256,128]{1,0:T(8,128)S(1)}, f32[256,128]{1,0:T(8,128)S(1)}, u32[]{:S(2)}, u32[]{:S(2)}) %collective-permute-start.12) | collective-permute-done | bytes 131104 | tf_op jit(solution)/shard_map/ppermute | solution.py:25
  70.5 1.1 %collective-permute-done.13 = f32[128,128]{1,0:T(8,128)S(1)} collective-permute-done((f32[128,128]{1,0:T(8,128)S(1)}, f32[128,128]{1,0:T(8,128)S(1)}, u32[]{:S(2)}, u32[]{:S(2)}) %collective-permute-start.13) | collective-permute-done | bytes 65568 | tf_op jit(solution)/shard_map/ppermute | solution.py:25
  71.5 2.6 %collective-permute-start.15 = (f32[256,128]{1,0:T(8,128)S(1)}, f32[256,128]{1,0:T(8,128)S(1)}, u32[]{:S(2)}, u32[]{:S(2)}) collective-permute-start(f32[256,128]{1,0:T(8,128)S(1)} %add.11.own_ref), channel_id=1, source_target_pairs={{0,16},{1,17},{2,18},{3,19},{4,20},{5,21},{6,22},{7,23},{8,24},{9,... | collective-permute-start | bytes 393224 | tf_op jit(solution)/shard_map/ppermute | solution.py:25
  74.1 0.0 collective-permute-start.14
  74.1 1.3 %collective-permute-done.14 = f32[128,128]{1,0:T(8,128)S(1)} collective-permute-done((f32[128,128]{1,0:T(8,128)S(1)}, f32[128,128]{1,0:T(8,128)S(1)}, u32[]{:S(2)}, u32[]{:S(2)}) %collective-permute-start.14) | collective-permute-done | bytes 65568 | tf_op jit(solution)/shard_map/ppermute | solution.py:25
  75.4 4.4 %merge_orth_4.1 = (f32[5,128,128]{2,1,0:T(8,128)S(1)}, f32[128,256]{1,0:T(8,128)S(1)}, f32[8,128]{1,0:T(8,128)}) fusion(f32[5,128,128]{2,1,0:T(8,128)S(1)} %get-tuple-element.78, bf16[1,5,128,128]{3,2,1,0:T(8,128)(2,1)S(1)} %copy-done, f32[256,128]{1,0:T(8,128)S(1)} %get-tuple-element.79, f32[128,128]{1,0:T(8,128)S(1)} %collective-permute-done.13, ...), kind=kCustom, calls=%fused_computation.2 | custom fusion | flops 80000000 | bytes 757760 | tf_op jit(solution)/shard_map/merge_orth_4/pallas_call | solution.py:387
  79.8 0.0 copy-start.4
  79.8 0.0 collective-permute-done.15.other_ref
  79.8 0.6 top_sample.1.refs_0_
  80.4 0.2 collective-permute-start.16
  80.6 0.5 collective-permute-start.17
  81.1 1.2 %collective-permute-start.18 = (f32[128,128]{1,0:T(8,128)S(1)}, f32[128,128]{1,0:T(8,128)S(1)}, u32[]{:S(2)}, u32[]{:S(2)}) collective-permute-start(f32[128,128]{1,0:T(8,128)S(1)} %top_sample.1.refs_0_), channel_id=1, source_target_pairs={{0,3},{1,2},{2,1},{3,0},{4,7},{5,6},{6,5},{7,4},{8,11},{9,10},{10,... | collective-permute-start | bytes 196616 | tf_op jit(solution)/shard_map/ppermute | solution.py:25
  82.3 0.0 collective-permute-done.16.refs_1_
  82.3 3.2 %collective-permute-done.17.refs_2_ = f32[128,128]{1,0:T(8,128)S(1)} collective-permute-done((f32[128,128]{1,0:T(8,128)S(1)}, f32[128,128]{1,0:T(8,128)S(1)}, u32[]{:S(2)}, u32[]{:S(2)}) %collective-permute-start.17) | collective-permute-done | bytes 65568 | tf_op jit(solution)/shard_map/ppermute | solution.py:25
  85.5 0.3 collective-permute-done.18.refs_3_
  85.8 0.7 top_columns.1
  86.5 0.0 copy-done.4
  (5 shorter events, 0.0 us)
Async XLA Ops:
  0.6 12.0 %copy-start.2 = (f32[512,128]{1,0:T(8,128)S(1)}, f32[512,128]{1,0:T(8,128)}, u32[]{:S(2)}) copy-start(f32[512,128]{1,0:T(8,128)} %refs_0_.8) | copy-start | bytes 786436
  0.6 13.2 %copy-start.1 = (bf16[256,512]{1,0:T(8,128)(2,1)S(1)}, bf16[256,512]{1,0:T(8,128)(2,1)}, u32[]{:S(2)}) copy-start(bf16[256,512]{1,0:T(8,128)(2,1)} %refs_3_.1) | copy-start | bytes 786436
  0.7 0.7 copy-start.3
  12.6 17.2 %copy-start = (bf16[1,5,128,128]{3,2,1,0:T(8,128)(2,1)S(1)}, bf16[1,5,128,128]{3,2,1,0:T(8,128)(2,1)}, u32[]{:S(2)}) copy-start(bf16[1,5,128,128]{3,2,1,0:T(8,128)(2,1)} %coupling_ref.1) | copy-start | bytes 491524
  13.3 1.7 %collective-permute-start = (f32[512,128]{1,0:T(8,128)S(1)}, f32[512,128]{1,0:T(8,128)S(1)}, u32[]{:S(2)}, u32[]{:S(2)}) collective-permute-start(f32[512,128]{1,0:T(8,128)S(1)} %reduced_1.1), channel_id=1, source_target_pairs={{0,1},{1,0},{2,3},{3,2},{4,5},{5,4},{6,7},{7,6},{8,9},{9,8},{10,11... | collective-permute-start | bytes 786440 | tf_op jit(solution)/shard_map/ppermute | solution.py:25
  15.0 3.1 %collective-permute-start.1 = (f32[512,512]{1,0:T(8,128)S(1)}, f32[512,512]{1,0:T(8,128)S(1)}, u32[]{:S(2)}, u32[]{:S(2)}) collective-permute-start(f32[512,512]{1,0:T(8,128)S(1)} %get-tuple-element.39.refs_1_), channel_id=1, source_target_pairs={{0,1},{1,0},{2,3},{3,2},{4,5},{5,4},{6,7},{7,6},{8,9},{9,8},{10,11... | collective-permute-start | bytes 3145736 | tf_op jit(solution)/shard_map/ppermute | solution.py:25
  15.5 6.7 %collective-permute-start.2 = (f32[256,128]{1,0:T(8,128)S(1)}, f32[256,128]{1,0:T(8,128)S(1)}, u32[]{:S(2)}, u32[]{:S(2)}) collective-permute-start(f32[256,128]{1,0:T(8,128)S(1)} %slice_add_fusion.1), channel_id=1, source_target_pairs={{0,2},{1,3},{2,0},{3,1},{4,6},{5,7},{6,4},{7,5},{8,10},{9,11},{10,... | collective-permute-start | bytes 393224 | tf_op jit(solution)/shard_map/ppermute | solution.py:25
  22.2 17.9 %collective-permute-start.5 = (f32[256,512]{1,0:T(8,128)S(1)}, f32[256,512]{1,0:T(8,128)S(1)}, u32[]{:S(2)}, u32[]{:S(2)}) collective-permute-start(f32[256,512]{1,0:T(8,128)S(1)} %slice_add_fusion._), channel_id=1, source_target_pairs={{0,2},{1,3},{2,0},{3,1},{4,6},{5,7},{6,4},{7,5},{8,10},{9,11},{10,... | collective-permute-start | bytes 1572872 | tf_op jit(solution)/shard_map/ppermute | solution.py:25
  28.4 1.4 %collective-permute-start.3 = (f32[256,128]{1,0:T(8,128)S(1)}, f32[256,128]{1,0:T(8,128)S(1)}, u32[]{:S(2)}, u32[]{:S(2)}) collective-permute-start(f32[256,128]{1,0:T(8,128)S(1)} %get-tuple-element.46.refs_1_), channel_id=1, source_target_pairs={{0,1},{1,0},{2,3},{3,2},{4,5},{5,4},{6,7},{7,6},{8,9},{9,8},{10,11... | collective-permute-start | bytes 393224 | tf_op jit(solution)/shard_map/ppermute | solution.py:25
  34.4 5.6 %collective-permute-start.4 = (f32[256,128]{1,0:T(8,128)S(1)}, f32[256,128]{1,0:T(8,128)S(1)}, u32[]{:S(2)}, u32[]{:S(2)}) collective-permute-start(f32[256,128]{1,0:T(8,128)S(1)} %get-tuple-element.48.refs_1_), channel_id=1, source_target_pairs={{0,2},{1,3},{2,0},{3,1},{4,6},{5,7},{6,4},{7,5},{8,10},{9,11},{10,... | collective-permute-start | bytes 393224 | tf_op jit(solution)/shard_map/ppermute | solution.py:25
  44.5 5.6 %collective-permute-start.6 = (f32[256,128]{1,0:T(8,128)S(1)}, f32[256,128]{1,0:T(8,128)S(1)}, u32[]{:S(2)}, u32[]{:S(2)}) collective-permute-start(f32[256,128]{1,0:T(8,128)S(1)} %get-tuple-element.51.refs_1_), channel_id=1, source_target_pairs={{0,4},{1,5},{2,6},{3,7},{4,0},{5,1},{6,2},{7,3},{8,12},{9,13},{10,... | collective-permute-start | bytes 393224 | tf_op jit(solution)/shard_map/ppermute | solution.py:25
  47.9 8.3 %collective-permute-start.10 = (f32[256,128]{1,0:T(8,128)S(1)}, f32[256,128]{1,0:T(8,128)S(1)}, u32[]{:S(2)}, u32[]{:S(2)}) collective-permute-start(f32[256,128]{1,0:T(8,128)S(1)} %get-tuple-element.59), channel_id=1, source_target_pairs={{0,3},{1,2},{2,1},{3,0},{4,7},{5,6},{6,5},{7,4},{8,11},{9,10},{10,... | collective-permute-start | bytes 393224 | tf_op jit(solution)/shard_map/ppermute | solution.py:25
  48.0 8.2 %collective-permute-start.8 = (f32[256,128]{1,0:T(8,128)S(1)}, f32[256,128]{1,0:T(8,128)S(1)}, u32[]{:S(2)}, u32[]{:S(2)}) collective-permute-start(f32[256,128]{1,0:T(8,128)S(1)} %get-tuple-element.57), channel_id=1, source_target_pairs={{0,1},{1,0},{2,3},{3,2},{4,5},{5,4},{6,7},{7,6},{8,9},{9,8},{10,11... | collective-permute-start | bytes 393224 | tf_op jit(solution)/shard_map/ppermute | solution.py:25
  48.6 7.6 %collective-permute-start.9 = (f32[256,128]{1,0:T(8,128)S(1)}, f32[256,128]{1,0:T(8,128)S(1)}, u32[]{:S(2)}, u32[]{:S(2)}) collective-permute-start(f32[256,128]{1,0:T(8,128)S(1)} %get-tuple-element.58), channel_id=1, source_target_pairs={{0,2},{1,3},{2,0},{3,1},{4,6},{5,7},{6,4},{7,5},{8,10},{9,11},{10,... | collective-permute-start | bytes 393224 | tf_op jit(solution)/shard_map/ppermute | solution.py:25
  54.6 5.2 %collective-permute-start.7 = (f32[256,128]{1,0:T(8,128)S(1)}, f32[256,128]{1,0:T(8,128)S(1)}, u32[]{:S(2)}, u32[]{:S(2)}) collective-permute-start(f32[256,128]{1,0:T(8,128)S(1)} %get-tuple-element.56), channel_id=1, source_target_pairs={{0,8},{1,9},{2,10},{3,11},{4,12},{5,13},{6,14},{7,15},{8,0},{9,1},... | collective-permute-start | bytes 393224 | tf_op jit(solution)/shard_map/ppermute | solution.py:25
  56.5 7.9 %collective-permute-start.11 = (f32[256,128]{1,0:T(8,128)S(1)}, f32[256,128]{1,0:T(8,128)S(1)}, u32[]{:S(2)}, u32[]{:S(2)}) collective-permute-start(f32[256,128]{1,0:T(8,128)S(1)} %upper_maps_2.1.refs_0_), channel_id=1, source_target_pairs={{0,4},{1,5},{2,6},{3,7},{4,0},{5,1},{6,2},{7,3},{8,12},{9,13},{10,... | collective-permute-start | bytes 393224 | tf_op jit(solution)/shard_map/ppermute | solution.py:25
  64.7 5.7 %collective-permute-start.12 = (f32[256,128]{1,0:T(8,128)S(1)}, f32[256,128]{1,0:T(8,128)S(1)}, u32[]{:S(2)}, u32[]{:S(2)}) collective-permute-start(f32[256,128]{1,0:T(8,128)S(1)} %upper_maps_3.1), channel_id=1, source_target_pairs={{0,8},{1,9},{2,10},{3,11},{4,12},{5,13},{6,14},{7,15},{8,0},{9,1},... | collective-permute-start | bytes 393224 | tf_op jit(solution)/shard_map/ppermute | solution.py:25
  66.4 5.2 %collective-permute-start.13 = (f32[128,128]{1,0:T(8,128)S(1)}, f32[128,128]{1,0:T(8,128)S(1)}, u32[]{:S(2)}, u32[]{:S(2)}) collective-permute-start(f32[128,128]{1,0:T(8,128)S(1)} %get-tuple-element.83), channel_id=1, source_target_pairs={{0,16},{1,17},{2,18},{3,19},{4,20},{5,21},{6,22},{7,23},{8,24},{9,... | collective-permute-start | bytes 196616 | tf_op jit(solution)/shard_map/ppermute | solution.py:25
  71.5 8.3 %collective-permute-start.15 = (f32[256,128]{1,0:T(8,128)S(1)}, f32[256,128]{1,0:T(8,128)S(1)}, u32[]{:S(2)}, u32[]{:S(2)}) collective-permute-start(f32[256,128]{1,0:T(8,128)S(1)} %add.11.own_ref), channel_id=1, source_target_pairs={{0,16},{1,17},{2,18},{3,19},{4,20},{5,21},{6,22},{7,23},{8,24},{9,... | collective-permute-start | bytes 393224 | tf_op jit(solution)/shard_map/ppermute | solution.py:25
  74.1 1.3 %collective-permute-start.14 = (f32[128,128]{1,0:T(8,128)S(1)}, f32[128,128]{1,0:T(8,128)S(1)}, u32[]{:S(2)}, u32[]{:S(2)}) collective-permute-start(f32[128,128]{1,0:T(8,128)S(1)} %collective-permute-done.13), channel_id=1, source_target_pairs={{0,1},{1,0},{2,3},{3,2},{4,5},{5,4},{6,7},{7,6},{8,9},{9,8},{10,11... | collective-permute-start | bytes 196616 | tf_op jit(solution)/shard_map/ppermute | solution.py:25
  79.8 6.8 %copy-start.4 = (f32[5,128,128]{2,1,0:T(8,128)}, f32[5,128,128]{2,1,0:T(8,128)S(1)}, u32[]{:S(2)}) copy-start(f32[5,128,128]{2,1,0:T(8,128)S(1)} %get-tuple-element.72) | copy-start | bytes 983044
  80.4 1.9 %collective-permute-start.16 = (f32[128,128]{1,0:T(8,128)S(1)}, f32[128,128]{1,0:T(8,128)S(1)}, u32[]{:S(2)}, u32[]{:S(2)}) collective-permute-start(f32[128,128]{1,0:T(8,128)S(1)} %top_sample.1.refs_0_), channel_id=1, source_target_pairs={{0,1},{1,0},{2,3},{3,2},{4,5},{5,4},{6,7},{7,6},{8,9},{9,8},{10,11... | collective-permute-start | bytes 196616 | tf_op jit(solution)/shard_map/ppermute | solution.py:25
  80.6 4.9 %collective-permute-start.17 = (f32[128,128]{1,0:T(8,128)S(1)}, f32[128,128]{1,0:T(8,128)S(1)}, u32[]{:S(2)}, u32[]{:S(2)}) collective-permute-start(f32[128,128]{1,0:T(8,128)S(1)} %top_sample.1.refs_0_), channel_id=1, source_target_pairs={{0,2},{1,3},{2,0},{3,1},{4,6},{5,7},{6,4},{7,5},{8,10},{9,11},{10,... | collective-permute-start | bytes 196616 | tf_op jit(solution)/shard_map/ppermute | solution.py:25
  81.1 4.7 %collective-permute-start.18 = (f32[128,128]{1,0:T(8,128)S(1)}, f32[128,128]{1,0:T(8,128)S(1)}, u32[]{:S(2)}, u32[]{:S(2)}) collective-permute-start(f32[128,128]{1,0:T(8,128)S(1)} %top_sample.1.refs_0_), channel_id=1, source_target_pairs={{0,3},{1,2},{2,1},{3,0},{4,7},{5,6},{6,5},{7,4},{8,11},{9,10},{10,... | collective-permute-start | bytes 196616 | tf_op jit(solution)/shard_map/ppermute | solution.py:25

commit v6 on v5

--- a/solution.py
+++ b/solution.py
@@ -360,26 +360,28 @@
     )
     both = dot(stacked_t, stacked if last else right)
     if not last:
-        crossed = dot(other_t, back)
+        sides = [own_t, dot(other_t, back)]
+        if maps_ref.shape[0] == 4:
+            sides += [other_t, dot(own_t, ahead)]
     inverse = inverse_factor(both[:, :rank], square_sum(own) + square_sum(other))
     block_ref[...] = dot_nt(own, inverse)
     if last:
         pair_ref[...] = dot(inverse, stacked_t)
         return
-    moved = dot(inverse, jnp.concatenate([both, own_t, crossed], axis=1))
+    moved = dot(inverse, jnp.concatenate([both] + sides, axis=1))
     pair_ref[:rank, :] = moved[:, :rank]
     pair_ref[rank:, :] = moved[:, rank : 2 * rank]
     if tree_level == LEVELS - 2:
         half_ref[...] = jnp.where(odd, moved[:, rank : 2 * rank], moved[:, :rank])
-    maps_ref[0] = moved[:, 2 * rank : 3 * rank]
-    maps_ref[1] = moved[:, 3 * rank :]
+    for side in range(len(sides)):
+        maps_ref[side] = moved[:, (2 + side) * rank : (3 + side) * rank]
 
 
 def coupling_spec(couplings, tree_level):
     return pl.BlockSpec((1, 1) + couplings.shape[2:], lambda step: (0, tree_level, 0, 0))
 
 
-def merge_step(tree_level, own, others, couplings, after):
+def merge_step(tree_level, own, others, couplings, sides, after):
     rank = own.shape[1]
     f32 = jnp.float32
     last = tree_level == LEVELS - 1
@@ -389,7 +391,7 @@
         grid=(1,),
         out_shape=[
             jax.ShapeDtypeStruct((rank, rank), f32),
-            jax.ShapeDtypeStruct((8, rank) if last else (2, rank, rank), f32),
+            jax.ShapeDtypeStruct((8, rank) if last else (2 * sides, rank, rank), f32),
             jax.ShapeDtypeStruct((rank, 2 * rank) if last else (2 * rank, rank), f32),
         ]
         + [jax.ShapeDtypeStruct((rank, rank), f32)] * split,
@@ -442,28 +444,35 @@
     )(keep, first, second, row_sketch, basis_t, *maps)
 
 
-def upper_body(*refs):
+def upper_body(count, *refs):
     maps_ref, out_ref = refs[-2:]
-    total = refs[0][...]
-    for ref in refs[1:-2]:
-        total = total + ref[...]
+
+    def total(parts):
+        added = parts[0][...]
+        for ref in parts[1:]:
+            added = added + ref[...]
+        return added
+
     rank = maps_ref.shape[1]
-    sample, sketch = total[:rank], total[rank:]
-    lifted = maps_ref[0]
-    out_ref[:rank, :] = dot(lifted, sample) - dot(maps_ref[1], sketch)
-    out_ref[rank:, :] = dot(lifted, sketch)
-
-
-def upper_step(tree_level, parts, maps):
-    return pl.pallas_call(
-        upper_body,
-        out_shape=jax.ShapeDtypeStruct(parts[0].shape, jnp.float32),
-        in_specs=[VMEM] * (len(parts) + 1),
+    own, other = total(refs[:count]), total(refs[count:-2])
+    nodes = jnp.concatenate([own, other], axis=0)
+    sketches = jnp.concatenate([own[rank:], other[rank:]], axis=0)
+    lifts = jnp.concatenate([maps_ref[0], maps_ref[2]], axis=1)
+    signed = jnp.concatenate([maps_ref[0], -maps_ref[1], maps_ref[2], -maps_ref[3]], axis=1)
+    out_ref[:rank, :] = dot(signed, nodes)
+    out_ref[rank:, :] = dot(lifts, sketches)
+
+
+def upper_step(tree_level, own, other, maps):
+    return pl.pallas_call(
+        functools.partial(upper_body, len(own)),
+        out_shape=jax.ShapeDtypeStruct(own[0].shape, jnp.float32),
+        in_specs=[VMEM] * (len(own) + len(other) + 1),
         out_specs=VMEM,
         compiler_params=small_params(),
-        cost_estimate=small_cost(200),
+        cost_estimate=small_cost(1),
         name=f"upper_maps_{tree_level}",
-    )(*parts, maps)
+    )(*own, *other, maps)
 
 
 def top_body(own_ref, other_ref, coupling_ref, basis_t_ref, out_ref):
@@ -536,35 +545,35 @@
     passed, second_red = lax.optimization_barrier((keep[leaf:] + first[leaf:], second_red))
     second = from_partner(passed, "col", 2)
     basis_t, pair = leaf_step(keep_red, first_red, second_red, sketch_red, passed)
-    blocks, low_maps, after, parts = [], [], [], []
+    blocks, low_maps, after = [], [], []
     for tree_level in range(LEVELS):
         if tree_level < LEVELS - 1:
             others = [from_partner(pair, ROW_COL, 2**tree_level)]
         else:
             others = [waiting, from_partner(waiting, ROW_COL, 1)]
-        if tree_level == col_bits - 1:
+        if tree_level == 1:
             leaf_basis, mark = basis_step(basis_t)
-            after = [second, mark]
-        block, maps, pair, *half = merge_step(tree_level, pair, others, couplings, after)
+            after = after + [mark]
+        sides = 1 if tree_level < col_bits - 1 else 2
+        block, maps, pair, *half = merge_step(tree_level, pair, others, couplings, sides, after)
         blocks.append(block)
         if tree_level == LEVELS - 1:
             break
-        if tree_level < col_bits:
+        if tree_level == LEVELS - 2:
+            waiting = from_partner(half[0], ROW_COL, 2 ** (LEVELS - 1))
+        if tree_level < col_bits - 1:
             low_maps.append(maps)
         else:
-            mine = upper_step(tree_level, parts, maps)
-            parts = [mine, from_partner(mine, ROW_COL, 2**tree_level)]
-            after = [mine]
-        if tree_level == col_bits - 1:
+            total = upper_step(tree_level, own, other, maps)
+            own = [total]
+            other = [from_partner(total, ROW_COL, 2 ** (tree_level + 1))]
+            after = [total]
+        if tree_level == col_bits - 2:
             cut = lower_step(keep, first, second, row_sketch, basis_t, low_maps)
-            parts = [cut[0]] + [from_partner(cut[away], "col", away) for away in range(1, ways)]
+            cut = [cut[0]] + [from_partner(cut[away], "col", away) for away in range(1, ways)]
+            own, other = cut[: ways // 2], cut[ways // 2 :]
             after = [cut[0]]
-        if tree_level == LEVELS - 2:
-            waiting = from_partner(half[0], ROW_COL, 2 ** (LEVELS - 1))
-            whole, waiting = lax.optimization_barrier((parts[0] + parts[1], waiting))
-            far = from_partner(whole, ROW_COL, 2 ** (LEVELS - 1))
-            after = [whole]
-    top = top_step(whole, far, couplings, pair)
+    top = top_step(own[0], other[0], couplings, pair)
     pieces = [top] + [from_partner(top, "col", away) for away in range(1, ways)]
     transfer = jnp.stack(blocks, axis=0)[None]
     return (leaf_basis, transfer, columns_step(pieces))

time: 86.9 us -> 86.1 us (level)
  starting transfers between devices: 20.9 us -> 18.2 us
  waiting for transfers between devices: 19.6 us -> 20.8 us
    ppermute x19, starting transfers between devices: 20.9 us -> 18.2 us  [from_partner(): return lax.ppermute(block, axis, route)]
    ppermute x19, waiting for transfers between devices: 19.6 us -> 20.8 us  [from_partner(): return lax.ppermute(block, axis, route)]
  transfers between devices with their start and end apart: 19 -> 19, of which waited for: 10 -> 11; matrix products, arithmetic and copies ran while one was open for 11% -> 11% of each run, Pallas kernels for 20% -> 26%
where the time goes in v6:
time: 86.1 us; the launch traced here: 85.9 us
  Pallas kernels  35.8 us (42%)
  waiting for transfers between devices  20.8 us (24%)
  starting transfers between devices  18.2 us (21%)
  other arithmetic  9.24 us (11%)
  between operations  1.01 us (1%)
    ppermute x19, waiting for transfers between devices, from_partner(): return lax.ppermute(block, axis, route)  20.8 us
    ppermute x19, starting transfers between devices, from_partner(): return lax.ppermute(block, axis, route)  18.2 us
    pallas_call x3, Pallas kernels, merge_step(): pl.pallas_call(functools.partial(merge_body, tree_level), grid=(1,), out_...  13.7 us
    pallas_call x1, Pallas kernels, sample_rows(): pl.pallas_call(functools.partial(spmm_body, leaves=leaves), out_shape=[ja...  11.2 us
    pallas_call x2, other arithmetic, merge_step(): pl.pallas_call(functools.partial(merge_body, tree_level), grid=(1,), out_...  9.14 us
    pallas_call x1, Pallas kernels, leaf_step(): pl.pallas_call(leaf_body, grid=(1,), out_shape=[jax.ShapeDtypeStruct((ran...  4.49 us
  transfers between devices with their start and end apart: 19, of which 11 were waited for; matrix products, arithmetic and copies ran while one was open for 11% of the time, Pallas kernels for 26%

profile of v6, /device:TPU:0, one launch (start us, length us, event | category | flops | bytes accessed | tf_op | source)
XLA Modules:
  0.0 85.9 jit_solution(6298878377923575431)
XLA Ops:
  0.6 0.0 copy-start.2
  0.6 0.0 copy-start.1
  0.7 0.0 copy-start.3
  0.7 0.7 copy-done.3
  1.4 11.2 %spmm.1 = (f32[512,512]{1,0:T(8,128)S(1)}, f32[512,512]{1,0:T(8,128)S(1)}) custom-call(s32[168]{0:T(256)S(1)} %copy-done.3, bf16[168,128,128]{2,1,0:T(8,128)(2,1)} %tiles_ref.1, bf16[6144,512]{1,0:T(8,128)(2,1)} %sketch_ref.1), custom_call_target="tpu_custom_call" | custom-call | flops 6442450944 | bytes 13893632 | tf_op jit(solution)/shard_map/spmm/pallas_call | solution.py:215
  12.6 0.0 copy-start
  12.6 0.0 copy-done.2
  12.6 0.7 reduced_1.1
  13.3 0.5 collective-permute-start
  13.9 0.0 copy-done.1
  13.9 0.9 %reduced_2.1 = (f32[512,128]{1,0:T(8,128)S(1)}, f32[256,128]{1,0:T(8,128)S(1)}) custom-call(f32[512,128]{1,0:T(8,128)S(1)} %copy-done.2, f32[512,512]{1,0:T(8,128)S(1)} %get-tuple-element.34.refs_1_.refs_0_, bf16[256,512]{1,0:T(8,128)(2,1)S(1)} %copy-done.1), custom_call_target="tpu_custom_call" | custom-call | flops 10000000 | bytes 30000 | tf_op jit(solution)/shard_map/reduced_2/pallas_call | solution.py:256
  14.7 0.3 collective-permute-done.first_ref
  15.0 0.4 collective-permute-start.1
  15.5 2.7 %collective-permute-start.2 = (f32[256,128]{1,0:T(8,128)S(1)}, f32[256,128]{1,0:T(8,128)S(1)}, u32[]{:S(2)}, u32[]{:S(2)}) collective-permute-start(f32[256,128]{1,0:T(8,128)S(1)} %slice_add_fusion.1), channel_id=1, source_target_pairs={{0,2},{1,3},{2,0},{3,1},{4,6},{5,7},{6,4},{7,5},{8,10},{9,11},{10,... | collective-permute-start | bytes 393224 | tf_op jit(solution)/shard_map/ppermute | solution.py:25
  18.1 0.0 collective-permute-done.1.refs_1_
  18.1 0.1 slice_add_fusion._
  18.2 3.9 %collective-permute-done.2.second_ref = f32[256,128]{1,0:T(8,128)S(1)} collective-permute-done((f32[256,128]{1,0:T(8,128)S(1)}, f32[256,128]{1,0:T(8,128)S(1)}, u32[]{:S(2)}, u32[]{:S(2)}) %collective-permute-start.2) | collective-permute-done | bytes 131104 | tf_op jit(solution)/shard_map/ppermute | solution.py:25
  22.2 1.7 %collective-permute-start.5 = (f32[256,512]{1,0:T(8,128)S(1)}, f32[256,512]{1,0:T(8,128)S(1)}, u32[]{:S(2)}, u32[]{:S(2)}) collective-permute-start(f32[256,512]{1,0:T(8,128)S(1)} %slice_add_fusion._), channel_id=1, source_target_pairs={{0,2},{1,3},{2,0},{3,1},{4,6},{5,7},{6,4},{7,5},{8,10},{9,11},{10,... | collective-permute-start | bytes 1572872 | tf_op jit(solution)/shard_map/ppermute | solution.py:25
  23.9 4.5 %leaf_orth.1 = (f32[128,256]{1,0:T(8,128)S(1)}, f32[256,128]{1,0:T(8,128)S(1)}) custom-call(f32[512,128]{1,0:T(8,128)S(1)} %get-tuple-element.35.keep_ref, f32[512,128]{1,0:T(8,128)S(1)} %collective-permute-done.first_ref, f32[256,128]{1,0:T(8,128)S(1)} %collective-permute-done.2.second_ref, f32[256,128]{1,0:T(8,128)S(1)} %get-tuple-element.40.sketch_red_ref, ...), custom_call_target="tpu_custom_call" | custom-call | flops 80000000 | bytes 240000 | tf_op jit(solution)/shard_map/leaf_orth/pallas_call | solution.py:291
  28.4 0.1 collective-permute-start.3
  28.5 0.8 leaf_basis.1
  29.2 0.6 collective-permute-done.3.refs_2_
  29.8 4.6 %merge_orth_0.1 = (f32[128,128]{1,0:T(8,128)S(1)}, f32[2,128,128]{2,1,0:T(8,128)S(1)}, f32[256,128]{1,0:T(8,128)S(1)}) custom-call(bf16[1,5,128,128]{3,2,1,0:T(8,128)(2,1)S(1)} %copy-done, f32[256,128]{1,0:T(8,128)S(1)} %get-tuple-element.44.refs_1_, f32[256,128]{1,0:T(8,128)S(1)} %collective-permute-done.3.refs_2_), custom_call_target="tpu_custom_call" | custom-call | flops 80000000 | bytes 240000 | tf_op jit(solution)/shard_map/merge_orth_0/pallas_call | solution.py:389
  34.4 0.3 collective-permute-start.4
  34.8 1.0 %collective-permute-done.5.refs_2_ = f32[256,512]{1,0:T(8,128)S(1)} collective-permute-done((f32[256,512]{1,0:T(8,128)S(1)}, f32[256,512]{1,0:T(8,128)S(1)}, u32[]{:S(2)}, u32[]{:S(2)}) %collective-permute-start.5) | collective-permute-done | bytes 524320 | tf_op jit(solution)/shard_map/ppermute | solution.py:25
  35.8 1.4 %lower_maps.1 = (f32[256,128]{1,0:T(8,128)S(1)}, f32[256,128]{1,0:T(8,128)S(1)}, f32[256,128]{1,0:T(8,128)S(1)}, f32[256,128]{1,0:T(8,128)S(1)}) custom-call(f32[512,512]{1,0:T(8,128)S(1)} %get-tuple-element.34.refs_1_.refs_0_, f32[512,512]{1,0:T(8,128)S(1)} %collective-permute-done.1.refs_1_, f32[256,512]{1,0:T(8,128)S(1)} %collective-permute-done.5.refs_2_, ...), custom_call_target="tpu_custom_call" | custom-call | flops 20000000 | bytes 60000 | tf_op jit(solution)/shard_map/lower_maps/pallas_call | solution.py:434
  37.2 0.1 collective-permute-start.7
  37.2 1.6 %collective-permute-start.8 = (f32[256,128]{1,0:T(8,128)S(1)}, f32[256,128]{1,0:T(8,128)S(1)}, u32[]{:S(2)}, u32[]{:S(2)}) collective-permute-start(f32[256,128]{1,0:T(8,128)S(1)} %get-tuple-element.53), channel_id=1, source_target_pairs={{0,2},{1,3},{2,0},{3,1},{4,6},{5,7},{6,4},{7,5},{8,10},{9,11},{10,... | collective-permute-start | bytes 393224 | tf_op jit(solution)/shard_map/ppermute | solution.py:25
  38.8 0.3 collective-permute-start.9
  39.1 1.0 %collective-permute-done.4.refs_2_ = f32[256,128]{1,0:T(8,128)S(1)} collective-permute-done((f32[256,128]{1,0:T(8,128)S(1)}, f32[256,128]{1,0:T(8,128)S(1)}, u32[]{:S(2)}, u32[]{:S(2)}) %collective-permute-start.4) | collective-permute-done | bytes 131104 | tf_op jit(solution)/shard_map/ppermute | solution.py:25
  40.1 4.5 %merge_orth_1.1 = (f32[128,128]{1,0:T(8,128)S(1)}, f32[4,128,128]{2,1,0:T(8,128)S(1)}, f32[256,128]{1,0:T(8,128)S(1)}) custom-call(bf16[1,5,128,128]{3,2,1,0:T(8,128)(2,1)S(1)} %copy-done, f32[256,128]{1,0:T(8,128)S(1)} %get-tuple-element.46.refs_1_, f32[256,128]{1,0:T(8,128)S(1)} %collective-permute-done.4.refs_2_, ...), custom_call_target="tpu_custom_call" | custom-call | flops 80000000 | bytes 240000 | tf_op jit(solution)/shard_map/merge_orth_1/pallas_call | solution.py:389
  44.6 1.6 %collective-permute-start.6 = (f32[256,128]{1,0:T(8,128)S(1)}, f32[256,128]{1,0:T(8,128)S(1)}, u32[]{:S(2)}, u32[]{:S(2)}) collective-permute-start(f32[256,128]{1,0:T(8,128)S(1)} %get-tuple-element.51.refs_1_), channel_id=1, source_target_pairs={{0,4},{1,5},{2,6},{3,7},{4,0},{5,1},{6,2},{7,3},{8,12},{9,13},{10,... | collective-permute-start | bytes 393224 | tf_op jit(solution)/shard_map/ppermute | solution.py:25
  46.2 0.0 collective-permute-done.7.refs_1_
  46.2 0.0 collective-permute-done.8.refs_2_
  46.2 0.0 collective-permute-done.9.refs_3_
  46.2 0.5 upper_maps_1.1.refs_3_.refs_0_
  46.7 0.9 %collective-permute-start.11 = (f32[256,128]{1,0:T(8,128)S(1)}, f32[256,128]{1,0:T(8,128)S(1)}, u32[]{:S(2)}, u32[]{:S(2)}) collective-permute-start(f32[256,128]{1,0:T(8,128)S(1)} %upper_maps_1.1.refs_3_.refs_0_), channel_id=1, source_target_pairs={{0,4},{1,5},{2,6},{3,7},{4,0},{5,1},{6,2},{7,3},{8,12},{9,13},{10,... | collective-permute-start | bytes 393224 | tf_op jit(solution)/shard_map/ppermute | solution.py:25
  47.5 2.9 %collective-permute-done.6.refs_2_ = f32[256,128]{1,0:T(8,128)S(1)} collective-permute-done((f32[256,128]{1,0:T(8,128)S(1)}, f32[256,128]{1,0:T(8,128)S(1)}, u32[]{:S(2)}, u32[]{:S(2)}) %collective-permute-start.6) | collective-permute-done | bytes 131104 | tf_op jit(solution)/shard_map/ppermute | solution.py:25
  50.4 4.5 %merge_orth_2.1 = (f32[128,128]{1,0:T(8,128)S(1)}, f32[4,128,128]{2,1,0:T(8,128)S(1)}, f32[256,128]{1,0:T(8,128)S(1)}) custom-call(bf16[1,5,128,128]{3,2,1,0:T(8,128)(2,1)S(1)} %copy-done, f32[256,128]{1,0:T(8,128)S(1)} %get-tuple-element.51.refs_1_, f32[256,128]{1,0:T(8,128)S(1)} %collective-permute-done.6.refs_2_, f32[256,128]{1,0:T(8,128)S(1)} %upper_maps_1.1.refs_3_.refs_0_), custom_call_target="tpu_custom_call" | custom-call | flops 80000000 | bytes 240000 | tf_op jit(solution)/shard_map/merge_orth_2/pallas_call | solution.py:389
  54.9 1.7 %collective-permute-start.10 = (f32[256,128]{1,0:T(8,128)S(1)}, f32[256,128]{1,0:T(8,128)S(1)}, u32[]{:S(2)}, u32[]{:S(2)}) collective-permute-start(f32[256,128]{1,0:T(8,128)S(1)} %get-tuple-element.57), channel_id=1, source_target_pairs={{0,8},{1,9},{2,10},{3,11},{4,12},{5,13},{6,14},{7,15},{8,0},{9,1},... | collective-permute-start | bytes 393224 | tf_op jit(solution)/shard_map/ppermute | solution.py:25
  56.6 0.0 collective-permute-done.11.refs_1_
  56.6 0.5 upper_maps_2.1.refs_0_
  57.1 0.5 collective-permute-start.14
  57.6 2.4 %collective-permute-done.10 = f32[256,128]{1,0:T(8,128)S(1)} collective-permute-done((f32[256,128]{1,0:T(8,128)S(1)}, f32[256,128]{1,0:T(8,128)S(1)}, u32[]{:S(2)}, u32[]{:S(2)}) %collective-permute-start.10) | collective-permute-done | bytes 131104 | tf_op jit(solution)/shard_map/ppermute | solution.py:25
  60.0 4.7 %merge_orth_3.1 = (f32[5,128,128]{2,1,0:T(8,128)S(1)}, f32[256,128]{1,0:T(8,128)S(1)}, f32[128,128]{1,0:T(8,128)S(1)}, f32[4,128,128]{2,1,0:T(8,128)S(1)}) fusion(f32[5,128,128]{2,1,0:T(8,128)S(1)} %bitcast_dynamic-update-slice_fusion.2, bf16[1,5,128,128]{3,2,1,0:T(8,128)(2,1)S(1)} %copy-done, f32[256,128]{1,0:T(8,128)S(1)} %get-tuple-element.57, ...), kind=kCustom, calls=%fused_computation.3 | custom fusion | flops 80000000 | bytes 1081344 | tf_op jit(solution)/shard_map/merge_orth_3/pallas_call | solution.py:389
  64.7 2.7 %collective-permute-start.12 = (f32[128,128]{1,0:T(8,128)S(1)}, f32[128,128]{1,0:T(8,128)S(1)}, u32[]{:S(2)}, u32[]{:S(2)}) collective-permute-start(f32[128,128]{1,0:T(8,128)S(1)} %get-tuple-element.77), channel_id=1, source_target_pairs={{0,16},{1,17},{2,18},{3,19},{4,20},{5,21},{6,22},{7,23},{8,24},{9,... | collective-permute-start | bytes 196616 | tf_op jit(solution)/shard_map/ppermute | solution.py:25
  67.4 0.0 collective-permute-done.14.refs_1_
  67.4 0.5 upper_maps_3.1.own_ref
  67.9 0.4 collective-permute-start.15
  68.3 3.4 %collective-permute-done.12 = f32[128,128]{1,0:T(8,128)S(1)} collective-permute-done((f32[128,128]{1,0:T(8,128)S(1)}, f32[128,128]{1,0:T(8,128)S(1)}, u32[]{:S(2)}, u32[]{:S(2)}) %collective-permute-start.12) | collective-permute-done | bytes 65568 | tf_op jit(solution)/shard_map/ppermute | solution.py:25
  71.7 0.0 collective-permute-start.13
  71.7 1.3 %collective-permute-done.13 = f32[128,128]{1,0:T(8,128)S(1)} collective-permute-done((f32[128,128]{1,0:T(8,128)S(1)}, f32[128,128]{1,0:T(8,128)S(1)}, u32[]{:S(2)}, u32[]{:S(2)}) %collective-permute-start.13) | collective-permute-done | bytes 65568 | tf_op jit(solution)/shard_map/ppermute | solution.py:25
  72.9 4.4 %merge_orth_4.1 = (f32[5,128,128]{2,1,0:T(8,128)S(1)}, f32[128,256]{1,0:T(8,128)S(1)}, f32[8,128]{1,0:T(8,128)}) fusion(f32[5,128,128]{2,1,0:T(8,128)S(1)} %get-tuple-element.74, bf16[1,5,128,128]{3,2,1,0:T(8,128)(2,1)S(1)} %copy-done, f32[256,128]{1,0:T(8,128)S(1)} %get-tuple-element.75, f32[128,128]{1,0:T(8,128)S(1)} %collective-permute-done.12, ...), kind=kCustom, calls=%fused_computation.2 | custom fusion | flops 80000000 | bytes 757760 | tf_op jit(solution)/shard_map/merge_orth_4/pallas_call | solution.py:389
  77.3 0.0 copy-start.4
  77.4 0.0 collective-permute-done.15.other_ref
  77.4 0.6 top_sample.1.refs_0_
  77.9 0.2 collective-permute-start.16
  78.2 2.7 %collective-permute-start.17 = (f32[128,128]{1,0:T(8,128)S(1)}, f32[128,128]{1,0:T(8,128)S(1)}, u32[]{:S(2)}, u32[]{:S(2)}) collective-permute-start(f32[128,128]{1,0:T(8,128)S(1)} %top_sample.1.refs_0_), channel_id=1, source_target_pairs={{0,2},{1,3},{2,0},{3,1},{4,6},{5,7},{6,4},{7,5},{8,10},{9,11},{10,... | collective-permute-start | bytes 196616 | tf_op jit(solution)/shard_map/ppermute | solution.py:25
  80.8 0.0 collective-permute-start.18
  80.8 0.0 collective-permute-done.16.refs_1_
  80.8 2.6 %collective-permute-done.17.refs_2_ = f32[128,128]{1,0:T(8,128)S(1)} collective-permute-done((f32[128,128]{1,0:T(8,128)S(1)}, f32[128,128]{1,0:T(8,128)S(1)}, u32[]{:S(2)}, u32[]{:S(2)}) %collective-permute-start.17) | collective-permute-done | bytes 65568 | tf_op jit(solution)/shard_map/ppermute | solution.py:25
  83.4 1.6 %collective-permute-done.18.refs_3_ = f32[128,128]{1,0:T(8,128)S(1)} collective-permute-done((f32[128,128]{1,0:T(8,128)S(1)}, f32[128,128]{1,0:T(8,128)S(1)}, u32[]{:S(2)}, u32[]{:S(2)}) %collective-permute-start.18) | collective-permute-done | bytes 65568 | tf_op jit(solution)/shard_map/ppermute | solution.py:25
  85.0 0.7 top_columns.1
  85.7 0.0 copy-done.4
  (5 shorter events, 0.0 us)
Async XLA Ops:
  0.6 12.0 %copy-start.2 = (f32[512,128]{1,0:T(8,128)S(1)}, f32[512,128]{1,0:T(8,128)}, u32[]{:S(2)}) copy-start(f32[512,128]{1,0:T(8,128)} %refs_0_.8) | copy-start | bytes 786436
  0.6 13.2 %copy-start.1 = (bf16[256,512]{1,0:T(8,128)(2,1)S(1)}, bf16[256,512]{1,0:T(8,128)(2,1)}, u32[]{:S(2)}) copy-start(bf16[256,512]{1,0:T(8,128)(2,1)} %refs_3_.1) | copy-start | bytes 786436
  0.7 0.7 copy-start.3
  12.6 17.2 %copy-start = (bf16[1,5,128,128]{3,2,1,0:T(8,128)(2,1)S(1)}, bf16[1,5,128,128]{3,2,1,0:T(8,128)(2,1)}, u32[]{:S(2)}) copy-start(bf16[1,5,128,128]{3,2,1,0:T(8,128)(2,1)} %coupling_ref.1) | copy-start | bytes 491524
  13.3 1.7 %collective-permute-start = (f32[512,128]{1,0:T(8,128)S(1)}, f32[512,128]{1,0:T(8,128)S(1)}, u32[]{:S(2)}, u32[]{:S(2)}) collective-permute-start(f32[512,128]{1,0:T(8,128)S(1)} %reduced_1.1), channel_id=1, source_target_pairs={{0,1},{1,0},{2,3},{3,2},{4,5},{5,4},{6,7},{7,6},{8,9},{9,8},{10,11... | collective-permute-start | bytes 786440 | tf_op jit(solution)/shard_map/ppermute | solution.py:25
  15.0 3.1 %collective-permute-start.1 = (f32[512,512]{1,0:T(8,128)S(1)}, f32[512,512]{1,0:T(8,128)S(1)}, u32[]{:S(2)}, u32[]{:S(2)}) collective-permute-start(f32[512,512]{1,0:T(8,128)S(1)} %get-tuple-element.37.refs_1_), channel_id=1, source_target_pairs={{0,1},{1,0},{2,3},{3,2},{4,5},{5,4},{6,7},{7,6},{8,9},{9,8},{10,11... | collective-permute-start | bytes 3145736 | tf_op jit(solution)/shard_map/ppermute | solution.py:25
  15.5 6.7 %collective-permute-start.2 = (f32[256,128]{1,0:T(8,128)S(1)}, f32[256,128]{1,0:T(8,128)S(1)}, u32[]{:S(2)}, u32[]{:S(2)}) collective-permute-start(f32[256,128]{1,0:T(8,128)S(1)} %slice_add_fusion.1), channel_id=1, source_target_pairs={{0,2},{1,3},{2,0},{3,1},{4,6},{5,7},{6,4},{7,5},{8,10},{9,11},{10,... | collective-permute-start | bytes 393224 | tf_op jit(solution)/shard_map/ppermute | solution.py:25
  22.2 13.6 %collective-permute-start.5 = (f32[256,512]{1,0:T(8,128)S(1)}, f32[256,512]{1,0:T(8,128)S(1)}, u32[]{:S(2)}, u32[]{:S(2)}) collective-permute-start(f32[256,512]{1,0:T(8,128)S(1)} %slice_add_fusion._), channel_id=1, source_target_pairs={{0,2},{1,3},{2,0},{3,1},{4,6},{5,7},{6,4},{7,5},{8,10},{9,11},{10,... | collective-permute-start | bytes 1572872 | tf_op jit(solution)/shard_map/ppermute | solution.py:25
  28.4 1.4 %collective-permute-start.3 = (f32[256,128]{1,0:T(8,128)S(1)}, f32[256,128]{1,0:T(8,128)S(1)}, u32[]{:S(2)}, u32[]{:S(2)}) collective-permute-start(f32[256,128]{1,0:T(8,128)S(1)} %get-tuple-element.44.refs_1_), channel_id=1, source_target_pairs={{0,1},{1,0},{2,3},{3,2},{4,5},{5,4},{6,7},{7,6},{8,9},{9,8},{10,11... | collective-permute-start | bytes 393224 | tf_op jit(solution)/shard_map/ppermute | solution.py:25
  34.4 5.6 %collective-permute-start.4 = (f32[256,128]{1,0:T(8,128)S(1)}, f32[256,128]{1,0:T(8,128)S(1)}, u32[]{:S(2)}, u32[]{:S(2)}) collective-permute-start(f32[256,128]{1,0:T(8,128)S(1)} %get-tuple-element.46.refs_1_), channel_id=1, source_target_pairs={{0,2},{1,3},{2,0},{3,1},{4,6},{5,7},{6,4},{7,5},{8,10},{9,11},{10,... | collective-permute-start | bytes 393224 | tf_op jit(solution)/shard_map/ppermute | solution.py:25
  37.2 9.0 %collective-permute-start.7 = (f32[256,128]{1,0:T(8,128)S(1)}, f32[256,128]{1,0:T(8,128)S(1)}, u32[]{:S(2)}, u32[]{:S(2)}) collective-permute-start(f32[256,128]{1,0:T(8,128)S(1)} %get-tuple-element.52), channel_id=1, source_target_pairs={{0,1},{1,0},{2,3},{3,2},{4,5},{5,4},{6,7},{7,6},{8,9},{9,8},{10,11... | collective-permute-start | bytes 393224 | tf_op jit(solution)/shard_map/ppermute | solution.py:25
  37.2 8.9 %collective-permute-start.8 = (f32[256,128]{1,0:T(8,128)S(1)}, f32[256,128]{1,0:T(8,128)S(1)}, u32[]{:S(2)}, u32[]{:S(2)}) collective-permute-start(f32[256,128]{1,0:T(8,128)S(1)} %get-tuple-element.53), channel_id=1, source_target_pairs={{0,2},{1,3},{2,0},{3,1},{4,6},{5,7},{6,4},{7,5},{8,10},{9,11},{10,... | collective-permute-start | bytes 393224 | tf_op jit(solution)/shard_map/ppermute | solution.py:25
  38.8 7.4 %collective-permute-start.9 = (f32[256,128]{1,0:T(8,128)S(1)}, f32[256,128]{1,0:T(8,128)S(1)}, u32[]{:S(2)}, u32[]{:S(2)}) collective-permute-start(f32[256,128]{1,0:T(8,128)S(1)} %get-tuple-element.54), channel_id=1, source_target_pairs={{0,3},{1,2},{2,1},{3,0},{4,7},{5,6},{6,5},{7,4},{8,11},{9,10},{10,... | collective-permute-start | bytes 393224 | tf_op jit(solution)/shard_map/ppermute | solution.py:25
  44.6 5.8 %collective-permute-start.6 = (f32[256,128]{1,0:T(8,128)S(1)}, f32[256,128]{1,0:T(8,128)S(1)}, u32[]{:S(2)}, u32[]{:S(2)}) collective-permute-start(f32[256,128]{1,0:T(8,128)S(1)} %get-tuple-element.51.refs_1_), channel_id=1, source_target_pairs={{0,4},{1,5},{2,6},{3,7},{4,0},{5,1},{6,2},{7,3},{8,12},{9,13},{10,... | collective-permute-start | bytes 393224 | tf_op jit(solution)/shard_map/ppermute | solution.py:25
  46.7 9.9 %collective-permute-start.11 = (f32[256,128]{1,0:T(8,128)S(1)}, f32[256,128]{1,0:T(8,128)S(1)}, u32[]{:S(2)}, u32[]{:S(2)}) collective-permute-start(f32[256,128]{1,0:T(8,128)S(1)} %upper_maps_1.1.refs_3_.refs_0_), channel_id=1, source_target_pairs={{0,4},{1,5},{2,6},{3,7},{4,0},{5,1},{6,2},{7,3},{8,12},{9,13},{10,... | collective-permute-start | bytes 393224 | tf_op jit(solution)/shard_map/ppermute | solution.py:25
  54.9 5.0 %collective-permute-start.10 = (f32[256,128]{1,0:T(8,128)S(1)}, f32[256,128]{1,0:T(8,128)S(1)}, u32[]{:S(2)}, u32[]{:S(2)}) collective-permute-start(f32[256,128]{1,0:T(8,128)S(1)} %get-tuple-element.57), channel_id=1, source_target_pairs={{0,8},{1,9},{2,10},{3,11},{4,12},{5,13},{6,14},{7,15},{8,0},{9,1},... | collective-permute-start | bytes 393224 | tf_op jit(solution)/shard_map/ppermute | solution.py:25
  57.1 10.3 %collective-permute-start.14 = (f32[256,128]{1,0:T(8,128)S(1)}, f32[256,128]{1,0:T(8,128)S(1)}, u32[]{:S(2)}, u32[]{:S(2)}) collective-permute-start(f32[256,128]{1,0:T(8,128)S(1)} %upper_maps_2.1.refs_0_), channel_id=1, source_target_pairs={{0,8},{1,9},{2,10},{3,11},{4,12},{5,13},{6,14},{7,15},{8,0},{9,1},... | collective-permute-start | bytes 393224 | tf_op jit(solution)/shard_map/ppermute | solution.py:25
  64.7 7.0 %collective-permute-start.12 = (f32[128,128]{1,0:T(8,128)S(1)}, f32[128,128]{1,0:T(8,128)S(1)}, u32[]{:S(2)}, u32[]{:S(2)}) collective-permute-start(f32[128,128]{1,0:T(8,128)S(1)} %get-tuple-element.77), channel_id=1, source_target_pairs={{0,16},{1,17},{2,18},{3,19},{4,20},{5,21},{6,22},{7,23},{8,24},{9,... | collective-permute-start | bytes 196616 | tf_op jit(solution)/shard_map/ppermute | solution.py:25
  67.9 9.5 %collective-permute-start.15 = (f32[256,128]{1,0:T(8,128)S(1)}, f32[256,128]{1,0:T(8,128)S(1)}, u32[]{:S(2)}, u32[]{:S(2)}) collective-permute-start(f32[256,128]{1,0:T(8,128)S(1)} %upper_maps_3.1.own_ref), channel_id=1, source_target_pairs={{0,16},{1,17},{2,18},{3,19},{4,20},{5,21},{6,22},{7,23},{8,24},{9,... | collective-permute-start | bytes 393224 | tf_op jit(solution)/shard_map/ppermute | solution.py:25
  71.7 1.3 %collective-permute-start.13 = (f32[128,128]{1,0:T(8,128)S(1)}, f32[128,128]{1,0:T(8,128)S(1)}, u32[]{:S(2)}, u32[]{:S(2)}) collective-permute-start(f32[128,128]{1,0:T(8,128)S(1)} %collective-permute-done.12), channel_id=1, source_target_pairs={{0,1},{1,0},{2,3},{3,2},{4,5},{5,4},{6,7},{7,6},{8,9},{9,8},{10,11... | collective-permute-start | bytes 196616 | tf_op jit(solution)/shard_map/ppermute | solution.py:25
  77.3 8.4 %copy-start.4 = (f32[5,128,128]{2,1,0:T(8,128)}, f32[5,128,128]{2,1,0:T(8,128)S(1)}, u32[]{:S(2)}) copy-start(f32[5,128,128]{2,1,0:T(8,128)S(1)} %get-tuple-element.68) | copy-start | bytes 983044
  77.9 2.9 %collective-permute-start.16 = (f32[128,128]{1,0:T(8,128)S(1)}, f32[128,128]{1,0:T(8,128)S(1)}, u32[]{:S(2)}, u32[]{:S(2)}) collective-permute-start(f32[128,128]{1,0:T(8,128)S(1)} %top_sample.1.refs_0_), channel_id=1, source_target_pairs={{0,1},{1,0},{2,3},{3,2},{4,5},{5,4},{6,7},{7,6},{8,9},{9,8},{10,11... | collective-permute-start | bytes 196616 | tf_op jit(solution)/shard_map/ppermute | solution.py:25
  78.2 5.3 %collective-permute-start.17 = (f32[128,128]{1,0:T(8,128)S(1)}, f32[128,128]{1,0:T(8,128)S(1)}, u32[]{:S(2)}, u32[]{:S(2)}) collective-permute-start(f32[128,128]{1,0:T(8,128)S(1)} %top_sample.1.refs_0_), channel_id=1, source_target_pairs={{0,2},{1,3},{2,0},{3,1},{4,6},{5,7},{6,4},{7,5},{8,10},{9,11},{10,... | collective-permute-start | bytes 196616 | tf_op jit(solution)/shard_map/ppermute | solution.py:25
  80.8 4.2 %collective-permute-start.18 = (f32[128,128]{1,0:T(8,128)S(1)}, f32[128,128]{1,0:T(8,128)S(1)}, u32[]{:S(2)}, u32[]{:S(2)}) collective-permute-start(f32[128,128]{1,0:T(8,128)S(1)} %top_sample.1.refs_0_), channel_id=1, source_target_pairs={{0,3},{1,2},{2,1},{3,0},{4,7},{5,6},{6,5},{7,4},{8,11},{9,10},{10,... | collective-permute-start | bytes 196616 | tf_op jit(solution)/shard_map/ppermute | solution.py:25

commit v7 on v6

--- a/solution.py
+++ b/solution.py
@@ -303,24 +303,24 @@
     )(keep, first, second, sketch_red, after)
 
 
-def basis_body(basis_t_ref, basis_ref, mark_ref):
+def basis_body(basis_t_ref, _, basis_ref, mark_ref):
     basis_ref[...] = basis_t_ref[...].T
     mark_ref[...] = jnp.zeros_like(mark_ref)
 
 
-def basis_step(basis_t):
+def basis_step(basis_t, after):
     return pl.pallas_call(
         basis_body,
         out_shape=[
             jax.ShapeDtypeStruct(basis_t.shape[::-1], jnp.float32),
             jax.ShapeDtypeStruct((8, 128), jnp.float32),
         ],
-        in_specs=[VMEM],
+        in_specs=[VMEM, ANY],
         out_specs=[VMEM] * 2,
         compiler_params=small_params(),
         cost_estimate=small_cost(1),
         name="leaf_basis",
-    )(basis_t)
+    )(basis_t, after)
 
 
 def position():
@@ -551,8 +551,8 @@
             others = [from_partner(pair, ROW_COL, 2**tree_level)]
         else:
             others = [waiting, from_partner(waiting, ROW_COL, 1)]
-        if tree_level == 1:
-            leaf_basis, mark = basis_step(basis_t)
+        if tree_level == LEVELS - 2:
+            leaf_basis, mark = basis_step(basis_t, after[0])
             after = after + [mark]
         sides = 1 if tree_level < col_bits - 1 else 2
         block, maps, pair, *half = merge_step(tree_level, pair, others, couplings, sides, after)
@@ -566,6 +566,8 @@
         else:
             total = upper_step(tree_level, own, other, maps)
             own = [total]
+            if tree_level == LEVELS - 2:
+                total, waiting = lax.optimization_barrier((total, waiting))
             other = [from_partner(total, ROW_COL, 2 ** (tree_level + 1))]
             after = [total]
         if tree_level == col_bits - 2:

time: 86.1 us -> 88.3 us (1.026)
  waiting for transfers between devices: 20.8 us -> 23 us
    ppermute x19, waiting for transfers between devices: 20.8 us -> 23 us  [from_partner(): return lax.ppermute(block, axis, route)]
  transfers between devices with their start and end apart: 19 -> 19, of which waited for: 11 -> 12; matrix products, arithmetic and copies ran while one was open for 11% -> 10% of each run, Pallas kernels for 26% -> 26%
where the time goes in v7:
time: 88.3 us; the launch traced here: 88.1 us
  Pallas kernels  35.8 us (41%)
  waiting for transfers between devices  23 us (26%)
  starting transfers between devices  18.2 us (21%)
  other arithmetic  9.24 us (10%)
  between operations  1.01 us (1%)
    ppermute x19, waiting for transfers between devices, from_partner(): return lax.ppermute(block, axis, route)  23 us
    ppermute x19, starting transfers between devices, from_partner(): return lax.ppermute(block, axis, route)  18.2 us
    pallas_call x3, Pallas kernels, merge_step(): pl.pallas_call(functools.partial(merge_body, tree_level), grid=(1,), out_...  13.7 us
    pallas_call x1, Pallas kernels, sample_rows(): pl.pallas_call(functools.partial(spmm_body, leaves=leaves), out_shape=[ja...  11.2 us
    pallas_call x2, other arithmetic, merge_step(): pl.pallas_call(functools.partial(merge_body, tree_level), grid=(1,), out_...  9.15 us
    pallas_call x1, Pallas kernels, leaf_step(): pl.pallas_call(leaf_body, grid=(1,), out_shape=[jax.ShapeDtypeStruct((ran...  4.49 us
  transfers between devices with their start and end apart: 19, of which 12 were waited for; matrix products, arithmetic and copies ran while one was open for 10% of the time, Pallas kernels for 26%

profile of v7, /device:TPU:0, one launch (start us, length us, event | category | flops | bytes accessed | tf_op | source)
XLA Modules:
  0.0 88.1 jit_solution(7942230542026895341)
XLA Ops:
  0.6 0.0 copy-start.2
  0.6 0.0 copy-start.1
  0.7 0.0 copy-start.3
  0.7 0.7 copy-done.3
  1.4 11.2 %spmm.1 = (f32[512,512]{1,0:T(8,128)S(1)}, f32[512,512]{1,0:T(8,128)S(1)}) custom-call(s32[168]{0:T(256)S(1)} %copy-done.3, bf16[168,128,128]{2,1,0:T(8,128)(2,1)} %tiles_ref.1, bf16[6144,512]{1,0:T(8,128)(2,1)} %sketch_ref.1), custom_call_target="tpu_custom_call" | custom-call | flops 6442450944 | bytes 13893632 | tf_op jit(solution)/shard_map/spmm/pallas_call | solution.py:215
  12.6 0.0 copy-start
  12.6 0.0 copy-done.2
  12.6 0.7 reduced_1.1
  13.3 0.5 collective-permute-start
  13.9 0.0 copy-done.1
  13.9 0.9 reduced_2.1
  14.7 0.3 collective-permute-done.first_ref
  15.0 0.4 collective-permute-start.1
  15.5 2.7 %collective-permute-start.2 = (f32[256,128]{1,0:T(8,128)S(1)}, f32[256,128]{1,0:T(8,128)S(1)}, u32[]{:S(2)}, u32[]{:S(2)}) collective-permute-start(f32[256,128]{1,0:T(8,128)S(1)} %slice_add_fusion.1), channel_id=1, source_target_pairs={{0,2},{1,3},{2,0},{3,1},{4,6},{5,7},{6,4},{7,5},{8,10},{9,11},{10,... | collective-permute-start | bytes 393224 | tf_op jit(solution)/shard_map/ppermute | solution.py:25
  18.1 0.0 collective-permute-done.1.refs_1_
  18.1 0.1 slice_add_fusion._
  18.2 3.9 %collective-permute-done.2.second_ref = f32[256,128]{1,0:T(8,128)S(1)} collective-permute-done((f32[256,128]{1,0:T(8,128)S(1)}, f32[256,128]{1,0:T(8,128)S(1)}, u32[]{:S(2)}, u32[]{:S(2)}) %collective-permute-start.2) | collective-permute-done | bytes 131104 | tf_op jit(solution)/shard_map/ppermute | solution.py:25
  22.2 1.7 %collective-permute-start.3 = (f32[256,512]{1,0:T(8,128)S(1)}, f32[256,512]{1,0:T(8,128)S(1)}, u32[]{:S(2)}, u32[]{:S(2)}) collective-permute-start(f32[256,512]{1,0:T(8,128)S(1)} %slice_add_fusion._), channel_id=1, source_target_pairs={{0,2},{1,3},{2,0},{3,1},{4,6},{5,7},{6,4},{7,5},{8,10},{9,11},{10,... | collective-permute-start | bytes 1572872 | tf_op jit(solution)/shard_map/ppermute | solution.py:25
  23.9 4.5 %leaf_orth.1 = (f32[128,256]{1,0:T(8,128)S(1)}, f32[256,128]{1,0:T(8,128)S(1)}) custom-call(f32[512,128]{1,0:T(8,128)S(1)} %get-tuple-element.37.keep_ref, f32[512,128]{1,0:T(8,128)S(1)} %collective-permute-done.first_ref, f32[256,128]{1,0:T(8,128)S(1)} %collective-permute-done.2.second_ref, f32[256,128]{1,0:T(8,128)S(1)} %get-tuple-element.42.sketch_red_ref, ...), custom_call_target="tpu_custom_call" | custom-call | flops 80000000 | bytes 240000 | tf_op jit(solution)/shard_map/leaf_orth/pallas_call | solution.py:291
  28.4 0.1 collective-permute-start.4
  28.5 1.3 %collective-permute-done.4.refs_2_ = f32[256,128]{1,0:T(8,128)S(1)} collective-permute-done((f32[256,128]{1,0:T(8,128)S(1)}, f32[256,128]{1,0:T(8,128)S(1)}, u32[]{:S(2)}, u32[]{:S(2)}) %collective-permute-start.4) | collective-permute-done | bytes 131104 | tf_op jit(solution)/shard_map/ppermute | solution.py:25
  29.8 0.0 copy-done
  29.8 4.6 %merge_orth_0.1 = (f32[128,128]{1,0:T(8,128)S(1)}, f32[2,128,128]{2,1,0:T(8,128)S(1)}, f32[256,128]{1,0:T(8,128)S(1)}) custom-call(bf16[1,5,128,128]{3,2,1,0:T(8,128)(2,1)S(1)} %copy-done, f32[256,128]{1,0:T(8,128)S(1)} %get-tuple-element.45.refs_1_, f32[256,128]{1,0:T(8,128)S(1)} %collective-permute-done.4.refs_2_), custom_call_target="tpu_custom_call" | custom-call | flops 80000000 | bytes 240000 | tf_op jit(solution)/shard_map/merge_orth_0/pallas_call | solution.py:389
  34.4 0.3 collective-permute-start.8
  34.8 1.0 %collective-permute-done.3.refs_2_ = f32[256,512]{1,0:T(8,128)S(1)} collective-permute-done((f32[256,512]{1,0:T(8,128)S(1)}, f32[256,512]{1,0:T(8,128)S(1)}, u32[]{:S(2)}, u32[]{:S(2)}) %collective-permute-start.3) | collective-permute-done | bytes 524320 | tf_op jit(solution)/shard_map/ppermute | solution.py:25
  35.8 1.4 %lower_maps.1 = (f32[256,128]{1,0:T(8,128)S(1)}, f32[256,128]{1,0:T(8,128)S(1)}, f32[256,128]{1,0:T(8,128)S(1)}, f32[256,128]{1,0:T(8,128)S(1)}) custom-call(f32[512,512]{1,0:T(8,128)S(1)} %get-tuple-element.36.refs_1_.refs_0_, f32[512,512]{1,0:T(8,128)S(1)} %collective-permute-done.1.refs_1_, f32[256,512]{1,0:T(8,128)S(1)} %collective-permute-done.3.refs_2_, ...), custom_call_target="tpu_custom_call" | custom-call | flops 20000000 | bytes 60000 | tf_op jit(solution)/shard_map/lower_maps/pallas_call | solution.py:434
  37.2 0.1 collective-permute-start.5
  37.2 1.6 %collective-permute-start.6 = (f32[256,128]{1,0:T(8,128)S(1)}, f32[256,128]{1,0:T(8,128)S(1)}, u32[]{:S(2)}, u32[]{:S(2)}) collective-permute-start(f32[256,128]{1,0:T(8,128)S(1)} %get-tuple-element.49), channel_id=1, source_target_pairs={{0,2},{1,3},{2,0},{3,1},{4,6},{5,7},{6,4},{7,5},{8,10},{9,11},{10,... | collective-permute-start | bytes 393224 | tf_op jit(solution)/shard_map/ppermute | solution.py:25
  38.8 0.3 collective-permute-start.7
  39.1 0.9 %collective-permute-done.8.refs_2_ = f32[256,128]{1,0:T(8,128)S(1)} collective-permute-done((f32[256,128]{1,0:T(8,128)S(1)}, f32[256,128]{1,0:T(8,128)S(1)}, u32[]{:S(2)}, u32[]{:S(2)}) %collective-permute-start.8) | collective-permute-done | bytes 131104 | tf_op jit(solution)/shard_map/ppermute | solution.py:25
  40.0 4.5 %merge_orth_1.1 = (f32[128,128]{1,0:T(8,128)S(1)}, f32[4,128,128]{2,1,0:T(8,128)S(1)}, f32[256,128]{1,0:T(8,128)S(1)}) custom-call(bf16[1,5,128,128]{3,2,1,0:T(8,128)(2,1)S(1)} %copy-done, f32[256,128]{1,0:T(8,128)S(1)} %get-tuple-element.51.refs_1_, f32[256,128]{1,0:T(8,128)S(1)} %collective-permute-done.8.refs_2_, ...), custom_call_target="tpu_custom_call" | custom-call | flops 80000000 | bytes 240000 | tf_op jit(solution)/shard_map/merge_orth_1/pallas_call | solution.py:389
  44.6 1.6 %collective-permute-start.10 = (f32[256,128]{1,0:T(8,128)S(1)}, f32[256,128]{1,0:T(8,128)S(1)}, u32[]{:S(2)}, u32[]{:S(2)}) collective-permute-start(f32[256,128]{1,0:T(8,128)S(1)} %get-tuple-element.53.refs_1_), channel_id=1, source_target_pairs={{0,4},{1,5},{2,6},{3,7},{4,0},{5,1},{6,2},{7,3},{8,12},{9,13},{10,... | collective-permute-start | bytes 393224 | tf_op jit(solution)/shard_map/ppermute | solution.py:25
  46.1 0.0 collective-permute-done.5.refs_1_
  46.1 0.0 collective-permute-done.6.refs_2_
  46.1 0.0 collective-permute-done.7.refs_3_
  46.2 0.5 upper_maps_1.1.refs_3_.refs_0_
  46.6 0.9 collective-permute-start.9
  47.5 2.8 %collective-permute-done.10.refs_2_ = f32[256,128]{1,0:T(8,128)S(1)} collective-permute-done((f32[256,128]{1,0:T(8,128)S(1)}, f32[256,128]{1,0:T(8,128)S(1)}, u32[]{:S(2)}, u32[]{:S(2)}) %collective-permute-start.10) | collective-permute-done | bytes 131104 | tf_op jit(solution)/shard_map/ppermute | solution.py:25
  50.4 4.5 %merge_orth_2.1 = (f32[128,128]{1,0:T(8,128)S(1)}, f32[4,128,128]{2,1,0:T(8,128)S(1)}, f32[256,128]{1,0:T(8,128)S(1)}) custom-call(bf16[1,5,128,128]{3,2,1,0:T(8,128)(2,1)S(1)} %copy-done, f32[256,128]{1,0:T(8,128)S(1)} %get-tuple-element.53.refs_1_, f32[256,128]{1,0:T(8,128)S(1)} %collective-permute-done.10.refs_2_, f32[256,128]{1,0:T(8,128)S(1)} %upper_maps_1.1.refs_3_.refs_0_), custom_call_target="tpu_custom_call" | custom-call | flops 80000000 | bytes 240000 | tf_op jit(solution)/shard_map/merge_orth_2/pallas_call | solution.py:389
  54.9 1.7 %collective-permute-start.11 = (f32[256,128]{1,0:T(8,128)S(1)}, f32[256,128]{1,0:T(8,128)S(1)}, u32[]{:S(2)}, u32[]{:S(2)}) collective-permute-start(f32[256,128]{1,0:T(8,128)S(1)} %get-tuple-element.59), channel_id=1, source_target_pairs={{0,8},{1,9},{2,10},{3,11},{4,12},{5,13},{6,14},{7,15},{8,0},{9,1},... | collective-permute-start | bytes 393224 | tf_op jit(solution)/shard_map/ppermute | solution.py:25
  56.6 0.0 collective-permute-done.9.refs_1_
  56.6 0.5 upper_maps_2.1._.refs_0_
  57.1 0.5 collective-permute-start.12
  57.5 0.8 leaf_basis.1
  58.3 1.6 %collective-permute-done.11 = f32[256,128]{1,0:T(8,128)S(1)} collective-permute-done((f32[256,128]{1,0:T(8,128)S(1)}, f32[256,128]{1,0:T(8,128)S(1)}, u32[]{:S(2)}, u32[]{:S(2)}) %collective-permute-start.11) | collective-permute-done | bytes 131104 | tf_op jit(solution)/shard_map/ppermute | solution.py:25
  59.9 4.7 %merge_orth_3.1 = (f32[5,128,128]{2,1,0:T(8,128)S(1)}, f32[256,128]{1,0:T(8,128)S(1)}, f32[4,128,128]{2,1,0:T(8,128)S(1)}, f32[128,128]{1,0:T(8,128)S(1)}) fusion(f32[5,128,128]{2,1,0:T(8,128)S(1)} %bitcast_dynamic-update-slice_fusion.2, bf16[1,5,128,128]{3,2,1,0:T(8,128)(2,1)S(1)} %copy-done, f32[256,128]{1,0:T(8,128)S(1)} %get-tuple-element.59, ...), kind=kCustom, calls=%fused_computation.3 | custom fusion | flops 80000000 | bytes 1085440 | tf_op jit(solution)/shard_map/merge_orth_3/pallas_call | solution.py:389
  64.7 2.7 %collective-permute-start.13 = (f32[128,128]{1,0:T(8,128)S(1)}, f32[128,128]{1,0:T(8,128)S(1)}, u32[]{:S(2)}, u32[]{:S(2)}) collective-permute-start(f32[128,128]{1,0:T(8,128)S(1)} %get-tuple-element.76), channel_id=1, source_target_pairs={{0,16},{1,17},{2,18},{3,19},{4,20},{5,21},{6,22},{7,23},{8,24},{9,... | collective-permute-start | bytes 196616 | tf_op jit(solution)/shard_map/ppermute | solution.py:25
  67.4 0.0 collective-permute-done.12.refs_1_
  67.4 0.5 upper_maps_3.1.own_ref
  67.8 4.8 %collective-permute-done.13 = f32[128,128]{1,0:T(8,128)S(1)} collective-permute-done((f32[128,128]{1,0:T(8,128)S(1)}, f32[128,128]{1,0:T(8,128)S(1)}, u32[]{:S(2)}, u32[]{:S(2)}) %collective-permute-start.13) | collective-permute-done | bytes 65568 | tf_op jit(solution)/shard_map/ppermute | solution.py:25
  72.7 0.6 collective-permute-start.15
  73.3 0.0 collective-permute-start.14
  73.3 1.3 %collective-permute-done.14 = f32[128,128]{1,0:T(8,128)S(1)} collective-permute-done((f32[128,128]{1,0:T(8,128)S(1)}, f32[128,128]{1,0:T(8,128)S(1)}, u32[]{:S(2)}, u32[]{:S(2)}) %collective-permute-start.14) | collective-permute-done | bytes 65568 | tf_op jit(solution)/shard_map/ppermute | solution.py:25
  74.5 4.4 %merge_orth_4.1 = (f32[5,128,128]{2,1,0:T(8,128)S(1)}, f32[128,256]{1,0:T(8,128)S(1)}, f32[8,128]{1,0:T(8,128)}) fusion(f32[5,128,128]{2,1,0:T(8,128)S(1)} %get-tuple-element.71, bf16[1,5,128,128]{3,2,1,0:T(8,128)(2,1)S(1)} %copy-done, f32[256,128]{1,0:T(8,128)S(1)} %get-tuple-element.72, f32[128,128]{1,0:T(8,128)S(1)} %collective-permute-done.13, ...), kind=kCustom, calls=%fused_computation.2 | custom fusion | flops 80000000 | bytes 757760 | tf_op jit(solution)/shard_map/merge_orth_4/pallas_call | solution.py:389
  78.9 0.0 copy-start.4
  78.9 1.0 %collective-permute-done.15.other_ref = f32[256,128]{1,0:T(8,128)S(1)} collective-permute-done((f32[256,128]{1,0:T(8,128)S(1)}, f32[256,128]{1,0:T(8,128)S(1)}, u32[]{:S(2)}, u32[]{:S(2)}) %collective-permute-start.15) | collective-permute-done | bytes 131104 | tf_op jit(solution)/shard_map/ppermute | solution.py:25
  79.9 0.6 top_sample.1.refs_0_
  80.5 0.1 collective-permute-start.16
  80.6 2.5 %collective-permute-start.17 = (f32[128,128]{1,0:T(8,128)S(1)}, f32[128,128]{1,0:T(8,128)S(1)}, u32[]{:S(2)}, u32[]{:S(2)}) collective-permute-start(f32[128,128]{1,0:T(8,128)S(1)} %top_sample.1.refs_0_), channel_id=1, source_target_pairs={{0,2},{1,3},{2,0},{3,1},{4,6},{5,7},{6,4},{7,5},{8,10},{9,11},{10,... | collective-permute-start | bytes 196616 | tf_op jit(solution)/shard_map/ppermute | solution.py:25
  83.1 0.1 collective-permute-start.18
  83.2 0.0 collective-permute-done.16.refs_1_
  83.2 2.6 %collective-permute-done.17.refs_2_ = f32[128,128]{1,0:T(8,128)S(1)} collective-permute-done((f32[128,128]{1,0:T(8,128)S(1)}, f32[128,128]{1,0:T(8,128)S(1)}, u32[]{:S(2)}, u32[]{:S(2)}) %collective-permute-start.17) | collective-permute-done | bytes 65568 | tf_op jit(solution)/shard_map/ppermute | solution.py:25
  85.8 1.4 %collective-permute-done.18.refs_3_ = f32[128,128]{1,0:T(8,128)S(1)} collective-permute-done((f32[128,128]{1,0:T(8,128)S(1)}, f32[128,128]{1,0:T(8,128)S(1)}, u32[]{:S(2)}, u32[]{:S(2)}) %collective-permute-start.18) | collective-permute-done | bytes 65568 | tf_op jit(solution)/shard_map/ppermute | solution.py:25
  87.1 0.7 top_columns.1
  (5 shorter events, 0.0 us)
Async XLA Ops:
  0.6 12.0 %copy-start.2 = (f32[512,128]{1,0:T(8,128)S(1)}, f32[512,128]{1,0:T(8,128)}, u32[]{:S(2)}) copy-start(f32[512,128]{1,0:T(8,128)} %refs_0_.8) | copy-start | bytes 786436
  0.6 13.2 %copy-start.1 = (bf16[256,512]{1,0:T(8,128)(2,1)S(1)}, bf16[256,512]{1,0:T(8,128)(2,1)}, u32[]{:S(2)}) copy-start(bf16[256,512]{1,0:T(8,128)(2,1)} %refs_3_.1) | copy-start | bytes 786436
  0.7 0.7 copy-start.3
  12.6 17.2 %copy-start = (bf16[1,5,128,128]{3,2,1,0:T(8,128)(2,1)S(1)}, bf16[1,5,128,128]{3,2,1,0:T(8,128)(2,1)}, u32[]{:S(2)}) copy-start(bf16[1,5,128,128]{3,2,1,0:T(8,128)(2,1)} %coupling_ref.1) | copy-start | bytes 491524
  13.3 1.7 %collective-permute-start = (f32[512,128]{1,0:T(8,128)S(1)}, f32[512,128]{1,0:T(8,128)S(1)}, u32[]{:S(2)}, u32[]{:S(2)}) collective-permute-start(f32[512,128]{1,0:T(8,128)S(1)} %reduced_1.1), channel_id=1, source_target_pairs={{0,1},{1,0},{2,3},{3,2},{4,5},{5,4},{6,7},{7,6},{8,9},{9,8},{10,11... | collective-permute-start | bytes 786440 | tf_op jit(solution)/shard_map/ppermute | solution.py:25
  15.0 3.1 %collective-permute-start.1 = (f32[512,512]{1,0:T(8,128)S(1)}, f32[512,512]{1,0:T(8,128)S(1)}, u32[]{:S(2)}, u32[]{:S(2)}) collective-permute-start(f32[512,512]{1,0:T(8,128)S(1)} %get-tuple-element.39.refs_1_), channel_id=1, source_target_pairs={{0,1},{1,0},{2,3},{3,2},{4,5},{5,4},{6,7},{7,6},{8,9},{9,8},{10,11... | collective-permute-start | bytes 3145736 | tf_op jit(solution)/shard_map/ppermute | solution.py:25
  15.5 6.7 %collective-permute-start.2 = (f32[256,128]{1,0:T(8,128)S(1)}, f32[256,128]{1,0:T(8,128)S(1)}, u32[]{:S(2)}, u32[]{:S(2)}) collective-permute-start(f32[256,128]{1,0:T(8,128)S(1)} %slice_add_fusion.1), channel_id=1, source_target_pairs={{0,2},{1,3},{2,0},{3,1},{4,6},{5,7},{6,4},{7,5},{8,10},{9,11},{10,... | collective-permute-start | bytes 393224 | tf_op jit(solution)/shard_map/ppermute | solution.py:25
  22.2 13.6 %collective-permute-start.3 = (f32[256,512]{1,0:T(8,128)S(1)}, f32[256,512]{1,0:T(8,128)S(1)}, u32[]{:S(2)}, u32[]{:S(2)}) collective-permute-start(f32[256,512]{1,0:T(8,128)S(1)} %slice_add_fusion._), channel_id=1, source_target_pairs={{0,2},{1,3},{2,0},{3,1},{4,6},{5,7},{6,4},{7,5},{8,10},{9,11},{10,... | collective-permute-start | bytes 1572872 | tf_op jit(solution)/shard_map/ppermute | solution.py:25
  28.4 1.4 %collective-permute-start.4 = (f32[256,128]{1,0:T(8,128)S(1)}, f32[256,128]{1,0:T(8,128)S(1)}, u32[]{:S(2)}, u32[]{:S(2)}) collective-permute-start(f32[256,128]{1,0:T(8,128)S(1)} %get-tuple-element.45.refs_1_), channel_id=1, source_target_pairs={{0,1},{1,0},{2,3},{3,2},{4,5},{5,4},{6,7},{7,6},{8,9},{9,8},{10,11... | collective-permute-start | bytes 393224 | tf_op jit(solution)/shard_map/ppermute | solution.py:25
  34.4 5.6 %collective-permute-start.8 = (f32[256,128]{1,0:T(8,128)S(1)}, f32[256,128]{1,0:T(8,128)S(1)}, u32[]{:S(2)}, u32[]{:S(2)}) collective-permute-start(f32[256,128]{1,0:T(8,128)S(1)} %get-tuple-element.51.refs_1_), channel_id=1, source_target_pairs={{0,2},{1,3},{2,0},{3,1},{4,6},{5,7},{6,4},{7,5},{8,10},{9,11},{10,... | collective-permute-start | bytes 393224 | tf_op jit(solution)/shard_map/ppermute | solution.py:25
  37.2 9.0 %collective-permute-start.5 = (f32[256,128]{1,0:T(8,128)S(1)}, f32[256,128]{1,0:T(8,128)S(1)}, u32[]{:S(2)}, u32[]{:S(2)}) collective-permute-start(f32[256,128]{1,0:T(8,128)S(1)} %get-tuple-element.48), channel_id=1, source_target_pairs={{0,1},{1,0},{2,3},{3,2},{4,5},{5,4},{6,7},{7,6},{8,9},{9,8},{10,11... | collective-permute-start | bytes 393224 | tf_op jit(solution)/shard_map/ppermute | solution.py:25
  37.2 8.9 %collective-permute-start.6 = (f32[256,128]{1,0:T(8,128)S(1)}, f32[256,128]{1,0:T(8,128)S(1)}, u32[]{:S(2)}, u32[]{:S(2)}) collective-permute-start(f32[256,128]{1,0:T(8,128)S(1)} %get-tuple-element.49), channel_id=1, source_target_pairs={{0,2},{1,3},{2,0},{3,1},{4,6},{5,7},{6,4},{7,5},{8,10},{9,11},{10,... | collective-permute-start | bytes 393224 | tf_op jit(solution)/shard_map/ppermute | solution.py:25
  38.8 7.3 %collective-permute-start.7 = (f32[256,128]{1,0:T(8,128)S(1)}, f32[256,128]{1,0:T(8,128)S(1)}, u32[]{:S(2)}, u32[]{:S(2)}) collective-permute-start(f32[256,128]{1,0:T(8,128)S(1)} %get-tuple-element.50), channel_id=1, source_target_pairs={{0,3},{1,2},{2,1},{3,0},{4,7},{5,6},{6,5},{7,4},{8,11},{9,10},{10,... | collective-permute-start | bytes 393224 | tf_op jit(solution)/shard_map/ppermute | solution.py:25
  44.6 5.8 %collective-permute-start.10 = (f32[256,128]{1,0:T(8,128)S(1)}, f32[256,128]{1,0:T(8,128)S(1)}, u32[]{:S(2)}, u32[]{:S(2)}) collective-permute-start(f32[256,128]{1,0:T(8,128)S(1)} %get-tuple-element.53.refs_1_), channel_id=1, source_target_pairs={{0,4},{1,5},{2,6},{3,7},{4,0},{5,1},{6,2},{7,3},{8,12},{9,13},{10,... | collective-permute-start | bytes 393224 | tf_op jit(solution)/shard_map/ppermute | solution.py:25
  46.6 9.9 %collective-permute-start.9 = (f32[256,128]{1,0:T(8,128)S(1)}, f32[256,128]{1,0:T(8,128)S(1)}, u32[]{:S(2)}, u32[]{:S(2)}) collective-permute-start(f32[256,128]{1,0:T(8,128)S(1)} %upper_maps_1.1.refs_3_.refs_0_), channel_id=1, source_target_pairs={{0,4},{1,5},{2,6},{3,7},{4,0},{5,1},{6,2},{7,3},{8,12},{9,13},{10,... | collective-permute-start | bytes 393224 | tf_op jit(solution)/shard_map/ppermute | solution.py:25
  54.9 5.0 %collective-permute-start.11 = (f32[256,128]{1,0:T(8,128)S(1)}, f32[256,128]{1,0:T(8,128)S(1)}, u32[]{:S(2)}, u32[]{:S(2)}) collective-permute-start(f32[256,128]{1,0:T(8,128)S(1)} %get-tuple-element.59), channel_id=1, source_target_pairs={{0,8},{1,9},{2,10},{3,11},{4,12},{5,13},{6,14},{7,15},{8,0},{9,1},... | collective-permute-start | bytes 393224 | tf_op jit(solution)/shard_map/ppermute | solution.py:25
  57.1 10.3 %collective-permute-start.12 = (f32[256,128]{1,0:T(8,128)S(1)}, f32[256,128]{1,0:T(8,128)S(1)}, u32[]{:S(2)}, u32[]{:S(2)}) collective-permute-start(f32[256,128]{1,0:T(8,128)S(1)} %upper_maps_2.1._.refs_0_), channel_id=1, source_target_pairs={{0,8},{1,9},{2,10},{3,11},{4,12},{5,13},{6,14},{7,15},{8,0},{9,1},... | collective-permute-start | bytes 393224 | tf_op jit(solution)/shard_map/ppermute | solution.py:25
  64.7 8.0 %collective-permute-start.13 = (f32[128,128]{1,0:T(8,128)S(1)}, f32[128,128]{1,0:T(8,128)S(1)}, u32[]{:S(2)}, u32[]{:S(2)}) collective-permute-start(f32[128,128]{1,0:T(8,128)S(1)} %get-tuple-element.76), channel_id=1, source_target_pairs={{0,16},{1,17},{2,18},{3,19},{4,20},{5,21},{6,22},{7,23},{8,24},{9,... | collective-permute-start | bytes 196616 | tf_op jit(solution)/shard_map/ppermute | solution.py:25
  72.7 7.3 %collective-permute-start.15 = (f32[256,128]{1,0:T(8,128)S(1)}, f32[256,128]{1,0:T(8,128)S(1)}, u32[]{:S(2)}, u32[]{:S(2)}) collective-permute-start(f32[256,128]{1,0:T(8,128)S(1)} %upper_maps_3.1.own_ref), channel_id=1, source_target_pairs={{0,16},{1,17},{2,18},{3,19},{4,20},{5,21},{6,22},{7,23},{8,24},{9,... | collective-permute-start | bytes 393224 | tf_op jit(solution)/shard_map/ppermute | solution.py:25
  73.3 1.3 %collective-permute-start.14 = (f32[128,128]{1,0:T(8,128)S(1)}, f32[128,128]{1,0:T(8,128)S(1)}, u32[]{:S(2)}, u32[]{:S(2)}) collective-permute-start(f32[128,128]{1,0:T(8,128)S(1)} %collective-permute-done.13), channel_id=1, source_target_pairs={{0,1},{1,0},{2,3},{3,2},{4,5},{5,4},{6,7},{7,6},{8,9},{9,8},{10,11... | collective-permute-start | bytes 196616 | tf_op jit(solution)/shard_map/ppermute | solution.py:25
  78.9 9.0 %copy-start.4 = (f32[5,128,128]{2,1,0:T(8,128)}, f32[5,128,128]{2,1,0:T(8,128)S(1)}, u32[]{:S(2)}) copy-start(f32[5,128,128]{2,1,0:T(8,128)S(1)} %get-tuple-element.80) | copy-start | bytes 983044
  80.5 2.7 %collective-permute-start.16 = (f32[128,128]{1,0:T(8,128)S(1)}, f32[128,128]{1,0:T(8,128)S(1)}, u32[]{:S(2)}, u32[]{:S(2)}) collective-permute-start(f32[128,128]{1,0:T(8,128)S(1)} %top_sample.1.refs_0_), channel_id=1, source_target_pairs={{0,1},{1,0},{2,3},{3,2},{4,5},{5,4},{6,7},{7,6},{8,9},{9,8},{10,11... | collective-permute-start | bytes 196616 | tf_op jit(solution)/shard_map/ppermute | solution.py:25
  80.6 5.2 %collective-permute-start.17 = (f32[128,128]{1,0:T(8,128)S(1)}, f32[128,128]{1,0:T(8,128)S(1)}, u32[]{:S(2)}, u32[]{:S(2)}) collective-permute-start(f32[128,128]{1,0:T(8,128)S(1)} %top_sample.1.refs_0_), channel_id=1, source_target_pairs={{0,2},{1,3},{2,0},{3,1},{4,6},{5,7},{6,4},{7,5},{8,10},{9,11},{10,... | collective-permute-start | bytes 196616 | tf_op jit(solution)/shard_map/ppermute | solution.py:25
  83.1 4.0 %collective-permute-start.18 = (f32[128,128]{1,0:T(8,128)S(1)}, f32[128,128]{1,0:T(8,128)S(1)}, u32[]{:S(2)}, u32[]{:S(2)}) collective-permute-start(f32[128,128]{1,0:T(8,128)S(1)} %top_sample.1.refs_0_), channel_id=1, source_target_pairs={{0,3},{1,2},{2,1},{3,0},{4,7},{5,6},{6,5},{7,4},{8,11},{9,10},{10,... | collective-permute-start | bytes 196616 | tf_op jit(solution)/shard_map/ppermute | solution.py:25

commit v8 on v6

--- a/solution.py
+++ b/solution.py
@@ -337,19 +337,11 @@
 def merge_body(tree_level, *refs):
     last = tree_level == LEVELS - 1
     coupling_ref, own_ref, other_ref = refs[:3]
-    if tree_level == LEVELS - 2:
-        block_ref, maps_ref, pair_ref, half_ref = refs[-4:]
-    else:
-        block_ref, maps_ref, pair_ref = refs[-3:]
-    odd = position() % 2 == 1
+    block_ref, maps_ref, pair_ref = refs[-3:]
     rank = own_ref.shape[-1]
     ahead, back = turned(coupling_ref, tree_level)
     own_sample, own_sketch = own_ref[:rank], own_ref[rank:]
-    if last:
-        other_sample = jnp.where(odd, refs[3][...], other_ref[...])
-        other_sketch = jnp.where(odd, other_ref[...], refs[3][...])
-    else:
-        other_sample, other_sketch = other_ref[:rank], other_ref[rank:]
+    other_sample, other_sketch = other_ref[:rank], other_ref[rank:]
     own = own_sample - dot(ahead, other_sketch)
     other = other_sample - dot(back, own_sketch)
     own_t, other_t = own.T, other.T
@@ -371,8 +363,6 @@
     moved = dot(inverse, jnp.concatenate([both] + sides, axis=1))
     pair_ref[:rank, :] = moved[:, :rank]
     pair_ref[rank:, :] = moved[:, rank : 2 * rank]
-    if tree_level == LEVELS - 2:
-        half_ref[...] = jnp.where(odd, moved[:, rank : 2 * rank], moved[:, :rank])
     for side in range(len(sides)):
         maps_ref[side] = moved[:, (2 + side) * rank : (3 + side) * rank]
 
@@ -385,7 +375,7 @@
     rank = own.shape[1]
     f32 = jnp.float32
     last = tree_level == LEVELS - 1
-    split = tree_level == LEVELS - 2
+    split = 0
     return pl.pallas_call(
         functools.partial(merge_body, tree_level),
         grid=(1,),
@@ -547,20 +537,15 @@
     basis_t, pair = leaf_step(keep_red, first_red, second_red, sketch_red, passed)
     blocks, low_maps, after = [], [], []
     for tree_level in range(LEVELS):
-        if tree_level < LEVELS - 1:
-            others = [from_partner(pair, ROW_COL, 2**tree_level)]
-        else:
-            others = [waiting, from_partner(waiting, ROW_COL, 1)]
+        others = [from_partner(pair, ROW_COL, 2**tree_level)]
         if tree_level == 1:
             leaf_basis, mark = basis_step(basis_t)
             after = after + [mark]
         sides = 1 if tree_level < col_bits - 1 else 2
-        block, maps, pair, *half = merge_step(tree_level, pair, others, couplings, sides, after)
+        block, maps, pair = merge_step(tree_level, pair, others, couplings, sides, after)
         blocks.append(block)
         if tree_level == LEVELS - 1:
             break
-        if tree_level == LEVELS - 2:
-            waiting = from_partner(half[0], ROW_COL, 2 ** (LEVELS - 1))
         if tree_level < col_bits - 1:
             low_maps.append(maps)
         else:

time: 86.1 us -> 87.5 us (1.016)
  Pallas kernels: 35.8 us -> 40.6 us
  other arithmetic: 9.24 us -> 4.49 us
  starting transfers between devices: 18.2 us -> 19.6 us
    pallas_call x3 -> x4, Pallas kernels: 13.7 us -> 18.5 us  [merge_step(): pl.pallas_call(functools.partial(merge_body, tree_level), grid=(1,), out_...]
    pallas_call x2 -> x1, other arithmetic: 9.14 us -> 4.4 us  [merge_step(): pl.pallas_call(functools.partial(merge_body, tree_level), grid=(1,), out_...]
    ppermute x19 -> x18, starting transfers between devices: 18.2 us -> 19.6 us  [from_partner(): return lax.ppermute(block, axis, route)]
    ppermute x19 -> x18, waiting for transfers between devices: 20.8 us -> 20.8 us  [from_partner(): return lax.ppermute(block, axis, route)]
  transfers between devices with their start and end apart: 19 -> 18, of which waited for: 11 -> 10; matrix products, arithmetic and copies ran while one was open for 11% -> 5% of each run, Pallas kernels for 26% -> 31%
where the time goes in v8:
time: 87.5 us; the launch traced here: 87.3 us
  Pallas kernels  40.6 us (46%)
  waiting for transfers between devices  20.8 us (24%)
  starting transfers between devices  19.6 us (22%)
  other arithmetic  4.49 us (5%)
  between operations  1.01 us (1%)
    ppermute x18, waiting for transfers between devices, from_partner(): return lax.ppermute(block, axis, route)  20.8 us
    ppermute x18, starting transfers between devices, from_partner(): return lax.ppermute(block, axis, route)  19.6 us
    pallas_call x4, Pallas kernels, merge_step(): pl.pallas_call(functools.partial(merge_body, tree_level), grid=(1,), out_...  18.5 us
    pallas_call x1, Pallas kernels, sample_rows(): pl.pallas_call(functools.partial(spmm_body, leaves=leaves), out_shape=[ja...  11.2 us
    pallas_call x1, Pallas kernels, leaf_step(): pl.pallas_call(leaf_body, grid=(1,), out_shape=[jax.ShapeDtypeStruct((ran...  4.49 us
    pallas_call x1, other arithmetic, merge_step(): pl.pallas_call(functools.partial(merge_body, tree_level), grid=(1,), out_...  4.4 us
  transfers between devices with their start and end apart: 18, of which 10 were waited for; matrix products, arithmetic and copies ran while one was open for 5% of the time, Pallas kernels for 31%

profile of v8, /device:TPU:0, one launch (start us, length us, event | category | flops | bytes accessed | tf_op | source)
XLA Modules:
  0.0 87.3 jit_solution(878725165353309035)
XLA Ops:
  0.6 0.0 copy-start.2
  0.6 0.0 copy-start.1
  0.7 0.0 copy-start.3
  0.7 0.7 copy-done.3
  1.4 11.2 %spmm.1 = (f32[512,512]{1,0:T(8,128)S(1)}, f32[512,512]{1,0:T(8,128)S(1)}) custom-call(s32[168]{0:T(256)S(1)} %copy-done.3, bf16[168,128,128]{2,1,0:T(8,128)(2,1)} %tiles_ref.1, bf16[6144,512]{1,0:T(8,128)(2,1)} %sketch_ref.1), custom_call_target="tpu_custom_call" | custom-call | flops 6442450944 | bytes 13893632 | tf_op jit(solution)/shard_map/spmm/pallas_call | solution.py:215
  12.6 0.0 copy-start
  12.6 0.0 copy-done.2
  12.6 0.7 reduced_1.1
  13.3 0.5 collective-permute-start
  13.9 0.0 copy-done.1
  13.9 0.9 reduced_2.1
  14.7 0.3 collective-permute-done.first_ref
  15.0 0.4 collective-permute-start.1
  15.5 2.7 %collective-permute-start.2 = (f32[256,128]{1,0:T(8,128)S(1)}, f32[256,128]{1,0:T(8,128)S(1)}, u32[]{:S(2)}, u32[]{:S(2)}) collective-permute-start(f32[256,128]{1,0:T(8,128)S(1)} %slice_add_fusion.1), channel_id=1, source_target_pairs={{0,2},{1,3},{2,0},{3,1},{4,6},{5,7},{6,4},{7,5},{8,10},{9,11},{10,... | collective-permute-start | bytes 393224 | tf_op jit(solution)/shard_map/ppermute | solution.py:25
  18.1 0.0 collective-permute-done.1.refs_1_
  18.1 0.1 slice_add_fusion._
  18.2 3.9 %collective-permute-done.2.second_ref = f32[256,128]{1,0:T(8,128)S(1)} collective-permute-done((f32[256,128]{1,0:T(8,128)S(1)}, f32[256,128]{1,0:T(8,128)S(1)}, u32[]{:S(2)}, u32[]{:S(2)}) %collective-permute-start.2) | collective-permute-done | bytes 131104 | tf_op jit(solution)/shard_map/ppermute | solution.py:25
  22.2 1.7 %collective-permute-start.5 = (f32[256,512]{1,0:T(8,128)S(1)}, f32[256,512]{1,0:T(8,128)S(1)}, u32[]{:S(2)}, u32[]{:S(2)}) collective-permute-start(f32[256,512]{1,0:T(8,128)S(1)} %slice_add_fusion._), channel_id=1, source_target_pairs={{0,2},{1,3},{2,0},{3,1},{4,6},{5,7},{6,4},{7,5},{8,10},{9,11},{10,... | collective-permute-start | bytes 1572872 | tf_op jit(solution)/shard_map/ppermute | solution.py:25
  23.9 4.5 %leaf_orth.1 = (f32[128,256]{1,0:T(8,128)S(1)}, f32[256,128]{1,0:T(8,128)S(1)}) custom-call(f32[512,128]{1,0:T(8,128)S(1)} %get-tuple-element.34.keep_ref, f32[512,128]{1,0:T(8,128)S(1)} %collective-permute-done.first_ref, f32[256,128]{1,0:T(8,128)S(1)} %collective-permute-done.2.second_ref, f32[256,128]{1,0:T(8,128)S(1)} %get-tuple-element.39.sketch_red_ref, ...), custom_call_target="tpu_custom_call" | custom-call | flops 80000000 | bytes 240000 | tf_op jit(solution)/shard_map/leaf_orth/pallas_call | solution.py:291
  28.4 0.1 collective-permute-start.3
  28.5 0.8 leaf_basis.1
  29.2 0.6 collective-permute-done.3.refs_2_
  29.8 0.0 copy-done
  29.8 4.6 %merge_orth_0.1 = (f32[128,128]{1,0:T(8,128)S(1)}, f32[2,128,128]{2,1,0:T(8,128)S(1)}, f32[256,128]{1,0:T(8,128)S(1)}) custom-call(bf16[1,5,128,128]{3,2,1,0:T(8,128)(2,1)S(1)} %copy-done, f32[256,128]{1,0:T(8,128)S(1)} %get-tuple-element.43.refs_1_, f32[256,128]{1,0:T(8,128)S(1)} %collective-permute-done.3.refs_2_), custom_call_target="tpu_custom_call" | custom-call | flops 80000000 | bytes 240000 | tf_op jit(solution)/shard_map/merge_orth_0/pallas_call | solution.py:379
  34.4 0.3 collective-permute-start.4
  34.8 1.0 %collective-permute-done.5.refs_2_ = f32[256,512]{1,0:T(8,128)S(1)} collective-permute-done((f32[256,512]{1,0:T(8,128)S(1)}, f32[256,512]{1,0:T(8,128)S(1)}, u32[]{:S(2)}, u32[]{:S(2)}) %collective-permute-start.5) | collective-permute-done | bytes 524320 | tf_op jit(solution)/shard_map/ppermute | solution.py:25
  35.8 1.4 %lower_maps.1 = (f32[256,128]{1,0:T(8,128)S(1)}, f32[256,128]{1,0:T(8,128)S(1)}, f32[256,128]{1,0:T(8,128)S(1)}, f32[256,128]{1,0:T(8,128)S(1)}) custom-call(f32[512,512]{1,0:T(8,128)S(1)} %get-tuple-element.33.refs_1_.refs_0_, f32[512,512]{1,0:T(8,128)S(1)} %collective-permute-done.1.refs_1_, f32[256,512]{1,0:T(8,128)S(1)} %collective-permute-done.5.refs_2_, ...), custom_call_target="tpu_custom_call" | custom-call | flops 20000000 | bytes 60000 | tf_op jit(solution)/shard_map/lower_maps/pallas_call | solution.py:424
  37.2 0.1 collective-permute-start.7
  37.2 1.6 %collective-permute-start.8 = (f32[256,128]{1,0:T(8,128)S(1)}, f32[256,128]{1,0:T(8,128)S(1)}, u32[]{:S(2)}, u32[]{:S(2)}) collective-permute-start(f32[256,128]{1,0:T(8,128)S(1)} %get-tuple-element.52), channel_id=1, source_target_pairs={{0,2},{1,3},{2,0},{3,1},{4,6},{5,7},{6,4},{7,5},{8,10},{9,11},{10,... | collective-permute-start | bytes 393224 | tf_op jit(solution)/shard_map/ppermute | solution.py:25
  38.8 0.3 collective-permute-start.9
  39.1 1.0 %collective-permute-done.4.refs_2_ = f32[256,128]{1,0:T(8,128)S(1)} collective-permute-done((f32[256,128]{1,0:T(8,128)S(1)}, f32[256,128]{1,0:T(8,128)S(1)}, u32[]{:S(2)}, u32[]{:S(2)}) %collective-permute-start.4) | collective-permute-done | bytes 131104 | tf_op jit(solution)/shard_map/ppermute | solution.py:25
  40.1 4.5 %merge_orth_1.1 = (f32[128,128]{1,0:T(8,128)S(1)}, f32[4,128,128]{2,1,0:T(8,128)S(1)}, f32[256,128]{1,0:T(8,128)S(1)}) custom-call(bf16[1,5,128,128]{3,2,1,0:T(8,128)(2,1)S(1)} %copy-done, f32[256,128]{1,0:T(8,128)S(1)} %get-tuple-element.45.refs_1_, f32[256,128]{1,0:T(8,128)S(1)} %collective-permute-done.4.refs_2_, ...), custom_call_target="tpu_custom_call" | custom-call | flops 80000000 | bytes 240000 | tf_op jit(solution)/shard_map/merge_orth_1/pallas_call | solution.py:379
  44.6 1.6 %collective-permute-start.6 = (f32[256,128]{1,0:T(8,128)S(1)}, f32[256,128]{1,0:T(8,128)S(1)}, u32[]{:S(2)}, u32[]{:S(2)}) collective-permute-start(f32[256,128]{1,0:T(8,128)S(1)} %get-tuple-element.50.refs_1_), channel_id=1, source_target_pairs={{0,4},{1,5},{2,6},{3,7},{4,0},{5,1},{6,2},{7,3},{8,12},{9,13},{10,... | collective-permute-start | bytes 393224 | tf_op jit(solution)/shard_map/ppermute | solution.py:25
  46.2 0.0 collective-permute-done.7.refs_1_
  46.2 0.0 collective-permute-done.8.refs_2_
  46.2 0.0 collective-permute-done.9.refs_3_
  46.2 0.5 upper_maps_1.1.refs_3_.refs_0_
  46.7 0.9 collective-permute-start.11
  47.5 2.9 %collective-permute-done.6.refs_2_ = f32[256,128]{1,0:T(8,128)S(1)} collective-permute-done((f32[256,128]{1,0:T(8,128)S(1)}, f32[256,128]{1,0:T(8,128)S(1)}, u32[]{:S(2)}, u32[]{:S(2)}) %collective-permute-start.6) | collective-permute-done | bytes 131104 | tf_op jit(solution)/shard_map/ppermute | solution.py:25
  50.4 4.5 %merge_orth_2.1 = (f32[128,128]{1,0:T(8,128)S(1)}, f32[4,128,128]{2,1,0:T(8,128)S(1)}, f32[256,128]{1,0:T(8,128)S(1)}) custom-call(bf16[1,5,128,128]{3,2,1,0:T(8,128)(2,1)S(1)} %copy-done, f32[256,128]{1,0:T(8,128)S(1)} %get-tuple-element.50.refs_1_, f32[256,128]{1,0:T(8,128)S(1)} %collective-permute-done.6.refs_2_, f32[256,128]{1,0:T(8,128)S(1)} %upper_maps_1.1.refs_3_.refs_0_), custom_call_target="tpu_custom_call" | custom-call | flops 80000000 | bytes 240000 | tf_op jit(solution)/shard_map/merge_orth_2/pallas_call | solution.py:379
  54.9 1.7 %collective-permute-start.10 = (f32[256,128]{1,0:T(8,128)S(1)}, f32[256,128]{1,0:T(8,128)S(1)}, u32[]{:S(2)}, u32[]{:S(2)}) collective-permute-start(f32[256,128]{1,0:T(8,128)S(1)} %get-tuple-element.56.refs_1_), channel_id=1, source_target_pairs={{0,8},{1,9},{2,10},{3,11},{4,12},{5,13},{6,14},{7,15},{8,0},{9,1},... | collective-permute-start | bytes 393224 | tf_op jit(solution)/shard_map/ppermute | solution.py:25
  56.6 0.0 collective-permute-done.11.refs_1_
  56.6 0.5 upper_maps_2.1.refs_3_.refs_0_
  57.1 0.5 collective-permute-start.13
  57.6 2.4 %collective-permute-done.10.refs_2_ = f32[256,128]{1,0:T(8,128)S(1)} collective-permute-done((f32[256,128]{1,0:T(8,128)S(1)}, f32[256,128]{1,0:T(8,128)S(1)}, u32[]{:S(2)}, u32[]{:S(2)}) %collective-permute-start.10) | collective-permute-done | bytes 131104 | tf_op jit(solution)/shard_map/ppermute | solution.py:25
  60.0 4.7 %merge_orth_3.1 = (f32[128,128]{1,0:T(8,128)S(1)}, f32[4,128,128]{2,1,0:T(8,128)S(1)}, f32[256,128]{1,0:T(8,128)S(1)}) custom-call(bf16[1,5,128,128]{3,2,1,0:T(8,128)(2,1)S(1)} %copy-done, f32[256,128]{1,0:T(8,128)S(1)} %get-tuple-element.56.refs_1_, f32[256,128]{1,0:T(8,128)S(1)} %collective-permute-done.10.refs_2_, f32[256,128]{1,0:T(8,128)S(1)} %upper_maps_2.1.refs_3_.refs_0_), custom_call_target="tpu_custom_call" | custom-call | flops 80000000 | bytes 240000 | tf_op jit(solution)/shard_map/merge_orth_3/pallas_call | solution.py:379
  64.7 2.7 %collective-permute-start.12 = (f32[256,128]{1,0:T(8,128)S(1)}, f32[256,128]{1,0:T(8,128)S(1)}, u32[]{:S(2)}, u32[]{:S(2)}) collective-permute-start(f32[256,128]{1,0:T(8,128)S(1)} %get-tuple-element.59), channel_id=1, source_target_pairs={{0,16},{1,17},{2,18},{3,19},{4,20},{5,21},{6,22},{7,23},{8,24},{9,... | collective-permute-start | bytes 393224 | tf_op jit(solution)/shard_map/ppermute | solution.py:25
  67.4 0.0 collective-permute-done.13.refs_1_
  67.4 0.5 upper_maps_3.1.own_ref
  67.9 0.4 collective-permute-start.14
  68.3 4.8 %collective-permute-done.12 = f32[256,128]{1,0:T(8,128)S(1)} collective-permute-done((f32[256,128]{1,0:T(8,128)S(1)}, f32[256,128]{1,0:T(8,128)S(1)}, u32[]{:S(2)}, u32[]{:S(2)}) %collective-permute-start.12) | collective-permute-done | bytes 131104 | tf_op jit(solution)/shard_map/ppermute | solution.py:25
  73.1 4.4 %merge_orth_4.1 = (f32[5,128,128]{2,1,0:T(8,128)S(1)}, f32[128,256]{1,0:T(8,128)S(1)}, f32[8,128]{1,0:T(8,128)}) fusion(f32[5,128,128]{2,1,0:T(8,128)S(1)} %bitcast_dynamic-update-slice_fusion.1, bf16[1,5,128,128]{3,2,1,0:T(8,128)(2,1)S(1)} %copy-done, f32[256,128]{1,0:T(8,128)S(1)} %get-tuple-element.59, f32[256,128]{1,0:T(8,128)S(1)} %collective-permute-done.12, ...), kind=kCustom, calls=%fused_computation.2 | custom fusion | flops 80000000 | bytes 757760 | tf_op jit(solution)/shard_map/merge_orth_4/pallas_call | solution.py:379
  77.5 0.0 copy-start.4
  77.5 0.0 collective-permute-done.14.other_ref
  77.5 0.6 top_sample.1.refs_0_
  78.1 0.1 collective-permute-start.15
  78.2 4.1 %collective-permute-start.16 = (f32[128,128]{1,0:T(8,128)S(1)}, f32[128,128]{1,0:T(8,128)S(1)}, u32[]{:S(2)}, u32[]{:S(2)}) collective-permute-start(f32[128,128]{1,0:T(8,128)S(1)} %top_sample.1.refs_0_), channel_id=1, source_target_pairs={{0,2},{1,3},{2,0},{3,1},{4,6},{5,7},{6,4},{7,5},{8,10},{9,11},{10,... | collective-permute-start | bytes 196616 | tf_op jit(solution)/shard_map/ppermute | solution.py:25
  82.3 0.1 collective-permute-start.17
  82.4 0.0 collective-permute-done.15.refs_1_
  82.4 2.6 %collective-permute-done.16.refs_2_ = f32[128,128]{1,0:T(8,128)S(1)} collective-permute-done((f32[128,128]{1,0:T(8,128)S(1)}, f32[128,128]{1,0:T(8,128)S(1)}, u32[]{:S(2)}, u32[]{:S(2)}) %collective-permute-start.16) | collective-permute-done | bytes 65568 | tf_op jit(solution)/shard_map/ppermute | solution.py:25
  85.0 1.4 %collective-permute-done.17.refs_3_ = f32[128,128]{1,0:T(8,128)S(1)} collective-permute-done((f32[128,128]{1,0:T(8,128)S(1)}, f32[128,128]{1,0:T(8,128)S(1)}, u32[]{:S(2)}, u32[]{:S(2)}) %collective-permute-start.17) | collective-permute-done | bytes 65568 | tf_op jit(solution)/shard_map/ppermute | solution.py:25
  86.3 0.7 top_columns.1
  87.1 0.0 copy-done.4
  (5 shorter events, 0.0 us)
Async XLA Ops:
  0.6 12.0 %copy-start.2 = (f32[512,128]{1,0:T(8,128)S(1)}, f32[512,128]{1,0:T(8,128)}, u32[]{:S(2)}) copy-start(f32[512,128]{1,0:T(8,128)} %refs_0_.8) | copy-start | bytes 786436
  0.6 13.2 %copy-start.1 = (bf16[256,512]{1,0:T(8,128)(2,1)S(1)}, bf16[256,512]{1,0:T(8,128)(2,1)}, u32[]{:S(2)}) copy-start(bf16[256,512]{1,0:T(8,128)(2,1)} %refs_3_.1) | copy-start | bytes 786436
  0.7 0.7 copy-start.3
  12.6 17.2 %copy-start = (bf16[1,5,128,128]{3,2,1,0:T(8,128)(2,1)S(1)}, bf16[1,5,128,128]{3,2,1,0:T(8,128)(2,1)}, u32[]{:S(2)}) copy-start(bf16[1,5,128,128]{3,2,1,0:T(8,128)(2,1)} %coupling_ref.1) | copy-start | bytes 491524
  13.3 1.7 %collective-permute-start = (f32[512,128]{1,0:T(8,128)S(1)}, f32[512,128]{1,0:T(8,128)S(1)}, u32[]{:S(2)}, u32[]{:S(2)}) collective-permute-start(f32[512,128]{1,0:T(8,128)S(1)} %reduced_1.1), channel_id=1, source_target_pairs={{0,1},{1,0},{2,3},{3,2},{4,5},{5,4},{6,7},{7,6},{8,9},{9,8},{10,11... | collective-permute-start | bytes 786440 | tf_op jit(solution)/shard_map/ppermute | solution.py:25
  15.0 3.1 %collective-permute-start.1 = (f32[512,512]{1,0:T(8,128)S(1)}, f32[512,512]{1,0:T(8,128)S(1)}, u32[]{:S(2)}, u32[]{:S(2)}) collective-permute-start(f32[512,512]{1,0:T(8,128)S(1)} %get-tuple-element.36.refs_1_), channel_id=1, source_target_pairs={{0,1},{1,0},{2,3},{3,2},{4,5},{5,4},{6,7},{7,6},{8,9},{9,8},{10,11... | collective-permute-start | bytes 3145736 | tf_op jit(solution)/shard_map/ppermute | solution.py:25
  15.5 6.7 %collective-permute-start.2 = (f32[256,128]{1,0:T(8,128)S(1)}, f32[256,128]{1,0:T(8,128)S(1)}, u32[]{:S(2)}, u32[]{:S(2)}) collective-permute-start(f32[256,128]{1,0:T(8,128)S(1)} %slice_add_fusion.1), channel_id=1, source_target_pairs={{0,2},{1,3},{2,0},{3,1},{4,6},{5,7},{6,4},{7,5},{8,10},{9,11},{10,... | collective-permute-start | bytes 393224 | tf_op jit(solution)/shard_map/ppermute | solution.py:25
  22.2 13.6 %collective-permute-start.5 = (f32[256,512]{1,0:T(8,128)S(1)}, f32[256,512]{1,0:T(8,128)S(1)}, u32[]{:S(2)}, u32[]{:S(2)}) collective-permute-start(f32[256,512]{1,0:T(8,128)S(1)} %slice_add_fusion._), channel_id=1, source_target_pairs={{0,2},{1,3},{2,0},{3,1},{4,6},{5,7},{6,4},{7,5},{8,10},{9,11},{10,... | collective-permute-start | bytes 1572872 | tf_op jit(solution)/shard_map/ppermute | solution.py:25
  28.4 1.4 %collective-permute-start.3 = (f32[256,128]{1,0:T(8,128)S(1)}, f32[256,128]{1,0:T(8,128)S(1)}, u32[]{:S(2)}, u32[]{:S(2)}) collective-permute-start(f32[256,128]{1,0:T(8,128)S(1)} %get-tuple-element.43.refs_1_), channel_id=1, source_target_pairs={{0,1},{1,0},{2,3},{3,2},{4,5},{5,4},{6,7},{7,6},{8,9},{9,8},{10,11... | collective-permute-start | bytes 393224 | tf_op jit(solution)/shard_map/ppermute | solution.py:25
  34.4 5.6 %collective-permute-start.4 = (f32[256,128]{1,0:T(8,128)S(1)}, f32[256,128]{1,0:T(8,128)S(1)}, u32[]{:S(2)}, u32[]{:S(2)}) collective-permute-start(f32[256,128]{1,0:T(8,128)S(1)} %get-tuple-element.45.refs_1_), channel_id=1, source_target_pairs={{0,2},{1,3},{2,0},{3,1},{4,6},{5,7},{6,4},{7,5},{8,10},{9,11},{10,... | collective-permute-start | bytes 393224 | tf_op jit(solution)/shard_map/ppermute | solution.py:25
  37.2 9.0 %collective-permute-start.7 = (f32[256,128]{1,0:T(8,128)S(1)}, f32[256,128]{1,0:T(8,128)S(1)}, u32[]{:S(2)}, u32[]{:S(2)}) collective-permute-start(f32[256,128]{1,0:T(8,128)S(1)} %get-tuple-element.51), channel_id=1, source_target_pairs={{0,1},{1,0},{2,3},{3,2},{4,5},{5,4},{6,7},{7,6},{8,9},{9,8},{10,11... | collective-permute-start | bytes 393224 | tf_op jit(solution)/shard_map/ppermute | solution.py:25
  37.2 8.9 %collective-permute-start.8 = (f32[256,128]{1,0:T(8,128)S(1)}, f32[256,128]{1,0:T(8,128)S(1)}, u32[]{:S(2)}, u32[]{:S(2)}) collective-permute-start(f32[256,128]{1,0:T(8,128)S(1)} %get-tuple-element.52), channel_id=1, source_target_pairs={{0,2},{1,3},{2,0},{3,1},{4,6},{5,7},{6,4},{7,5},{8,10},{9,11},{10,... | collective-permute-start | bytes 393224 | tf_op jit(solution)/shard_map/ppermute | solution.py:25
  38.8 7.4 %collective-permute-start.9 = (f32[256,128]{1,0:T(8,128)S(1)}, f32[256,128]{1,0:T(8,128)S(1)}, u32[]{:S(2)}, u32[]{:S(2)}) collective-permute-start(f32[256,128]{1,0:T(8,128)S(1)} %get-tuple-element.53), channel_id=1, source_target_pairs={{0,3},{1,2},{2,1},{3,0},{4,7},{5,6},{6,5},{7,4},{8,11},{9,10},{10,... | collective-permute-start | bytes 393224 | tf_op jit(solution)/shard_map/ppermute | solution.py:25
  44.6 5.8 %collective-permute-start.6 = (f32[256,128]{1,0:T(8,128)S(1)}, f32[256,128]{1,0:T(8,128)S(1)}, u32[]{:S(2)}, u32[]{:S(2)}) collective-permute-start(f32[256,128]{1,0:T(8,128)S(1)} %get-tuple-element.50.refs_1_), channel_id=1, source_target_pairs={{0,4},{1,5},{2,6},{3,7},{4,0},{5,1},{6,2},{7,3},{8,12},{9,13},{10,... | collective-permute-start | bytes 393224 | tf_op jit(solution)/shard_map/ppermute | solution.py:25
  46.7 9.9 %collective-permute-start.11 = (f32[256,128]{1,0:T(8,128)S(1)}, f32[256,128]{1,0:T(8,128)S(1)}, u32[]{:S(2)}, u32[]{:S(2)}) collective-permute-start(f32[256,128]{1,0:T(8,128)S(1)} %upper_maps_1.1.refs_3_.refs_0_), channel_id=1, source_target_pairs={{0,4},{1,5},{2,6},{3,7},{4,0},{5,1},{6,2},{7,3},{8,12},{9,13},{10,... | collective-permute-start | bytes 393224 | tf_op jit(solution)/shard_map/ppermute | solution.py:25
  54.9 5.0 %collective-permute-start.10 = (f32[256,128]{1,0:T(8,128)S(1)}, f32[256,128]{1,0:T(8,128)S(1)}, u32[]{:S(2)}, u32[]{:S(2)}) collective-permute-start(f32[256,128]{1,0:T(8,128)S(1)} %get-tuple-element.56.refs_1_), channel_id=1, source_target_pairs={{0,8},{1,9},{2,10},{3,11},{4,12},{5,13},{6,14},{7,15},{8,0},{9,1},... | collective-permute-start | bytes 393224 | tf_op jit(solution)/shard_map/ppermute | solution.py:25
  57.1 10.3 %collective-permute-start.13 = (f32[256,128]{1,0:T(8,128)S(1)}, f32[256,128]{1,0:T(8,128)S(1)}, u32[]{:S(2)}, u32[]{:S(2)}) collective-permute-start(f32[256,128]{1,0:T(8,128)S(1)} %upper_maps_2.1.refs_3_.refs_0_), channel_id=1, source_target_pairs={{0,8},{1,9},{2,10},{3,11},{4,12},{5,13},{6,14},{7,15},{8,0},{9,1},... | collective-permute-start | bytes 393224 | tf_op jit(solution)/shard_map/ppermute | solution.py:25
  64.7 8.4 %collective-permute-start.12 = (f32[256,128]{1,0:T(8,128)S(1)}, f32[256,128]{1,0:T(8,128)S(1)}, u32[]{:S(2)}, u32[]{:S(2)}) collective-permute-start(f32[256,128]{1,0:T(8,128)S(1)} %get-tuple-element.59), channel_id=1, source_target_pairs={{0,16},{1,17},{2,18},{3,19},{4,20},{5,21},{6,22},{7,23},{8,24},{9,... | collective-permute-start | bytes 393224 | tf_op jit(solution)/shard_map/ppermute | solution.py:25
  67.9 9.6 %collective-permute-start.14 = (f32[256,128]{1,0:T(8,128)S(1)}, f32[256,128]{1,0:T(8,128)S(1)}, u32[]{:S(2)}, u32[]{:S(2)}) collective-permute-start(f32[256,128]{1,0:T(8,128)S(1)} %upper_maps_3.1.own_ref), channel_id=1, source_target_pairs={{0,16},{1,17},{2,18},{3,19},{4,20},{5,21},{6,22},{7,23},{8,24},{9,... | collective-permute-start | bytes 393224 | tf_op jit(solution)/shard_map/ppermute | solution.py:25
  77.5 9.6 %copy-start.4 = (f32[5,128,128]{2,1,0:T(8,128)}, f32[5,128,128]{2,1,0:T(8,128)S(1)}, u32[]{:S(2)}) copy-start(f32[5,128,128]{2,1,0:T(8,128)S(1)} %get-tuple-element.66) | copy-start | bytes 983044
  78.1 4.3 %collective-permute-start.15 = (f32[128,128]{1,0:T(8,128)S(1)}, f32[128,128]{1,0:T(8,128)S(1)}, u32[]{:S(2)}, u32[]{:S(2)}) collective-permute-start(f32[128,128]{1,0:T(8,128)S(1)} %top_sample.1.refs_0_), channel_id=1, source_target_pairs={{0,1},{1,0},{2,3},{3,2},{4,5},{5,4},{6,7},{7,6},{8,9},{9,8},{10,11... | collective-permute-start | bytes 196616 | tf_op jit(solution)/shard_map/ppermute | solution.py:25
  78.2 6.8 %collective-permute-start.16 = (f32[128,128]{1,0:T(8,128)S(1)}, f32[128,128]{1,0:T(8,128)S(1)}, u32[]{:S(2)}, u32[]{:S(2)}) collective-permute-start(f32[128,128]{1,0:T(8,128)S(1)} %top_sample.1.refs_0_), channel_id=1, source_target_pairs={{0,2},{1,3},{2,0},{3,1},{4,6},{5,7},{6,4},{7,5},{8,10},{9,11},{10,... | collective-permute-start | bytes 196616 | tf_op jit(solution)/shard_map/ppermute | solution.py:25
  82.3 4.0 %collective-permute-start.17 = (f32[128,128]{1,0:T(8,128)S(1)}, f32[128,128]{1,0:T(8,128)S(1)}, u32[]{:S(2)}, u32[]{:S(2)}) collective-permute-start(f32[128,128]{1,0:T(8,128)S(1)} %top_sample.1.refs_0_), channel_id=1, source_target_pairs={{0,3},{1,2},{2,1},{3,0},{4,7},{5,6},{6,5},{7,4},{8,11},{9,10},{10,... | collective-permute-start | bytes 196616 | tf_op jit(solution)/shard_map/ppermute | solution.py:25

commit v9 on v6

--- a/solution.py
+++ b/solution.py
@@ -211,7 +211,7 @@
     leaves = lax.axis_size("col")
     rows = leaf * leaves
     half = rows // 2
-    chunks = math.gcd(depth // tile_size, 4)
+    chunks = 1
     return pl.pallas_call(
         functools.partial(spmm_body, leaves=leaves),
         out_shape=[jax.ShapeDtypeStruct((half, width), jnp.float32)] * 2,

time: 86.1 us -> 85.9 us (level)
  no operation moved by 1% of the time
where the time goes in v9:
time: 85.9 us; the launch traced here: 85.7 us
  Pallas kernels  35.6 us (41%)
  waiting for transfers between devices  20.8 us (24%)
  starting transfers between devices  18.2 us (21%)
  other arithmetic  9.27 us (11%)
  between operations  1.01 us (1%)
    ppermute x19, waiting for transfers between devices, from_partner(): return lax.ppermute(block, axis, route)  20.8 us
    ppermute x19, starting transfers between devices, from_partner(): return lax.ppermute(block, axis, route)  18.2 us
    pallas_call x3, Pallas kernels, merge_step(): pl.pallas_call(functools.partial(merge_body, tree_level), grid=(1,), out_...  13.7 us
    pallas_call x1, Pallas kernels, sample_rows(): pl.pallas_call(functools.partial(spmm_body, leaves=leaves), out_shape=[ja...  11 us
    pallas_call x2, other arithmetic, merge_step(): pl.pallas_call(functools.partial(merge_body, tree_level), grid=(1,), out_...  9.17 us
    pallas_call x1, Pallas kernels, leaf_step(): pl.pallas_call(leaf_body, grid=(1,), out_shape=[jax.ShapeDtypeStruct((ran...  4.48 us
  transfers between devices with their start and end apart: 19, of which 11 were waited for; matrix products, arithmetic and copies ran while one was open for 11% of the time, Pallas kernels for 26%

profile of v9, /device:TPU:0, one launch (start us, length us, event | category | flops | bytes accessed | tf_op | source)
XLA Modules:
  0.0 85.7 jit_solution(2576501854231180043)
XLA Ops:
  0.6 0.0 copy-start.2
  0.6 0.0 copy-start.1
  0.7 0.0 copy-start.3
  0.7 0.7 copy-done.3
  1.4 11.0 %spmm.1 = (f32[512,512]{1,0:T(8,128)S(1)}, f32[512,512]{1,0:T(8,128)S(1)}) custom-call(s32[168]{0:T(256)S(1)} %copy-done.3, bf16[168,128,128]{2,1,0:T(8,128)(2,1)} %tiles_ref.1, bf16[6144,512]{1,0:T(8,128)(2,1)} %sketch_ref.1), custom_call_target="tpu_custom_call" | custom-call | flops 6442450944 | bytes 13893632 | tf_op jit(solution)/shard_map/spmm/pallas_call | solution.py:215
  12.4 0.0 copy-start
  12.4 0.0 copy-done.2
  12.4 0.7 reduced_1.1
  13.1 0.5 collective-permute-start
  13.7 0.0 copy-done.1
  13.7 0.9 %reduced_2.1 = (f32[512,128]{1,0:T(8,128)S(1)}, f32[256,128]{1,0:T(8,128)S(1)}) custom-call(f32[512,128]{1,0:T(8,128)S(1)} %copy-done.2, f32[512,512]{1,0:T(8,128)S(1)} %get-tuple-element.34.refs_1_.refs_0_, bf16[256,512]{1,0:T(8,128)(2,1)S(1)} %copy-done.1), custom_call_target="tpu_custom_call" | custom-call | flops 10000000 | bytes 30000 | tf_op jit(solution)/shard_map/reduced_2/pallas_call | solution.py:256
  14.5 0.3 collective-permute-done.first_ref
  14.8 0.4 collective-permute-start.1
  15.3 2.7 %collective-permute-start.2 = (f32[256,128]{1,0:T(8,128)S(1)}, f32[256,128]{1,0:T(8,128)S(1)}, u32[]{:S(2)}, u32[]{:S(2)}) collective-permute-start(f32[256,128]{1,0:T(8,128)S(1)} %slice_add_fusion.1), channel_id=1, source_target_pairs={{0,2},{1,3},{2,0},{3,1},{4,6},{5,7},{6,4},{7,5},{8,10},{9,11},{10,... | collective-permute-start | bytes 393224 | tf_op jit(solution)/shard_map/ppermute | solution.py:25
  17.9 0.0 collective-permute-done.1.refs_1_
  17.9 0.1 slice_add_fusion._
  18.0 3.9 %collective-permute-done.2.second_ref = f32[256,128]{1,0:T(8,128)S(1)} collective-permute-done((f32[256,128]{1,0:T(8,128)S(1)}, f32[256,128]{1,0:T(8,128)S(1)}, u32[]{:S(2)}, u32[]{:S(2)}) %collective-permute-start.2) | collective-permute-done | bytes 131104 | tf_op jit(solution)/shard_map/ppermute | solution.py:25
  22.0 1.7 %collective-permute-start.5 = (f32[256,512]{1,0:T(8,128)S(1)}, f32[256,512]{1,0:T(8,128)S(1)}, u32[]{:S(2)}, u32[]{:S(2)}) collective-permute-start(f32[256,512]{1,0:T(8,128)S(1)} %slice_add_fusion._), channel_id=1, source_target_pairs={{0,2},{1,3},{2,0},{3,1},{4,6},{5,7},{6,4},{7,5},{8,10},{9,11},{10,... | collective-permute-start | bytes 1572872 | tf_op jit(solution)/shard_map/ppermute | solution.py:25
  23.7 4.5 %leaf_orth.1 = (f32[128,256]{1,0:T(8,128)S(1)}, f32[256,128]{1,0:T(8,128)S(1)}) custom-call(f32[512,128]{1,0:T(8,128)S(1)} %get-tuple-element.35.keep_ref, f32[512,128]{1,0:T(8,128)S(1)} %collective-permute-done.first_ref, f32[256,128]{1,0:T(8,128)S(1)} %collective-permute-done.2.second_ref, f32[256,128]{1,0:T(8,128)S(1)} %get-tuple-element.40.sketch_red_ref, ...), custom_call_target="tpu_custom_call" | custom-call | flops 80000000 | bytes 240000 | tf_op jit(solution)/shard_map/leaf_orth/pallas_call | solution.py:291
  28.2 0.1 collective-permute-start.3
  28.3 0.8 leaf_basis.1
  29.0 0.6 collective-permute-done.3.refs_2_
  29.6 4.6 %merge_orth_0.1 = (f32[128,128]{1,0:T(8,128)S(1)}, f32[2,128,128]{2,1,0:T(8,128)S(1)}, f32[256,128]{1,0:T(8,128)S(1)}) custom-call(bf16[1,5,128,128]{3,2,1,0:T(8,128)(2,1)S(1)} %copy-done, f32[256,128]{1,0:T(8,128)S(1)} %get-tuple-element.44.refs_1_, f32[256,128]{1,0:T(8,128)S(1)} %collective-permute-done.3.refs_2_), custom_call_target="tpu_custom_call" | custom-call | flops 80000000 | bytes 240000 | tf_op jit(solution)/shard_map/merge_orth_0/pallas_call | solution.py:389
  34.2 0.4 collective-permute-start.4
  34.6 1.0 %collective-permute-done.5.refs_2_ = f32[256,512]{1,0:T(8,128)S(1)} collective-permute-done((f32[256,512]{1,0:T(8,128)S(1)}, f32[256,512]{1,0:T(8,128)S(1)}, u32[]{:S(2)}, u32[]{:S(2)}) %collective-permute-start.5) | collective-permute-done | bytes 524320 | tf_op jit(solution)/shard_map/ppermute | solution.py:25
  35.6 1.4 %lower_maps.1 = (f32[256,128]{1,0:T(8,128)S(1)}, f32[256,128]{1,0:T(8,128)S(1)}, f32[256,128]{1,0:T(8,128)S(1)}, f32[256,128]{1,0:T(8,128)S(1)}) custom-call(f32[512,512]{1,0:T(8,128)S(1)} %get-tuple-element.34.refs_1_.refs_0_, f32[512,512]{1,0:T(8,128)S(1)} %collective-permute-done.1.refs_1_, f32[256,512]{1,0:T(8,128)S(1)} %collective-permute-done.5.refs_2_, ...), custom_call_target="tpu_custom_call" | custom-call | flops 20000000 | bytes 60000 | tf_op jit(solution)/shard_map/lower_maps/pallas_call | solution.py:434
  37.0 0.1 collective-permute-start.7
  37.0 1.6 %collective-permute-start.8 = (f32[256,128]{1,0:T(8,128)S(1)}, f32[256,128]{1,0:T(8,128)S(1)}, u32[]{:S(2)}, u32[]{:S(2)}) collective-permute-start(f32[256,128]{1,0:T(8,128)S(1)} %get-tuple-element.53), channel_id=1, source_target_pairs={{0,2},{1,3},{2,0},{3,1},{4,6},{5,7},{6,4},{7,5},{8,10},{9,11},{10,... | collective-permute-start | bytes 393224 | tf_op jit(solution)/shard_map/ppermute | solution.py:25
  38.6 0.3 collective-permute-start.9
  38.9 0.9 %collective-permute-done.4.refs_2_ = f32[256,128]{1,0:T(8,128)S(1)} collective-permute-done((f32[256,128]{1,0:T(8,128)S(1)}, f32[256,128]{1,0:T(8,128)S(1)}, u32[]{:S(2)}, u32[]{:S(2)}) %collective-permute-start.4) | collective-permute-done | bytes 131104 | tf_op jit(solution)/shard_map/ppermute | solution.py:25
  39.8 4.5 %merge_orth_1.1 = (f32[128,128]{1,0:T(8,128)S(1)}, f32[4,128,128]{2,1,0:T(8,128)S(1)}, f32[256,128]{1,0:T(8,128)S(1)}) custom-call(bf16[1,5,128,128]{3,2,1,0:T(8,128)(2,1)S(1)} %copy-done, f32[256,128]{1,0:T(8,128)S(1)} %get-tuple-element.46.refs_1_, f32[256,128]{1,0:T(8,128)S(1)} %collective-permute-done.4.refs_2_, ...), custom_call_target="tpu_custom_call" | custom-call | flops 80000000 | bytes 240000 | tf_op jit(solution)/shard_map/merge_orth_1/pallas_call | solution.py:389
  44.4 1.6 %collective-permute-start.6 = (f32[256,128]{1,0:T(8,128)S(1)}, f32[256,128]{1,0:T(8,128)S(1)}, u32[]{:S(2)}, u32[]{:S(2)}) collective-permute-start(f32[256,128]{1,0:T(8,128)S(1)} %get-tuple-element.51.refs_1_), channel_id=1, source_target_pairs={{0,4},{1,5},{2,6},{3,7},{4,0},{5,1},{6,2},{7,3},{8,12},{9,13},{10,... | collective-permute-start | bytes 393224 | tf_op jit(solution)/shard_map/ppermute | solution.py:25
  46.0 0.0 collective-permute-done.7.refs_1_
  46.0 0.0 collective-permute-done.8.refs_2_
  46.0 0.0 collective-permute-done.9.refs_3_
  46.0 0.5 upper_maps_1.1.refs_3_.refs_0_
  46.5 0.9 %collective-permute-start.11 = (f32[256,128]{1,0:T(8,128)S(1)}, f32[256,128]{1,0:T(8,128)S(1)}, u32[]{:S(2)}, u32[]{:S(2)}) collective-permute-start(f32[256,128]{1,0:T(8,128)S(1)} %upper_maps_1.1.refs_3_.refs_0_), channel_id=1, source_target_pairs={{0,4},{1,5},{2,6},{3,7},{4,0},{5,1},{6,2},{7,3},{8,12},{9,13},{10,... | collective-permute-start | bytes 393224 | tf_op jit(solution)/shard_map/ppermute | solution.py:25
  47.3 2.9 %collective-permute-done.6.refs_2_ = f32[256,128]{1,0:T(8,128)S(1)} collective-permute-done((f32[256,128]{1,0:T(8,128)S(1)}, f32[256,128]{1,0:T(8,128)S(1)}, u32[]{:S(2)}, u32[]{:S(2)}) %collective-permute-start.6) | collective-permute-done | bytes 131104 | tf_op jit(solution)/shard_map/ppermute | solution.py:25
  50.2 4.5 %merge_orth_2.1 = (f32[128,128]{1,0:T(8,128)S(1)}, f32[4,128,128]{2,1,0:T(8,128)S(1)}, f32[256,128]{1,0:T(8,128)S(1)}) custom-call(bf16[1,5,128,128]{3,2,1,0:T(8,128)(2,1)S(1)} %copy-done, f32[256,128]{1,0:T(8,128)S(1)} %get-tuple-element.51.refs_1_, f32[256,128]{1,0:T(8,128)S(1)} %collective-permute-done.6.refs_2_, f32[256,128]{1,0:T(8,128)S(1)} %upper_maps_1.1.refs_3_.refs_0_), custom_call_target="tpu_custom_call" | custom-call | flops 80000000 | bytes 240000 | tf_op jit(solution)/shard_map/merge_orth_2/pallas_call | solution.py:389
  54.7 1.6 %collective-permute-start.10 = (f32[256,128]{1,0:T(8,128)S(1)}, f32[256,128]{1,0:T(8,128)S(1)}, u32[]{:S(2)}, u32[]{:S(2)}) collective-permute-start(f32[256,128]{1,0:T(8,128)S(1)} %get-tuple-element.57), channel_id=1, source_target_pairs={{0,8},{1,9},{2,10},{3,11},{4,12},{5,13},{6,14},{7,15},{8,0},{9,1},... | collective-permute-start | bytes 393224 | tf_op jit(solution)/shard_map/ppermute | solution.py:25
  56.4 0.0 collective-permute-done.11.refs_1_
  56.4 0.5 upper_maps_2.1.refs_0_
  56.9 0.5 collective-permute-start.14
  57.4 2.4 %collective-permute-done.10 = f32[256,128]{1,0:T(8,128)S(1)} collective-permute-done((f32[256,128]{1,0:T(8,128)S(1)}, f32[256,128]{1,0:T(8,128)S(1)}, u32[]{:S(2)}, u32[]{:S(2)}) %collective-permute-start.10) | collective-permute-done | bytes 131104 | tf_op jit(solution)/shard_map/ppermute | solution.py:25
  59.8 4.8 %merge_orth_3.1 = (f32[5,128,128]{2,1,0:T(8,128)S(1)}, f32[256,128]{1,0:T(8,128)S(1)}, f32[128,128]{1,0:T(8,128)S(1)}, f32[4,128,128]{2,1,0:T(8,128)S(1)}) fusion(f32[5,128,128]{2,1,0:T(8,128)S(1)} %bitcast_dynamic-update-slice_fusion.2, bf16[1,5,128,128]{3,2,1,0:T(8,128)(2,1)S(1)} %copy-done, f32[256,128]{1,0:T(8,128)S(1)} %get-tuple-element.57, ...), kind=kCustom, calls=%fused_computation.3 | custom fusion | flops 80000000 | bytes 1081344 | tf_op jit(solution)/shard_map/merge_orth_3/pallas_call | solution.py:389
  64.5 2.7 %collective-permute-start.12 = (f32[128,128]{1,0:T(8,128)S(1)}, f32[128,128]{1,0:T(8,128)S(1)}, u32[]{:S(2)}, u32[]{:S(2)}) collective-permute-start(f32[128,128]{1,0:T(8,128)S(1)} %get-tuple-element.77), channel_id=1, source_target_pairs={{0,16},{1,17},{2,18},{3,19},{4,20},{5,21},{6,22},{7,23},{8,24},{9,... | collective-permute-start | bytes 196616 | tf_op jit(solution)/shard_map/ppermute | solution.py:25
  67.2 0.0 collective-permute-done.14.refs_1_
  67.2 0.5 upper_maps_3.1.own_ref
  67.7 0.4 collective-permute-start.15
  68.1 3.4 %collective-permute-done.12 = f32[128,128]{1,0:T(8,128)S(1)} collective-permute-done((f32[128,128]{1,0:T(8,128)S(1)}, f32[128,128]{1,0:T(8,128)S(1)}, u32[]{:S(2)}, u32[]{:S(2)}) %collective-permute-start.12) | collective-permute-done | bytes 65568 | tf_op jit(solution)/shard_map/ppermute | solution.py:25
  71.5 0.0 collective-permute-start.13
  71.5 1.3 %collective-permute-done.13 = f32[128,128]{1,0:T(8,128)S(1)} collective-permute-done((f32[128,128]{1,0:T(8,128)S(1)}, f32[128,128]{1,0:T(8,128)S(1)}, u32[]{:S(2)}, u32[]{:S(2)}) %collective-permute-start.13) | collective-permute-done | bytes 65568 | tf_op jit(solution)/shard_map/ppermute | solution.py:25
  72.8 4.4 %merge_orth_4.1 = (f32[5,128,128]{2,1,0:T(8,128)S(1)}, f32[128,256]{1,0:T(8,128)S(1)}, f32[8,128]{1,0:T(8,128)}) fusion(f32[5,128,128]{2,1,0:T(8,128)S(1)} %get-tuple-element.74, bf16[1,5,128,128]{3,2,1,0:T(8,128)(2,1)S(1)} %copy-done, f32[256,128]{1,0:T(8,128)S(1)} %get-tuple-element.75, f32[128,128]{1,0:T(8,128)S(1)} %collective-permute-done.12, ...), kind=kCustom, calls=%fused_computation.2 | custom fusion | flops 80000000 | bytes 757760 | tf_op jit(solution)/shard_map/merge_orth_4/pallas_call | solution.py:389
  77.2 0.0 copy-start.4
  77.2 0.0 collective-permute-done.15.other_ref
  77.2 0.6 top_sample.1.refs_0_
  77.8 0.2 collective-permute-start.16
  78.0 2.7 %collective-permute-start.17 = (f32[128,128]{1,0:T(8,128)S(1)}, f32[128,128]{1,0:T(8,128)S(1)}, u32[]{:S(2)}, u32[]{:S(2)}) collective-permute-start(f32[128,128]{1,0:T(8,128)S(1)} %top_sample.1.refs_0_), channel_id=1, source_target_pairs={{0,2},{1,3},{2,0},{3,1},{4,6},{5,7},{6,4},{7,5},{8,10},{9,11},{10,... | collective-permute-start | bytes 196616 | tf_op jit(solution)/shard_map/ppermute | solution.py:25
  80.7 0.0 collective-permute-start.18
  80.7 0.0 collective-permute-done.16.refs_1_
  80.7 2.6 %collective-permute-done.17.refs_2_ = f32[128,128]{1,0:T(8,128)S(1)} collective-permute-done((f32[128,128]{1,0:T(8,128)S(1)}, f32[128,128]{1,0:T(8,128)S(1)}, u32[]{:S(2)}, u32[]{:S(2)}) %collective-permute-start.17) | collective-permute-done | bytes 65568 | tf_op jit(solution)/shard_map/ppermute | solution.py:25
  83.3 1.6 %collective-permute-done.18.refs_3_ = f32[128,128]{1,0:T(8,128)S(1)} collective-permute-done((f32[128,128]{1,0:T(8,128)S(1)}, f32[128,128]{1,0:T(8,128)S(1)}, u32[]{:S(2)}, u32[]{:S(2)}) %collective-permute-start.18) | collective-permute-done | bytes 65568 | tf_op jit(solution)/shard_map/ppermute | solution.py:25
  84.8 0.7 top_columns.1
  85.5 0.0 copy-done.4
  (5 shorter events, 0.0 us)
Async XLA Ops:
  0.6 11.8 %copy-start.2 = (f32[512,128]{1,0:T(8,128)S(1)}, f32[512,128]{1,0:T(8,128)}, u32[]{:S(2)}) copy-start(f32[512,128]{1,0:T(8,128)} %refs_0_.8) | copy-start | bytes 786436
  0.6 13.0 %copy-start.1 = (bf16[256,512]{1,0:T(8,128)(2,1)S(1)}, bf16[256,512]{1,0:T(8,128)(2,1)}, u32[]{:S(2)}) copy-start(bf16[256,512]{1,0:T(8,128)(2,1)} %refs_3_.1) | copy-start | bytes 786436
  0.7 0.7 copy-start.3
  12.4 17.2 %copy-start = (bf16[1,5,128,128]{3,2,1,0:T(8,128)(2,1)S(1)}, bf16[1,5,128,128]{3,2,1,0:T(8,128)(2,1)}, u32[]{:S(2)}) copy-start(bf16[1,5,128,128]{3,2,1,0:T(8,128)(2,1)} %coupling_ref.1) | copy-start | bytes 491524
  13.1 1.7 %collective-permute-start = (f32[512,128]{1,0:T(8,128)S(1)}, f32[512,128]{1,0:T(8,128)S(1)}, u32[]{:S(2)}, u32[]{:S(2)}) collective-permute-start(f32[512,128]{1,0:T(8,128)S(1)} %reduced_1.1), channel_id=1, source_target_pairs={{0,1},{1,0},{2,3},{3,2},{4,5},{5,4},{6,7},{7,6},{8,9},{9,8},{10,11... | collective-permute-start | bytes 786440 | tf_op jit(solution)/shard_map/ppermute | solution.py:25
  14.8 3.1 %collective-permute-start.1 = (f32[512,512]{1,0:T(8,128)S(1)}, f32[512,512]{1,0:T(8,128)S(1)}, u32[]{:S(2)}, u32[]{:S(2)}) collective-permute-start(f32[512,512]{1,0:T(8,128)S(1)} %get-tuple-element.37.refs_1_), channel_id=1, source_target_pairs={{0,1},{1,0},{2,3},{3,2},{4,5},{5,4},{6,7},{7,6},{8,9},{9,8},{10,11... | collective-permute-start | bytes 3145736 | tf_op jit(solution)/shard_map/ppermute | solution.py:25
  15.3 6.7 %collective-permute-start.2 = (f32[256,128]{1,0:T(8,128)S(1)}, f32[256,128]{1,0:T(8,128)S(1)}, u32[]{:S(2)}, u32[]{:S(2)}) collective-permute-start(f32[256,128]{1,0:T(8,128)S(1)} %slice_add_fusion.1), channel_id=1, source_target_pairs={{0,2},{1,3},{2,0},{3,1},{4,6},{5,7},{6,4},{7,5},{8,10},{9,11},{10,... | collective-permute-start | bytes 393224 | tf_op jit(solution)/shard_map/ppermute | solution.py:25
  22.0 13.6 %collective-permute-start.5 = (f32[256,512]{1,0:T(8,128)S(1)}, f32[256,512]{1,0:T(8,128)S(1)}, u32[]{:S(2)}, u32[]{:S(2)}) collective-permute-start(f32[256,512]{1,0:T(8,128)S(1)} %slice_add_fusion._), channel_id=1, source_target_pairs={{0,2},{1,3},{2,0},{3,1},{4,6},{5,7},{6,4},{7,5},{8,10},{9,11},{10,... | collective-permute-start | bytes 1572872 | tf_op jit(solution)/shard_map/ppermute | solution.py:25
  28.2 1.4 %collective-permute-start.3 = (f32[256,128]{1,0:T(8,128)S(1)}, f32[256,128]{1,0:T(8,128)S(1)}, u32[]{:S(2)}, u32[]{:S(2)}) collective-permute-start(f32[256,128]{1,0:T(8,128)S(1)} %get-tuple-element.44.refs_1_), channel_id=1, source_target_pairs={{0,1},{1,0},{2,3},{3,2},{4,5},{5,4},{6,7},{7,6},{8,9},{9,8},{10,11... | collective-permute-start | bytes 393224 | tf_op jit(solution)/shard_map/ppermute | solution.py:25
  34.2 5.6 %collective-permute-start.4 = (f32[256,128]{1,0:T(8,128)S(1)}, f32[256,128]{1,0:T(8,128)S(1)}, u32[]{:S(2)}, u32[]{:S(2)}) collective-permute-start(f32[256,128]{1,0:T(8,128)S(1)} %get-tuple-element.46.refs_1_), channel_id=1, source_target_pairs={{0,2},{1,3},{2,0},{3,1},{4,6},{5,7},{6,4},{7,5},{8,10},{9,11},{10,... | collective-permute-start | bytes 393224 | tf_op jit(solution)/shard_map/ppermute | solution.py:25
  37.0 9.0 %collective-permute-start.7 = (f32[256,128]{1,0:T(8,128)S(1)}, f32[256,128]{1,0:T(8,128)S(1)}, u32[]{:S(2)}, u32[]{:S(2)}) collective-permute-start(f32[256,128]{1,0:T(8,128)S(1)} %get-tuple-element.52), channel_id=1, source_target_pairs={{0,1},{1,0},{2,3},{3,2},{4,5},{5,4},{6,7},{7,6},{8,9},{9,8},{10,11... | collective-permute-start | bytes 393224 | tf_op jit(solution)/shard_map/ppermute | solution.py:25
  37.0 8.9 %collective-permute-start.8 = (f32[256,128]{1,0:T(8,128)S(1)}, f32[256,128]{1,0:T(8,128)S(1)}, u32[]{:S(2)}, u32[]{:S(2)}) collective-permute-start(f32[256,128]{1,0:T(8,128)S(1)} %get-tuple-element.53), channel_id=1, source_target_pairs={{0,2},{1,3},{2,0},{3,1},{4,6},{5,7},{6,4},{7,5},{8,10},{9,11},{10,... | collective-permute-start | bytes 393224 | tf_op jit(solution)/shard_map/ppermute | solution.py:25
  38.6 7.4 %collective-permute-start.9 = (f32[256,128]{1,0:T(8,128)S(1)}, f32[256,128]{1,0:T(8,128)S(1)}, u32[]{:S(2)}, u32[]{:S(2)}) collective-permute-start(f32[256,128]{1,0:T(8,128)S(1)} %get-tuple-element.54), channel_id=1, source_target_pairs={{0,3},{1,2},{2,1},{3,0},{4,7},{5,6},{6,5},{7,4},{8,11},{9,10},{10,... | collective-permute-start | bytes 393224 | tf_op jit(solution)/shard_map/ppermute | solution.py:25
  44.4 5.8 %collective-permute-start.6 = (f32[256,128]{1,0:T(8,128)S(1)}, f32[256,128]{1,0:T(8,128)S(1)}, u32[]{:S(2)}, u32[]{:S(2)}) collective-permute-start(f32[256,128]{1,0:T(8,128)S(1)} %get-tuple-element.51.refs_1_), channel_id=1, source_target_pairs={{0,4},{1,5},{2,6},{3,7},{4,0},{5,1},{6,2},{7,3},{8,12},{9,13},{10,... | collective-permute-start | bytes 393224 | tf_op jit(solution)/shard_map/ppermute | solution.py:25
  46.5 9.9 %collective-permute-start.11 = (f32[256,128]{1,0:T(8,128)S(1)}, f32[256,128]{1,0:T(8,128)S(1)}, u32[]{:S(2)}, u32[]{:S(2)}) collective-permute-start(f32[256,128]{1,0:T(8,128)S(1)} %upper_maps_1.1.refs_3_.refs_0_), channel_id=1, source_target_pairs={{0,4},{1,5},{2,6},{3,7},{4,0},{5,1},{6,2},{7,3},{8,12},{9,13},{10,... | collective-permute-start | bytes 393224 | tf_op jit(solution)/shard_map/ppermute | solution.py:25
  54.7 5.0 %collective-permute-start.10 = (f32[256,128]{1,0:T(8,128)S(1)}, f32[256,128]{1,0:T(8,128)S(1)}, u32[]{:S(2)}, u32[]{:S(2)}) collective-permute-start(f32[256,128]{1,0:T(8,128)S(1)} %get-tuple-element.57), channel_id=1, source_target_pairs={{0,8},{1,9},{2,10},{3,11},{4,12},{5,13},{6,14},{7,15},{8,0},{9,1},... | collective-permute-start | bytes 393224 | tf_op jit(solution)/shard_map/ppermute | solution.py:25
  56.9 10.3 %collective-permute-start.14 = (f32[256,128]{1,0:T(8,128)S(1)}, f32[256,128]{1,0:T(8,128)S(1)}, u32[]{:S(2)}, u32[]{:S(2)}) collective-permute-start(f32[256,128]{1,0:T(8,128)S(1)} %upper_maps_2.1.refs_0_), channel_id=1, source_target_pairs={{0,8},{1,9},{2,10},{3,11},{4,12},{5,13},{6,14},{7,15},{8,0},{9,1},... | collective-permute-start | bytes 393224 | tf_op jit(solution)/shard_map/ppermute | solution.py:25
  64.5 7.0 %collective-permute-start.12 = (f32[128,128]{1,0:T(8,128)S(1)}, f32[128,128]{1,0:T(8,128)S(1)}, u32[]{:S(2)}, u32[]{:S(2)}) collective-permute-start(f32[128,128]{1,0:T(8,128)S(1)} %get-tuple-element.77), channel_id=1, source_target_pairs={{0,16},{1,17},{2,18},{3,19},{4,20},{5,21},{6,22},{7,23},{8,24},{9,... | collective-permute-start | bytes 196616 | tf_op jit(solution)/shard_map/ppermute | solution.py:25
  67.7 9.5 %collective-permute-start.15 = (f32[256,128]{1,0:T(8,128)S(1)}, f32[256,128]{1,0:T(8,128)S(1)}, u32[]{:S(2)}, u32[]{:S(2)}) collective-permute-start(f32[256,128]{1,0:T(8,128)S(1)} %upper_maps_3.1.own_ref), channel_id=1, source_target_pairs={{0,16},{1,17},{2,18},{3,19},{4,20},{5,21},{6,22},{7,23},{8,24},{9,... | collective-permute-start | bytes 393224 | tf_op jit(solution)/shard_map/ppermute | solution.py:25
  71.5 1.3 %collective-permute-start.13 = (f32[128,128]{1,0:T(8,128)S(1)}, f32[128,128]{1,0:T(8,128)S(1)}, u32[]{:S(2)}, u32[]{:S(2)}) collective-permute-start(f32[128,128]{1,0:T(8,128)S(1)} %collective-permute-done.12), channel_id=1, source_target_pairs={{0,1},{1,0},{2,3},{3,2},{4,5},{5,4},{6,7},{7,6},{8,9},{9,8},{10,11... | collective-permute-start | bytes 196616 | tf_op jit(solution)/shard_map/ppermute | solution.py:25
  77.2 8.4 %copy-start.4 = (f32[5,128,128]{2,1,0:T(8,128)}, f32[5,128,128]{2,1,0:T(8,128)S(1)}, u32[]{:S(2)}) copy-start(f32[5,128,128]{2,1,0:T(8,128)S(1)} %get-tuple-element.68) | copy-start | bytes 983044
  77.8 2.9 %collective-permute-start.16 = (f32[128,128]{1,0:T(8,128)S(1)}, f32[128,128]{1,0:T(8,128)S(1)}, u32[]{:S(2)}, u32[]{:S(2)}) collective-permute-start(f32[128,128]{1,0:T(8,128)S(1)} %top_sample.1.refs_0_), channel_id=1, source_target_pairs={{0,1},{1,0},{2,3},{3,2},{4,5},{5,4},{6,7},{7,6},{8,9},{9,8},{10,11... | collective-permute-start | bytes 196616 | tf_op jit(solution)/shard_map/ppermute | solution.py:25
  78.0 5.3 %collective-permute-start.17 = (f32[128,128]{1,0:T(8,128)S(1)}, f32[128,128]{1,0:T(8,128)S(1)}, u32[]{:S(2)}, u32[]{:S(2)}) collective-permute-start(f32[128,128]{1,0:T(8,128)S(1)} %top_sample.1.refs_0_), channel_id=1, source_target_pairs={{0,2},{1,3},{2,0},{3,1},{4,6},{5,7},{6,4},{7,5},{8,10},{9,11},{10,... | collective-permute-start | bytes 196616 | tf_op jit(solution)/shard_map/ppermute | solution.py:25
  80.7 4.2 %collective-permute-start.18 = (f32[128,128]{1,0:T(8,128)S(1)}, f32[128,128]{1,0:T(8,128)S(1)}, u32[]{:S(2)}, u32[]{:S(2)}) collective-permute-start(f32[128,128]{1,0:T(8,128)S(1)} %top_sample.1.refs_0_), channel_id=1, source_target_pairs={{0,3},{1,2},{2,1},{3,0},{4,7},{5,6},{6,5},{7,4},{8,11},{9,10},{10,... | collective-permute-start | bytes 196616 | tf_op jit(solution)/shard_map/ppermute | solution.py:25
